TPU v7x, 32 devices: a whole 2x2x4 slice. The times are simulated.
32 devices in a mesh: dp: 4 (over z), blk: 8 (over y, x, core).
Axes of the slice: x: 2, y: 2, z: 4, core: 2. Of those that a mesh axis runs over, the one named last changes fastest.
Arguments:
- latents: bfloat16 [32, 64, 1536], P('dp', 'blk'), may hold values from -6 to 6
- media: bfloat16 [32, 256, 1536], P('dp', 'blk'), may hold values from -6 to 6
- media_lengths: int32 [32], P('dp'), may hold values from 1 to 256, as said below
- cotangent: bfloat16 [32, 64, 1536], P('dp', 'blk'), may hold values from -6 to 6
- query_weight: bfloat16 [1536, 1536], P(('dp', 'blk')), may hold values from -0.15625 to 0.15625
- kv_weight: bfloat16 [1536, 3072], P(('dp', 'blk')), may hold values from -0.15625 to 0.15625
- out_weight: bfloat16 [1536, 1536], P(('dp', 'blk')), may hold values from -1.25 to 1.25
- in_weight: bfloat16 [1536, 6144], P(('dp', 'blk')), may hold values from -0.15625 to 0.15625
- down_weight: bfloat16 [1536, 6144], P(('dp', 'blk')), may hold values from -0.078125 to 0.078125
- media_gain: bfloat16 [1536], P(('dp', 'blk')), may hold values from 0.5 to 1.5
- latent_gain: bfloat16 [1536], P(('dp', 'blk')), may hold values from 0.5 to 1.5
- ffn_gain: bfloat16 [1536], P(('dp', 'blk')), may hold values from 0.5 to 1.5
Outputs:
- resampled: bfloat16 [32, 64, 1536], P('dp', 'blk')
- latents_grad: float32 [32, 64, 1536], P('dp', 'blk')
- media_grad: float32 [32, 256, 1536], P('dp', 'blk')
- query_grad: float32 [1536, 1536], P(('dp', 'blk'))
- kv_grad: float32 [1536, 3072], P(('dp', 'blk'))
- out_grad: float32 [1536, 1536], P(('dp', 'blk'))
- in_grad: float32 [1536, 6144], P(('dp', 'blk'))
- down_grad: float32 [1536, 6144], P(('dp', 'blk'))
- media_gain_grad: float32 [1536], P(('dp', 'blk'))
- latent_gain_grad: float32 [1536], P(('dp', 'blk'))
- ffn_gain_grad: float32 [1536], P(('dp', 'blk'))
Inputs may be any that keep to these rules, and one draw needn't show every extreme that they name: `media_lengths`: a prefix of each image's patch rows is valid; in each aligned block of 8 images one image has all 256.
All inputs are finite; a program needn't handle non-finite values.
Results may differ from a plain program's by a relative error of at most 0.04.
Values may be sent and summed in bfloat16 or wider, within the bound.
No kernel may reach another device: no remote copies, remote signals or barrier semaphores. Data moves between devices by JAX's collectives and lax.ppermute only.
A program may use at most 256 MiB of HBM per device.

v0:
```python
from functools import partial
import math

import jax
import jax.numpy as jnp
from jax import lax
from jax.sharding import PartitionSpec as P

HEADS = 16


NORM_EPS = 1e-05
MASKED = -1e30
GAUSS_DENSITY = 0.3989422804014327


def normalize(values):
    center = values - jnp.mean(values, -1, keepdims=True)
    inverse = lax.rsqrt(jnp.mean(center * center, -1, keepdims=True) + NORM_EPS)
    return (center * inverse, inverse)


def norm_back(grad_norm, normed, inverse):
    return inverse * (
        grad_norm
        - jnp.mean(grad_norm, -1, keepdims=True)
        - normed * jnp.mean(grad_norm * normed, -1, keepdims=True)
    )


def gelu_slope(values):
    return (
        0.5 * (1.0 + jax.scipy.special.erf(values * 0.7071067811865476))
        + values * jnp.exp(-0.5 * values * values) * GAUSS_DENSITY
    )


def head_scores(queries, key_part, lengths, media_rows, shard_rows, score_scale):
    image_count, key_count = (key_part.shape[0], key_part.shape[1])
    head_count, head_size = (queries.shape[2], queries.shape[3])
    key_heads = key_part.reshape(image_count, key_count, head_count, head_size)
    scores = (
        jnp.einsum("blhe,bnhe->bhln", queries, key_heads, preferred_element_type=jnp.float32)
        * score_scale
    )
    position = jnp.arange(key_count, dtype=jnp.int32)
    owner_rank = position // shard_rows
    within = position % shard_rows
    media_index = owner_rank * media_rows + within
    allowed = (within[None, :] >= media_rows) | (media_index[None, :] < lengths[:, None])
    allowed = allowed[:, None, None, :]
    return (jnp.where(allowed, scores, MASKED), allowed, key_heads)


def attend_step(queries, lengths, media_rows, shard_rows, score_scale, carry, portion, first_row):
    top_score, denominator, weighted = carry
    key_part, value_part = portion
    scores, allowed, key_heads = head_scores(
        queries, key_part, lengths, media_rows, shard_rows, score_scale
    )
    new_top = jnp.maximum(top_score, jnp.max(scores, -1))
    weights = jnp.where(allowed, jnp.exp(scores - new_top[..., None]), 0.0)
    value_heads = value_part.reshape(key_heads.shape)
    weighted = jnp.einsum(
        "bhln,bnhe->bhle",
        weights.astype(jnp.bfloat16),
        value_heads,
        preferred_element_type=jnp.float32,
    )
    return (new_top, jnp.sum(weights, -1), weighted)


def back_pieces(
    queries, grads, log_total, delta, lengths, media_rows, shard_rows, score_scale, portion
):
    key_part, value_part = portion
    scores, allowed, key_heads = head_scores(
        queries, key_part, lengths, media_rows, shard_rows, score_scale
    )
    probs = jnp.where(allowed, jnp.exp(scores - log_total[..., None]), 0.0)
    value_heads = value_part.reshape(key_heads.shape)
    prob_grad = jnp.einsum(
        "blhe,bnhe->bhln", grads, value_heads, preferred_element_type=jnp.float32
    )
    score_grad = (probs * (prob_grad - delta[..., None])).astype(jnp.bfloat16)
    query_piece = score_scale * jnp.einsum(
        "bhln,bnhe->blhe", score_grad, key_heads, preferred_element_type=jnp.float32
    )
    key_piece = score_scale * jnp.einsum(
        "bhln,blhe->bnhe", score_grad, queries, preferred_element_type=jnp.float32
    )
    value_piece = jnp.einsum(
        "bhln,blhe->bnhe", probs.astype(jnp.bfloat16), grads, preferred_element_type=jnp.float32
    )
    return (query_piece, key_piece.reshape(key_part.shape), value_piece.reshape(value_part.shape))


def back_step(
    queries,
    grads,
    log_total,
    delta,
    lengths,
    media_rows,
    shard_rows,
    score_scale,
    carry,
    portion,
    first_row,
):
    query_piece, key_piece, value_piece = back_pieces(
        queries, grads, log_total, delta, lengths, media_rows, shard_rows, score_scale, portion
    )
    return (query_piece, key_piece, value_piece)


def owned_columns(piece, owner, dp_count, blk_count):
    row_count, width = piece.shape
    per_owner = width // (dp_count * blk_count)
    split = piece.reshape(row_count, dp_count, blk_count, per_owner)
    return lax.dynamic_slice_in_dim(split, owner, 1, 2).reshape(row_count, dp_count * per_owner)


def row_product(left, right):
    return jnp.einsum("rd,re->de", left, right, preferred_element_type=jnp.float32)


def body(
    latents,
    media,
    media_lengths,
    cotangent,
    query_weight,
    kv_weight,
    out_weight,
    in_weight,
    down_weight,
    media_gain,
    latent_gain,
    ffn_gain,
):
    w_query, w_kv, w_out, w_in, w_down, g_media, g_latent, g_ffn = (
        lax.all_gather(query_weight, ("dp", "blk"), axis=0, tiled=True),
        lax.all_gather(kv_weight, ("dp", "blk"), axis=0, tiled=True),
        lax.all_gather(out_weight, ("dp", "blk"), axis=0, tiled=True),
        lax.all_gather(in_weight, ("dp", "blk"), axis=0, tiled=True),
        lax.all_gather(down_weight, ("dp", "blk"), axis=0, tiled=True),
        lax.all_gather(media_gain, ("dp", "blk"), axis=0, tiled=True),
        lax.all_gather(latent_gain, ("dp", "blk"), axis=0, tiled=True),
        lax.all_gather(ffn_gain, ("dp", "blk"), axis=0, tiled=True),
    )
    image_count, latent_rows, model_width = latents.shape
    media_rows = media.shape[1]
    shard_rows = media_rows + latent_rows
    head_count = HEADS
    head_size = model_width // head_count
    score_scale = 1.0 / math.sqrt(head_size)
    latent_float = latents.astype(jnp.float32)
    media_norm, media_inverse = normalize(media.astype(jnp.float32))
    latent_norm, latent_inverse = normalize(latent_float)
    media_input = (media_norm * g_media).astype(jnp.bfloat16)
    latent_input = (latent_norm * g_latent).astype(jnp.bfloat16)
    queries = jnp.einsum(
        "bld,de->ble", latent_input, w_query, preferred_element_type=jnp.float32
    ).astype(jnp.bfloat16)
    kv_input = jnp.concatenate([media_input, latent_input], 1)
    kv_proj = jnp.einsum("brd,de->bre", kv_input, w_kv, preferred_element_type=jnp.float32)
    keys = kv_proj[..., :model_width].astype(jnp.bfloat16)
    values_proj = kv_proj[..., model_width:].astype(jnp.bfloat16)
    query_heads = queries.reshape(image_count, latent_rows, head_count, head_size)
    start_state = (
        jnp.full((image_count, head_count, latent_rows), MASKED, jnp.float32),
        jnp.zeros((image_count, head_count, latent_rows), jnp.float32),
        jnp.zeros((image_count, head_count, latent_rows, head_size), jnp.float32),
    )
    attend = partial(attend_step, query_heads, media_lengths, media_rows, shard_rows, score_scale)
    top_score, denominator, weighted = attend(
        start_state,
        (
            lax.all_gather(keys, "blk", axis=1, tiled=True),
            lax.all_gather(values_proj, "blk", axis=1, tiled=True),
        ),
        jnp.int32(0),
    )
    attended = weighted / denominator[..., None]
    log_total = top_score + jnp.log(denominator)
    attn_low = (
        attended.transpose(0, 2, 1, 3)
        .reshape(image_count, latent_rows, model_width)
        .astype(jnp.bfloat16)
    )
    mixed = latent_float + jnp.einsum(
        "ble,ed->bld", attn_low, w_out, preferred_element_type=jnp.float32
    )
    ffn_norm, ffn_inverse = normalize(mixed)
    ffn_input = (ffn_norm * g_ffn).astype(jnp.bfloat16)
    pre_act = jnp.einsum("bld,df->blf", ffn_input, w_in, preferred_element_type=jnp.float32)
    hidden = jax.nn.gelu(pre_act, approximate=False).astype(jnp.bfloat16)
    resampled = (
        mixed + jnp.einsum("blf,df->bld", hidden, w_down, preferred_element_type=jnp.float32)
    ).astype(jnp.bfloat16)
    w_query, w_kv, w_out, w_in, w_down, g_media, g_latent, g_ffn = (
        lax.all_gather(query_weight, ("dp", "blk"), axis=0, tiled=True),
        lax.all_gather(kv_weight, ("dp", "blk"), axis=0, tiled=True),
        lax.all_gather(out_weight, ("dp", "blk"), axis=0, tiled=True),
        lax.all_gather(in_weight, ("dp", "blk"), axis=0, tiled=True),
        lax.all_gather(down_weight, ("dp", "blk"), axis=0, tiled=True),
        lax.all_gather(media_gain, ("dp", "blk"), axis=0, tiled=True),
        lax.all_gather(latent_gain, ("dp", "blk"), axis=0, tiled=True),
        lax.all_gather(ffn_gain, ("dp", "blk"), axis=0, tiled=True),
    )
    hidden_grad = jnp.einsum("bld,df->blf", cotangent, w_down, preferred_element_type=jnp.float32)
    pre_grad = (hidden_grad * gelu_slope(pre_act)).astype(jnp.bfloat16)
    ffn_in_grad = jnp.einsum("blf,df->bld", pre_grad, w_in, preferred_element_type=jnp.float32)
    ffn_gain_grad = jnp.sum(ffn_in_grad * ffn_norm, axis=(0, 1))
    mixed_grad = cotangent.astype(jnp.float32) + norm_back(
        ffn_in_grad * g_ffn, ffn_norm, ffn_inverse
    )
    branch_grad = mixed_grad.astype(jnp.bfloat16)
    attended_grad = jnp.einsum(
        "bld,ed->ble", branch_grad, w_out, preferred_element_type=jnp.float32
    ).astype(jnp.bfloat16)
    grad_heads = attended_grad.reshape(image_count, latent_rows, head_count, head_size)
    delta = jnp.sum(grad_heads.astype(jnp.float32).transpose(0, 2, 1, 3) * attended, -1)
    half_images = image_count // 2
    all_rows = shard_rows * lax.axis_size("blk")
    query_parts = []
    key_parts = []
    value_parts = []
    for part_index in range(2):
        lower = part_index * half_images
        upper = lower + half_images
        revisit = partial(
            back_step,
            query_heads[lower:upper],
            grad_heads[lower:upper],
            log_total[lower:upper],
            delta[lower:upper],
            media_lengths[lower:upper],
            media_rows,
            shard_rows,
            score_scale,
        )
        zero_state = (
            jnp.zeros((half_images, latent_rows, head_count, head_size), jnp.float32),
            jnp.zeros((half_images, all_rows, model_width), jnp.float32),
            jnp.zeros((half_images, all_rows, model_width), jnp.float32),
        )
        part_query, part_keys, part_values = revisit(
            zero_state,
            (
                lax.all_gather(keys[lower:upper], "blk", axis=1, tiled=True),
                lax.all_gather(values_proj[lower:upper], "blk", axis=1, tiled=True),
            ),
            jnp.int32(0),
        )
        own_keys, own_values = (
            lax.psum_scatter(
                part_keys.astype(jnp.bfloat16), "blk", scatter_dimension=1, tiled=True
            ).astype(jnp.float32),
            lax.psum_scatter(
                part_values.astype(jnp.bfloat16), "blk", scatter_dimension=1, tiled=True
            ).astype(jnp.float32),
        )
        query_parts.append(part_query)
        key_parts.append(own_keys)
        value_parts.append(own_values)
    queries_grad = (
        jnp.concatenate(query_parts, 0)
        .reshape(image_count, latent_rows, model_width)
        .astype(jnp.bfloat16)
    )
    kv_out_grad = jnp.concatenate(
        [jnp.concatenate(key_parts, 0), jnp.concatenate(value_parts, 0)], -1
    ).astype(jnp.bfloat16)
    kv_in_grad = jnp.einsum("bre,de->brd", kv_out_grad, w_kv, preferred_element_type=jnp.float32)
    media_in_grad = kv_in_grad[:, :media_rows]
    latent_in_grad = kv_in_grad[:, media_rows:] + jnp.einsum(
        "ble,de->bld", queries_grad, w_query, preferred_element_type=jnp.float32
    )
    media_gain_grad = jnp.sum(media_in_grad * media_norm, axis=(0, 1))
    latent_gain_grad = jnp.sum(latent_in_grad * latent_norm, axis=(0, 1))
    media_grad = norm_back(media_in_grad * g_media, media_norm, media_inverse)
    latents_grad = mixed_grad + norm_back(latent_in_grad * g_latent, latent_norm, latent_inverse)
    dp_count = lax.axis_size("dp")
    blk_count = lax.axis_size("blk")
    owner = lax.axis_index("blk")

    def flat_rows(array):
        return array.reshape(-1, array.shape[-1])

    lat_piece = lax.all_gather(flat_rows(latent_input), "blk", axis=0, tiled=True)
    qgrad_piece = lax.all_gather(flat_rows(queries_grad), "blk", axis=0, tiled=True)
    attn_piece = lax.all_gather(flat_rows(attn_low), "blk", axis=0, tiled=True)
    branch_piece = lax.all_gather(flat_rows(branch_grad), "blk", axis=0, tiled=True)
    ffn_piece = lax.all_gather(flat_rows(ffn_input), "blk", axis=0, tiled=True)
    pre_piece = lax.all_gather(flat_rows(pre_grad), "blk", axis=0, tiled=True)
    cot_piece = lax.all_gather(flat_rows(cotangent), "blk", axis=0, tiled=True)
    hid_piece = lax.all_gather(flat_rows(hidden), "blk", axis=0, tiled=True)
    sum_query = row_product(owned_columns(lat_piece, owner, dp_count, blk_count), qgrad_piece)
    sum_out = row_product(owned_columns(attn_piece, owner, dp_count, blk_count), branch_piece)
    sum_in = row_product(owned_columns(ffn_piece, owner, dp_count, blk_count), pre_piece)
    sum_down = row_product(owned_columns(cot_piece, owner, dp_count, blk_count), hid_piece)
    in_piece = lax.all_gather(flat_rows(kv_input), "blk", axis=0, tiled=True)
    grad_piece = lax.all_gather(flat_rows(kv_out_grad), "blk", axis=0, tiled=True)
    kv_slice = row_product(owned_columns(in_piece, owner, dp_count, blk_count), grad_piece)
    summed = (
        lax.psum_scatter(
            sum_query.astype(jnp.bfloat16), "dp", scatter_dimension=0, tiled=True
        ).astype(jnp.float32),
        lax.psum_scatter(
            kv_slice.astype(jnp.bfloat16), "dp", scatter_dimension=0, tiled=True
        ).astype(jnp.float32),
        lax.psum_scatter(
            sum_out.astype(jnp.bfloat16), "dp", scatter_dimension=0, tiled=True
        ).astype(jnp.float32),
        lax.psum_scatter(sum_in.astype(jnp.bfloat16), "dp", scatter_dimension=0, tiled=True).astype(
            jnp.float32
        ),
        lax.psum_scatter(
            sum_down.astype(jnp.bfloat16), "dp", scatter_dimension=0, tiled=True
        ).astype(jnp.float32),
    )
    gains = (
        lax.psum_scatter(media_gain_grad, ("dp", "blk"), scatter_dimension=0, tiled=True),
        lax.psum_scatter(latent_gain_grad, ("dp", "blk"), scatter_dimension=0, tiled=True),
        lax.psum_scatter(ffn_gain_grad, ("dp", "blk"), scatter_dimension=0, tiled=True),
    )
    return (
        resampled,
        latents_grad,
        media_grad,
        summed[0],
        summed[1],
        summed[2],
        summed[3],
        summed[4],
        gains[0],
        gains[1],
        gains[2],
    )


def solution(mesh):
    return jax.shard_map(
        body,
        mesh=mesh,
        in_specs=(
            P("dp", "blk", None),
            P("dp", "blk", None),
            P("dp"),
            P("dp", "blk", None),
            P(("dp", "blk"), None),
            P(("dp", "blk"), None),
            P(("dp", "blk"), None),
            P(("dp", "blk"), None),
            P(("dp", "blk"), None),
            P(("dp", "blk")),
            P(("dp", "blk")),
            P(("dp", "blk")),
        ),
        out_specs=(
            P("dp", "blk", None),
            P("dp", "blk", None),
            P("dp", "blk", None),
            P(("dp", "blk"), None),
            P(("dp", "blk"), None),
            P(("dp", "blk"), None),
            P(("dp", "blk"), None),
            P(("dp", "blk"), None),
            P(("dp", "blk")),
            P(("dp", "blk")),
            P(("dp", "blk")),
        ),
        check_vma=False,
    )
```

profile of v0, /device:TPU:0, one launch (start us, length us, event | category | flops | bytes accessed | tf_op | source)
XLA Modules:
  0.0 1560.3 jit_solution(13832257413655477640)
XLA Ops:
  11.3 42.8 %all-reduce.7 = (bf16[1536]{0:T(1024)(128)(2,1)S(1)}, bf16[1536]{0:T(1024)(128)(2,1)S(1)}, bf16[1536]{0:T(1024)(128)(2,1)S(1)}) all-reduce(bf16[1536]{0:T(1024)(128)(2,1)S(1)} %dynamic-update-slice, bf16[1536]{0:T(1024)(128)(2,1)S(1)} %dynamic-update-slice.1, ...), channel_id=1, replica_groups=mesh['dp'=4,'blk'=8] {'dp','blk'}, use_global_device_ids=true, to_apply=%add | all-reduce | flops 4608 | bytes 18432
  58.5 37.6 %all-gather.24.cloned.1.call-done = bf16[1536,3072]{1,0:T(8,128)(2,1)} async-done(((bf16[48,3072]{1,0:T(8,128)(2,1)}), bf16[1536,3072]{1,0:T(8,128)(2,1)}) %all-gather.24.cloned.1.call-update) | async-done | bytes 9437200 | tf_op jit(solution)/shard_map/all_gather | solution.py:144
  96.1 6.9 fusion.26
  111.9 49.4 %all-gather.22.cloned.1.call-done = bf16[1536,1536]{1,0:T(8,128)(2,1)} async-done(((bf16[48,1536]{1,0:T(8,128)(2,1)}), bf16[1536,1536]{1,0:T(8,128)(2,1)}) %all-gather.22.cloned.1.call-update) | async-done | bytes 4718608 | tf_op jit(solution)/shard_map/all_gather | solution.py:143
  165.1 32.5 %all-gather.40.cloned.1.call-done = bf16[4,320,1536]{2,1,0:T(8,128)(2,1)} async-done(((bf16[4,40,1536]{2,1,0:T(8,128)(2,1)}), bf16[4,320,1536]{2,1,0:T(8,128)(2,1)}) %all-gather.40.cloned.1.call-update) | async-done | bytes 3932176 | tf_op jit(solution)/shard_map/all_gather | solution.py:252
  197.6 6.4 copy.113
  204.1 31.0 %all-gather.42.cloned.1.call-done = bf16[4,320,1536]{2,1,0:T(8,128)(2,1)} async-done(((bf16[4,40,1536]{2,1,0:T(8,128)(2,1)}), bf16[4,320,1536]{2,1,0:T(8,128)(2,1)}) %all-gather.42.cloned.1.call-update) | async-done | bytes 3932176 | tf_op jit(solution)/shard_map/all_gather | solution.py:253
  235.1 6.4 copy.115
  241.5 31.0 %all-gather.36.cloned.1.call-done = bf16[4,320,1536]{2,1,0:T(8,128)(2,1)} async-done(((bf16[4,40,1536]{2,1,0:T(8,128)(2,1)}), bf16[4,320,1536]{2,1,0:T(8,128)(2,1)}) %all-gather.36.cloned.1.call-update) | async-done | bytes 3932176 | tf_op jit(solution)/shard_map/all_gather | solution.py:252
  272.5 6.4 copy.106
  278.9 31.5 %all-gather.38.cloned.1.call-done = bf16[4,320,1536]{2,1,0:T(8,128)(2,1)} async-done(((bf16[4,40,1536]{2,1,0:T(8,128)(2,1)}), bf16[4,320,1536]{2,1,0:T(8,128)(2,1)}) %all-gather.38.cloned.1.call-update) | async-done | bytes 3932176 | tf_op jit(solution)/shard_map/all_gather | solution.py:253
  310.4 6.4 copy.108
  316.9 48.3 %all-gather.26.cloned.1.call-done = bf16[8,320,1536]{2,1,0:T(8,128)(2,1)} async-done(((bf16[8,40,1536]{2,1,0:T(8,128)(2,1)}), bf16[8,320,1536]{2,1,0:T(8,128)(2,1)}) %all-gather.26.cloned.1.call-update) | async-done | bytes 7864336 | tf_op jit(solution)/shard_map/all_gather | solution.py:180
  365.1 11.8 copy.102
  382.3 37.5 %all-gather.28.cloned.1.call-done = bf16[8,320,1536]{2,1,0:T(8,128)(2,1)} async-done(((bf16[8,40,1536]{2,1,0:T(8,128)(2,1)}), bf16[8,320,1536]{2,1,0:T(8,128)(2,1)}) %all-gather.28.cloned.1.call-update) | async-done | bytes 7864336 | tf_op jit(solution)/shard_map/all_gather | solution.py:181
  419.8 11.6 copy.104
  431.5 7.9 fusion.98
  439.7 46.7 %all-gather.30.cloned.1.call-done = bf16[1536,1536]{1,0:T(8,128)(2,1)} async-done(((bf16[48,1536]{1,0:T(8,128)(2,1)}), bf16[1536,1536]{1,0:T(8,128)(2,1)}) %all-gather.30.cloned.1.call-update) | async-done | bytes 4718608 | tf_op jit(solution)/shard_map/all_gather | solution.py:145
  495.3 117.3 %all-gather.32.cloned.1.call-done = bf16[1536,6144]{1,0:T(8,128)(2,1)} async-done(((bf16[48,6144]{1,0:T(8,128)(2,1)}), bf16[1536,6144]{1,0:T(8,128)(2,1)}) %all-gather.32.cloned.1.call-update) | async-done | bytes 18874384 | tf_op jit(solution)/shard_map/all_gather | solution.py:146
  612.7 9.4 fusion.115
  622.0 116.4 %all-gather.34.cloned.1.call-done = bf16[1536,6144]{1,0:T(8,128)(2,1)} async-done(((bf16[48,6144]{1,0:T(8,128)(2,1)}), bf16[1536,6144]{1,0:T(8,128)(2,1)}) %all-gather.34.cloned.1.call-update) | async-done | bytes 18874384 | tf_op jit(solution)/shard_map/all_gather | solution.py:147
  738.4 10.9 fusion.15
  749.3 9.8 fusion.4
  795.6 8.7 copy.135
  814.0 8.8 copy.131
  822.7 5.2 copy.143
  832.3 8.7 copy.137
  850.8 8.7 copy.133
  885.6 35.0 %reduce-scatter.32.cloned.1.call-done = bf16[40,6144]{1,0:T(8,128)(2,1)} async-done(((bf16[320,6144]{1,0:T(8,128)(2,1)}), bf16[40,6144]{1,0:T(8,128)(2,1)}) %reduce-scatter.32.cloned.1.call-update) | async-done | bytes 491536
  922.8 51.6 %reduce-scatter.28.cloned.1.call-done = bf16[40,6144]{1,0:T(8,128)(2,1)} async-done(((bf16[320,6144]{1,0:T(8,128)(2,1)}), bf16[40,6144]{1,0:T(8,128)(2,1)}) %reduce-scatter.28.cloned.1.call-update) | async-done | bytes 491536
  976.7 51.2 %reduce-scatter.34.cloned.1.call-done = bf16[40,6144]{1,0:T(8,128)(2,1)} async-done(((bf16[320,6144]{1,0:T(8,128)(2,1)}), bf16[40,6144]{1,0:T(8,128)(2,1)}) %reduce-scatter.34.cloned.1.call-update) | async-done | bytes 491536
  1029.2 52.6 %reduce-scatter.30.cloned.1.call-done = bf16[40,6144]{1,0:T(8,128)(2,1)} async-done(((bf16[320,6144]{1,0:T(8,128)(2,1)}), bf16[40,6144]{1,0:T(8,128)(2,1)}) %reduce-scatter.30.cloned.1.call-update) | async-done | bytes 491536
  1088.3 21.6 %all-gather.56.cloned.1.call-done = bf16[512,1536]{1,0:T(8,128)(2,1)} async-done(((bf16[64,1536]{1,0:T(8,128)(2,1)}), bf16[512,1536]{1,0:T(8,128)(2,1)}) %all-gather.56.cloned.1.call-update) | async-done | bytes 1572880 | tf_op jit(solution)/shard_map/all_gather | solution.py:296
  1113.4 43.9 %all-gather.58.cloned.1.call-done = bf16[512,6144]{1,0:T(8,128)(2,1)} async-done(((bf16[64,6144]{1,0:T(8,128)(2,1)}), bf16[512,6144]{1,0:T(8,128)(2,1)}) %all-gather.58.cloned.1.call-update) | async-done | bytes 6291472 | tf_op jit(solution)/shard_map/all_gather | solution.py:297
  1157.3 5.7 convolution_convert_fusion.1
  1163.0 21.9 %all-gather.60.cloned.1.call-done = bf16[512,1536]{1,0:T(8,128)(2,1)} async-done(((bf16[64,1536]{1,0:T(8,128)(2,1)}), bf16[512,1536]{1,0:T(8,128)(2,1)}) %all-gather.60.cloned.1.call-update) | async-done | bytes 1572880 | tf_op jit(solution)/shard_map/all_gather | solution.py:298
  1188.4 43.9 %all-gather.62.cloned.1.call-done = bf16[512,6144]{1,0:T(8,128)(2,1)} async-done(((bf16[64,6144]{1,0:T(8,128)(2,1)}), bf16[512,6144]{1,0:T(8,128)(2,1)}) %all-gather.62.cloned.1.call-update) | async-done | bytes 6291472 | tf_op jit(solution)/shard_map/all_gather | solution.py:299
  1232.4 5.6 convolution_convert_fusion
  1238.3 48.0 %all-gather.48.cloned.1.call-done = bf16[2560,1536]{1,0:T(8,128)(2,1)} async-done(((bf16[320,1536]{1,0:T(8,128)(2,1)}), bf16[2560,1536]{1,0:T(8,128)(2,1)}) %all-gather.48.cloned.1.call-update) | async-done | bytes 7864336 | tf_op jit(solution)/shard_map/all_gather | solution.py:304
  1286.3 10.5 copy.126
  1300.0 12.5 fusion.38
  1314.1 19.5 %reduce-scatter.22.cloned.1.call-done = bf16[48,1536]{1,0:T(8,128)(2,1)} async-done(((bf16[192,1536]{1,0:T(8,128)(2,1)}), bf16[48,1536]{1,0:T(8,128)(2,1)}) %reduce-scatter.22.cloned.1.call-update) | async-done | bytes 147472 | tf_op jit(solution)/shard_map/reduce_scatter | solution.py:314
  1335.3 6.4 fusion.8
  1341.7 77.5 %all-gather.50.cloned.1.call-done = bf16[2560,3072]{1,0:T(8,128)(2,1)} async-done(((bf16[320,3072]{1,0:T(8,128)(2,1)}), bf16[2560,3072]{1,0:T(8,128)(2,1)}) %all-gather.50.cloned.1.call-update) | async-done | bytes 15728656 | tf_op jit(solution)/shard_map/all_gather | solution.py:305
  1419.2 10.0 convolution_convert_fusion.2
  1436.0 41.6 %all-reduce.6 = (f32[1536]{0:T(1024)S(1)}, f32[1536]{0:T(1024)S(1)}, f32[1536]{0:T(1024)S(1)}) all-reduce(f32[1536]{0:T(1024)S(1)} %get-tuple-element.11, f32[1536]{0:T(1024)S(1)} %get-tuple-element.18, f32[1536]{0:T(1024)S(1)} %get-tuple-element.16), channel_id=11, replica_groups=mesh['dp'=4,'blk'=8] {'dp','blk'}, use_global_device_ids=true, to_apply=%region_25.26.clone | all-reduce | flops 4608 | bytes 36864
  1485.2 35.2 %reduce-scatter.26.cloned.1.call-done = bf16[48,6144]{1,0:T(8,128)(2,1)} async-done(((bf16[192,6144]{1,0:T(8,128)(2,1)}), bf16[48,6144]{1,0:T(8,128)(2,1)}) %reduce-scatter.26.cloned.1.call-update) | async-done | bytes 589840 | tf_op jit(solution)/shard_map/reduce_scatter | solution.py:320
  1522.5 28.7 %reduce-scatter.20.cloned.1.call-done = bf16[48,3072]{1,0:T(8,128)(2,1)} async-done(((bf16[192,3072]{1,0:T(8,128)(2,1)}), bf16[48,3072]{1,0:T(8,128)(2,1)}) %reduce-scatter.20.cloned.1.call-update) | async-done | bytes 294928 | tf_op jit(solution)/shard_map/reduce_scatter | solution.py:311
  (272 shorter events, 165.6 us)
Async XLA Ops:
  7.2 50.8 %copy-start.3 = (bf16[8,8,1536]{2,1,0:T(8,128)(2,1)S(1)}, bf16[8,8,1536]{2,1,0:T(8,128)(2,1)}, u32[]{:S(2)}) copy-start(bf16[8,8,1536]{2,1,0:T(8,128)(2,1)} %param.12) | copy-start | bytes 589828
  7.2 50.4 %copy-start = (bf16[8,32,1536]{2,1,0:T(8,128)(2,1)S(1)}, bf16[8,32,1536]{2,1,0:T(8,128)(2,1)}, u32[]{:S(2)}) copy-start(bf16[8,32,1536]{2,1,0:T(8,128)(2,1)} %param.13) | copy-start | bytes 2359300
  7.2 88.9 %all-gather.24.cloned.1.call-start = ((), (), s32[]{:S(2)}) async-start(), calls=%async_computation.10 | async-start | bytes 9732096 | tf_op jit(solution)/shard_map/all_gather | solution.py:144
  7.9 153.3 %all-gather.22.cloned.1.call-start = ((), (), s32[]{:S(2)}) async-start(), calls=%async_computation.9 | async-start | bytes 4866048 | tf_op jit(solution)/shard_map/all_gather | solution.py:143
  8.7 189.0 %all-gather.40.cloned.1.call-start = ((), (), s32[]{:S(2)}) async-start(), calls=%async_computation.18 | async-start | bytes 4423680 | tf_op jit(solution)/shard_map/all_gather | solution.py:252
  54.1 56.4 %copy-start.25 = (f32[1536]{0:T(1024)}, f32[1536]{0:T(1024)S(1)}, u32[]{:S(2)}) copy-start(f32[1536]{0:T(1024)S(1)} %convert_element_type.162) | copy-start | bytes 18436
  55.2 55.3 %copy-start.30 = (f32[8,8]{1,0:T(8,128)}, f32[8,8]{1,0:T(8,128)S(1)}, u32[]{:S(2)}) copy-start(f32[8,8]{1,0:T(8,128)S(1)} %broadcast_multiply_fusion.8) | copy-start | bytes 772
  57.6 45.4 %copy-start.34 = (f32[8,32]{1,0:T(8,128)}, f32[8,32]{1,0:T(8,128)S(1)}, u32[]{:S(2)}) copy-start(f32[8,32]{1,0:T(8,128)S(1)} %broadcast_multiply_fusion.2) | copy-start | bytes 3076
  58.0 52.5 %copy-start.36 = (f32[8,8]{1,0:T(8,128)}, f32[8,8]{1,0:T(8,128)S(1)}, u32[]{:S(2)}) copy-start(f32[8,8]{1,0:T(8,128)S(1)} %add_rsqrt_fusion.2) | copy-start | bytes 772
  58.0 45.0 %copy-start.38 = (f32[8,32]{1,0:T(8,128)}, f32[8,32]{1,0:T(8,128)S(1)}, u32[]{:S(2)}) copy-start(f32[8,32]{1,0:T(8,128)S(1)} %add_rsqrt_fusion.1) | copy-start | bytes 3076
  58.2 103.1 %copy-start.13 = (bf16[8,8,1536]{2,1,0:T(8,128)(2,1)}, bf16[8,8,1536]{2,1,0:T(8,128)(2,1)S(1)}, u32[]{:S(2)}) copy-start(bf16[8,8,1536]{2,1,0:T(8,128)(2,1)S(1)} %fusion.105) | copy-start | bytes 589828
  58.5 44.5 %copy-start.8 = (bf16[8,32,1536]{2,1,0:T(8,128)(2,1)}, bf16[8,32,1536]{2,1,0:T(8,128)(2,1)S(1)}, u32[]{:S(2)}) copy-start(bf16[8,32,1536]{2,1,0:T(8,128)(2,1)S(1)} %fusion.56) | copy-start | bytes 2359300
  104.4 130.7 %all-gather.42.cloned.1.call-start = ((), (), s32[]{:S(2)}) async-start(), calls=%async_computation.19 | async-start | bytes 4423680 | tf_op jit(solution)/shard_map/all_gather | solution.py:253
  104.9 167.5 %all-gather.36.cloned.1.call-start = ((), (), s32[]{:S(2)}) async-start(), calls=%async_computation.16 | async-start | bytes 4423680 | tf_op jit(solution)/shard_map/all_gather | solution.py:252
  105.5 204.9 %all-gather.38.cloned.1.call-start = ((), (), s32[]{:S(2)}) async-start(), calls=%async_computation.17 | async-start | bytes 4423680 | tf_op jit(solution)/shard_map/all_gather | solution.py:253
  106.1 259.0 %all-gather.26.cloned.1.call-start = ((), (), s32[]{:S(2)}) async-start(), calls=%async_computation.11 | async-start | bytes 8847360 | tf_op jit(solution)/shard_map/all_gather | solution.py:180
  107.6 312.2 %all-gather.28.cloned.1.call-start = ((), (), s32[]{:S(2)}) async-start(), calls=%async_computation.12 | async-start | bytes 8847360 | tf_op jit(solution)/shard_map/all_gather | solution.py:181
  108.4 378.0 %all-gather.30.cloned.1.call-start = ((), (), s32[]{:S(2)}) async-start(), calls=%async_computation.13 | async-start | bytes 4866048 | tf_op jit(solution)/shard_map/all_gather | solution.py:145
  109.1 503.6 %all-gather.32.cloned.1.call-start = ((), (), s32[]{:S(2)}) async-start(), calls=%async_computation.14 | async-start | bytes 19464192 | tf_op jit(solution)/shard_map/all_gather | solution.py:146
  109.7 628.8 %all-gather.34.cloned.1.call-start = ((), (), s32[]{:S(2)}) async-start(), calls=%async_computation.15 | async-start | bytes 19464192 | tf_op jit(solution)/shard_map/all_gather | solution.py:147
  110.4 762.2 %all-gather.44.cloned.1.call-start = ((), (), s32[]{:S(2)}) async-start(), calls=%async_computation.20 | async-start | bytes 1769472 | tf_op jit(solution)/shard_map/all_gather | solution.py:292
  111.3 764.9 %all-gather.46.cloned.1.call-start = ((), (), s32[]{:S(2)}) async-start(), calls=%async_computation.21 | async-start | bytes 1769472 | tf_op jit(solution)/shard_map/all_gather | solution.py:293
  164.9 325.2 %copy-start.17 = (bf16[4,8,16,96]{3,2,1,0:T(8,128)(2,1)}, bf16[4,8,16,96]{3,2,1,0:T(8,128)(2,1)S(1)}, u32[]{:S(2)}) copy-start(bf16[4,8,16,96]{3,2,1,0:T(8,128)(2,1)S(1)} %slice.84) | copy-start | bytes 294916
  165.1 328.3 %copy-start.19 = (bf16[4,8,16,96]{3,2,1,0:T(8,128)(2,1)}, bf16[4,8,16,96]{3,2,1,0:T(8,128)(2,1)S(1)}, u32[]{:S(2)}) copy-start(bf16[4,8,16,96]{3,2,1,0:T(8,128)(2,1)S(1)} %slice.75) | copy-start | bytes 294916
  439.4 50.5 %copy-start.11 = (bf16[8,8,16,96]{3,2,1,0:T(8,128)(2,1)}, bf16[8,8,16,96]{3,2,1,0:T(8,128)(2,1)S(1)}, u32[]{:S(2)}) copy-start(bf16[8,8,16,96]{3,2,1,0:T(8,128)(2,1)S(1)} %copy.105) | copy-start | bytes 589828
  495.3 243.1 %copy-start.15 = (bf16[8,8,1536]{2,1,0:T(8,128)(2,1)S(1)}, bf16[8,8,1536]{2,1,0:T(8,128)(2,1)}, u32[]{:S(2)}) copy-start(bf16[8,8,1536]{2,1,0:T(8,128)(2,1)} %param.15) | copy-start | bytes 589828
  768.1 10.2 slice-start
  788.2 90.9 %all-gather.52.cloned.1.call-start = ((), (), s32[]{:S(2)}) async-start(), calls=%async_computation.26 | async-start | bytes 1769472 | tf_op jit(solution)/shard_map/all_gather | solution.py:294
  790.1 92.6 %all-gather.54.cloned.1.call-start = ((), (), s32[]{:S(2)}) async-start(), calls=%async_computation.27 | async-start | bytes 1769472 | tf_op jit(solution)/shard_map/all_gather | solution.py:295
  790.7 129.8 %reduce-scatter.32.cloned.1.call-start = ((), (), s32[]{:S(2)}) async-start(), calls=%async_computation.37 | async-start | bytes 4423680
  809.5 164.9 %reduce-scatter.28.cloned.1.call-start = ((), (), s32[]{:S(2)}) async-start(), calls=%async_computation.35 | async-start | bytes 4423680
  827.9 199.9 %reduce-scatter.34.cloned.1.call-start = ((), (), s32[]{:S(2)}) async-start(), calls=%async_computation.38 | async-start | bytes 4423680
  846.2 235.6 %reduce-scatter.30.cloned.1.call-start = ((), (), s32[]{:S(2)}) async-start(), calls=%async_computation.36 | async-start | bytes 4423680
  864.7 245.2 %all-gather.56.cloned.1.call-start = ((), (), s32[]{:S(2)}) async-start(), calls=%async_computation.29 | async-start | bytes 1769472 | tf_op jit(solution)/shard_map/all_gather | solution.py:296
  865.3 292.0 %all-gather.58.cloned.1.call-start = ((), (), s32[]{:S(2)}) async-start(), calls=%async_computation.30 | async-start | bytes 7077888 | tf_op jit(solution)/shard_map/all_gather | solution.py:297
  866.0 318.9 %all-gather.60.cloned.1.call-start = ((), (), s32[]{:S(2)}) async-start(), calls=%async_computation.32 | async-start | bytes 1769472 | tf_op jit(solution)/shard_map/all_gather | solution.py:298
  866.7 365.6 %all-gather.62.cloned.1.call-start = ((), (), s32[]{:S(2)}) async-start(), calls=%async_computation.33 | async-start | bytes 7077888 | tf_op jit(solution)/shard_map/all_gather | solution.py:299
  871.3 415.0 %all-gather.48.cloned.1.call-start = ((), (), s32[]{:S(2)}) async-start(), calls=%async_computation.23 | async-start | bytes 8847360 | tf_op jit(solution)/shard_map/all_gather | solution.py:304
  872.5 440.0 %reduce-scatter.18.cloned.1.call-start = ((), (), s32[]{:S(2)}) async-start(), calls=%async_computation.22 | async-start | bytes 737280 | tf_op jit(solution)/shard_map/reduce_scatter | solution.py:308
  879.0 454.6 %reduce-scatter.22.cloned.1.call-start = ((), (), s32[]{:S(2)}) async-start(), calls=%async_computation.28 | async-start | bytes 737280 | tf_op jit(solution)/shard_map/reduce_scatter | solution.py:314
  885.5 533.7 %all-gather.50.cloned.1.call-start = ((), (), s32[]{:S(2)}) async-start(), calls=%async_computation.24 | async-start | bytes 17694720 | tf_op jit(solution)/shard_map/all_gather | solution.py:305
  1088.2 394.8 %reduce-scatter.24.cloned.1.call-start = ((), (), s32[]{:S(2)}) async-start(), calls=%async_computation.31 | async-start | bytes 2949120 | tf_op jit(solution)/shard_map/reduce_scatter | solution.py:317
  1163.0 357.4 %reduce-scatter.26.cloned.1.call-start = ((), (), s32[]{:S(2)}) async-start(), calls=%async_computation.34 | async-start | bytes 2949120 | tf_op jit(solution)/shard_map/reduce_scatter | solution.py:320
  1238.0 313.3 %reduce-scatter.20.cloned.1.call-start = ((), (), s32[]{:S(2)}) async-start(), calls=%async_computation.25 | async-start | bytes 1474560 | tf_op jit(solution)/shard_map/reduce_scatter | solution.py:311
  1419.2 10.1 copy-start.33
  1419.2 10.1 copy-start.35
  1419.2 10.1 copy-start.39
  1431.3 48.1 %copy-start.5 = (f32[8,8,1536]{2,1,0:T(8,128)S(1)}, f32[8,8,1536]{2,1,0:T(8,128)}, u32[]{:S(2)}) copy-start(f32[8,8,1536]{2,1,0:T(8,128)} %copy-done.4) | copy-start | bytes 1179652
  (29 other events, 74.8 us)
Sparse Core Ops, SparseCore 0:
  10.9 85.1 all-gather.23
  99.0 62.2 all-gather.21
  163.2 34.4 all-gather.39
  199.4 35.6 all-gather.41
  236.8 35.6 all-gather.35
  274.8 35.6 all-gather.37
  312.9 52.1 all-gather.25
  367.6 52.1 all-gather.27
  422.7 63.6 all-gather.29
  489.1 123.4 all-gather.31
  615.6 122.8 all-gather.33
  740.2 23.8 all-gather.43
  788.3 23.8 all-gather.45
  813.9 25.6 all-gather.51
  841.4 25.6 all-gather.53
  870.5 50.0 reduce-scatter.31
  924.3 50.0 reduce-scatter.27
  977.8 50.0 reduce-scatter.33
  1031.8 50.0 reduce-scatter.29
  1084.1 25.6 all-gather.55
  1111.7 45.5 all-gather.57
  1159.2 25.6 all-gather.59
  1186.8 45.5 all-gather.61
  1234.1 52.1 all-gather.47
  1289.2 22.0 reduce-scatter.17
  1313.3 20.2 reduce-scatter.21
  1335.3 83.8 all-gather.49
  1421.5 48.9 reduce-scatter.23
  1472.8 47.4 reduce-scatter.25
  1522.5 28.6 reduce-scatter.19
where the time goes:
time: 1570 us; the launch traced here: 1560 us
  waiting for transfers between devices  1120 us (71%)
  local copies, waits for them, and re-layouts  166 us (11%)
  matrix products  141 us (9%)
  blocking collectives  84.4 us (5%)
  other arithmetic  32.2 us (2%)
    unnamed x34, waiting for transfers between devices  199 us
    all_gather x1, waiting for transfers between devices, body(): lax.all_gather(in_weight, ('dp', 'blk'), axis=0, tiled=True)  117 us
    all_gather x1, waiting for transfers between devices, body(): lax.all_gather(down_weight, ('dp', 'blk'), axis=0, tiled=True)  116 us
    unnamed x2, blocking collectives  84.4 us
    all_gather x1, waiting for transfers between devices, body(): lax.all_gather(flat_rows(kv_out_grad), 'blk', axis=0, tiled=True)  77.5 us
    unnamed x117, local copies, waits for them, and re-layouts  73.4 us
    all_gather x2, waiting for transfers between devices, body(): lax.all_gather(keys[lower:upper], 'blk', axis=1, tiled=True)  63.5 us
    all_gather x2, waiting for transfers between devices, body(): lax.all_gather(values_proj[lower:upper], 'blk', axis=1, tiled=True)  62.5 us
  transfers between devices with their start and end apart: 30, of which 24 were waited for; matrix products, arithmetic and copies ran while one was open for 21% of the time, Pallas kernels for 0%

commit v1 on v0

v1 whole, which is shorter than its diff:
```python
from functools import partial
import math

import jax
import jax.numpy as jnp
from jax import lax
from jax.experimental import pallas as pl
from jax.experimental.pallas import tpu as pltpu
from jax.sharding import PartitionSpec as P

HEADS = 16
NORM_EPS = 1e-05
MASKED = -1e30
GAUSS_DENSITY = 0.3989422804014327
BF = jnp.bfloat16
F32 = jnp.float32
MIB = 1 << 20


def swap(array, bit, axis="blk"):
    return lax.ppermute(array, axis, [(i, i ^ bit) for i in range(lax.axis_size(axis))])


def gather_slots(block):
    count = lax.axis_size("blk")
    half = block.shape[0] // 2
    slots = {0: block}
    for offset in range(2, count, 2):
        low = offset & -offset
        high = 1 << (offset.bit_length() - 1)
        if low == high:
            slots[offset] = swap(block, offset)
    for offset in range(2, count, 2):
        low = offset & -offset
        high = 1 << (offset.bit_length() - 1)
        if low != high:
            slots[offset] = jnp.concatenate(
                [swap(slots[offset ^ low][:half], low), swap(slots[offset ^ high][half:], high)], 0
            )
    for offset in range(0, count, 2):
        slots[offset + 1] = swap(slots[offset], 1)
    return [slots[k] for k in range(count)]


def scatter_sum(even, odd):
    total = even.astype(F32) + swap(odd, 1).astype(F32)
    pairs, rows, width = total.shape
    bits = pairs.bit_length() - 1
    half = rows // 2
    shaped = total.reshape((2,) * bits + (rows, width))
    first, second = shaped[..., :half, :], shaped[..., half:, :]
    for step in range(bits):
        send = first[..., 1, :, :]
        got = swap(send.astype(BF), 2 << step)
        keep = first[..., 0, :, :]
        send_b = second[1]
        got_b = swap(send_b.astype(BF), 2 << (bits - 1 - step))
        keep_b = second[0]
        if step == bits - 1:
            return (keep, got), (keep_b, got_b)
        first = keep + got.astype(F32)
        second = keep_b + got_b.astype(F32)


def joined(halves):
    return jnp.concatenate([keep + got.astype(F32) for keep, got in halves], 0)


def normalize(values):
    center = values - jnp.mean(values, -1, keepdims=True)
    inverse = lax.rsqrt(jnp.mean(center * center, -1, keepdims=True) + NORM_EPS)
    return (center * inverse, inverse)


def norm_back(grad_norm, normed, inverse):
    return inverse * (
        grad_norm
        - jnp.mean(grad_norm, -1, keepdims=True)
        - normed * jnp.mean(grad_norm * normed, -1, keepdims=True)
    )


def dot(left, right, dims=((1,), (0,))):
    return lax.dot_general(left, right, (dims, ((), ())), preferred_element_type=F32)


NT = ((1,), (1,))
TN = ((0,), (0,))


def call(kernel, out_shapes, smem=0, vmem=48):
    def run(*operands):
        specs = [
            pl.BlockSpec(memory_space=pltpu.SMEM if i < smem else pltpu.VMEM)
            for i in range(len(operands))
        ]
        outs = [jax.ShapeDtypeStruct(shape, kind) for shape, kind in out_shapes]
        return pl.pallas_call(
            kernel,
            out_shape=outs,
            in_specs=specs,
            out_specs=[pl.BlockSpec(memory_space=pltpu.VMEM)] * len(outs),
            compiler_params=pltpu.CompilerParams(vmem_limit_bytes=vmem * MIB),
        )(*operands)

    return run


def project_kernel(count, *refs):
    media, lats = refs[:count], refs[count : 2 * count]
    w_media, w_lat, kv_out, lat_out = refs[2 * count :]
    rows, lat_rows = media[0].shape[0], lats[0].shape[0]
    for k in range(count):
        kv_out[k * rows : (k + 1) * rows, :] = dot(media[k][...], w_media[...]).astype(BF)
    for k in range(count):
        lat_out[k * lat_rows : (k + 1) * lat_rows, :] = dot(lats[k][...], w_lat[...])


def head_masks(rows, width, heads, size):
    lane = lax.broadcasted_iota(jnp.int32, (rows, width), 1)
    return [(lane >= h * size) & (lane < (h + 1) * size) for h in range(heads)]


def stacked(values, masks):
    return jnp.concatenate([jnp.where(m, values, jnp.zeros_like(values)) for m in masks], 0)


def unstacked(values, masks):
    rows = values.shape[0] // len(masks)
    total = jnp.zeros((rows, values.shape[1]), F32)
    for h, m in enumerate(masks):
        total = jnp.where(m, values[h * rows : (h + 1) * rows], total)
    return total


def media_allowed(me, length, count, media_rows, rows):
    column = lax.broadcasted_iota(jnp.int32, (rows, count * media_rows), 1)
    slot = column // media_rows
    index = (slot ^ me) * media_rows + column % media_rows
    return index < length


def attend_kernel(
    count, heads, size, me_ref, len_ref, kv_ref, lat_ref, wo_ref, att_ref, lse_ref, even_ref, odd_ref
):
    images, pad = kv_ref.shape[1], wo_ref.shape[0]
    media_rows = kv_ref.shape[2]
    lat_rows = lat_ref.shape[2]
    rows = count * lat_rows
    scale = 1.0 / math.sqrt(size)
    masks = head_masks(rows, pad, heads, size)
    me = me_ref[0]
    for i in range(images):
        keys = kv_ref[:, i, :, :pad].reshape(count * media_rows, pad)
        values = kv_ref[:, i, :, pad:].reshape(count * media_rows, pad)
        lat = lat_ref[:, i].reshape(rows, 3 * pad).astype(BF)
        lat_keys, lat_values = lat[:, :pad], lat[:, pad : 2 * pad]
        queries = stacked(lat[:, 2 * pad :], masks)
        allowed = media_allowed(me, len_ref[i], count, media_rows, heads * rows)
        scores = jnp.where(allowed, dot(queries, keys, NT) * scale, MASKED)
        lat_scores = dot(queries, lat_keys, NT) * scale
        top = jnp.maximum(
            jnp.max(scores, -1, keepdims=True), jnp.max(lat_scores, -1, keepdims=True)
        )
        probs = jnp.where(allowed, jnp.exp(scores - top), 0.0)
        lat_probs = jnp.exp(lat_scores - top)
        denominator = jnp.sum(probs, -1, keepdims=True) + jnp.sum(lat_probs, -1, keepdims=True)
        weighted = dot(probs.astype(BF), values) + dot(lat_probs.astype(BF), lat_values)
        attended = unstacked(weighted / denominator, masks)
        att_ref[:, i] = attended.reshape(count, lat_rows, pad)
        lse_ref[i] = jnp.broadcast_to(top + jnp.log(denominator), (heads * rows, 128))
    flat = att_ref[...].reshape(count * images * lat_rows, pad).astype(BF)
    part = dot(flat, wo_ref[...]).astype(BF)
    block = images * lat_rows
    for k in range(count):
        out = odd_ref if k % 2 else even_ref
        out[k // 2] = part[k * block : (k + 1) * block]


def attend_back_kernel(
    count,
    heads,
    size,
    me_ref,
    len_ref,
    kv_ref,
    lat_ref,
    wo_ref,
    att_ref,
    lse_ref,
    *refs,
):
    branch = refs[:count]
    dkv_ref, dlat_ref, dlat_wide, datt_wide = refs[count:]
    images, pad = kv_ref.shape[1], wo_ref.shape[0]
    media_rows = kv_ref.shape[2]
    lat_rows = lat_ref.shape[2]
    rows = count * lat_rows
    scale = 1.0 / math.sqrt(size)
    masks = head_masks(rows, pad, heads, size)
    me = me_ref[0]
    for k in range(count):
        part = dot(branch[k][...], wo_ref[...], NT)
        datt_wide[k] = part.reshape(images, lat_rows, pad)
    for i in range(images):
        keys = kv_ref[:, i, :, :pad].reshape(count * media_rows, pad)
        values = kv_ref[:, i, :, pad:].reshape(count * media_rows, pad)
        lat = lat_ref[:, i].reshape(rows, 3 * pad).astype(BF)
        lat_keys, lat_values = lat[:, :pad], lat[:, pad : 2 * pad]
        queries = stacked(lat[:, 2 * pad :], masks)
        grads = datt_wide[:, i].reshape(rows, pad).astype(BF)
        attended = att_ref[:, i].reshape(rows, pad)
        grad_heads = stacked(grads, masks)
        product = stacked(grads.astype(F32) * attended, masks)
        delta = jnp.sum(product, -1, keepdims=True)
        total = lse_ref[i][:, :1]
        allowed = media_allowed(me, len_ref[i], count, media_rows, heads * rows)
        scores = jnp.where(allowed, dot(queries, keys, NT) * scale, MASKED)
        lat_scores = dot(queries, lat_keys, NT) * scale
        probs = jnp.where(allowed, jnp.exp(scores - total), 0.0)
        lat_probs = jnp.exp(lat_scores - total)
        score_grad = (probs * (dot(grad_heads, values, NT) - delta)).astype(BF)
        lat_score_grad = (lat_probs * (dot(grad_heads, lat_values, NT) - delta)).astype(BF)
        query_grad = scale * unstacked(dot(score_grad, keys) + dot(lat_score_grad, lat_keys), masks)
        dkv_ref[:, i, :, :pad] = (
            (scale * dot(score_grad, queries, TN)).astype(BF).reshape(count, media_rows, pad)
        )
        dkv_ref[:, i, :, pad:] = (
            dot(probs.astype(BF), grad_heads, TN).astype(BF).reshape(count, media_rows, pad)
        )
        lat_grad = jnp.concatenate(
            [
                scale * dot(lat_score_grad, queries, TN),
                dot(lat_probs.astype(BF), grad_heads, TN),
                query_grad,
            ],
            1,
        )
        dlat_wide[:, i] = lat_grad.reshape(count, lat_rows, 3 * pad)
    block = images * lat_rows
    dlat_ref[...] = dlat_wide[...].reshape(count * block, 3 * pad).astype(BF)


def input_grad_kernel(count, dkv_ref, dlat_ref, w_media, w_lat, even, odd, even_lat, odd_lat):
    rows = dkv_ref.shape[0] // count
    lat_rows = dlat_ref.shape[0] // count
    for k in range(count):
        out, out_lat = (odd, odd_lat) if k % 2 else (even, even_lat)
        out[k // 2] = dot(dkv_ref[k * rows : (k + 1) * rows, :], w_media[...], NT).astype(BF)
        out_lat[k // 2] = dot(
            dlat_ref[k * lat_rows : (k + 1) * lat_rows, :], w_lat[...], NT
        ).astype(BF)


def erf_parts(values):
    cdf = 0.5 * (1.0 + lax.erf(values * 0.7071067811865476))
    return cdf, cdf + values * jnp.exp(-0.5 * values * values) * GAUSS_DENSITY


def ffn_kernel(count, *refs):
    rows_in, cots = refs[:count], refs[count : 2 * count]
    w_in, w_down, hidden_ref, pre_ref, even, odd = refs[2 * count :]
    rows = rows_in[0].shape[0]
    for k in range(count):
        pre = dot(rows_in[k][...], w_in[...])
        cdf, slope = erf_parts(pre)
        hidden_ref[k * rows : (k + 1) * rows, :] = (pre * cdf).astype(BF)
        back = dot(cots[k][...], w_down[...])
        pre_grad = (back * slope).astype(BF)
        pre_ref[k * rows : (k + 1) * rows, :] = pre_grad
        out = odd if k % 2 else even
        out[k // 2] = dot(pre_grad, w_in[...], NT).astype(BF)


def down_kernel(count, hidden_ref, w_down, even, odd):
    rows = hidden_ref.shape[0] // count
    for k in range(count):
        out = odd if k % 2 else even
        out[k // 2] = dot(hidden_ref[k * rows : (k + 1) * rows, :], w_down[...], NT).astype(BF)


def weight_grad_kernel(count, *refs):
    lefts, right, out = refs[:count], refs[count], refs[count + 1]
    left = jnp.concatenate([r[...] for r in lefts], 0)
    out[...] = dot(left, right[...], TN).astype(out.dtype)


def body(
    latents,
    media,
    media_lengths,
    cotangent,
    query_weight,
    kv_weight,
    out_weight,
    in_weight,
    down_weight,
    media_gain,
    latent_gain,
    ffn_gain,
):
    images, lat_rows, width = latents.shape
    media_rows = media.shape[1]
    nb, nd = lax.axis_size("blk"), lax.axis_size("dp")
    size = width // HEADS
    heads = HEADS // nb
    own = query_weight.shape[0]
    span = heads * size
    pad = -(-span // 128) * 128
    hidden_width = in_weight.shape[1]
    part_hidden = hidden_width // nb
    me = lax.axis_index("blk").astype(jnp.int32).reshape(1)
    ring = size // own
    per_ring = nd // ring
    groups = nb // ring

    def by_owner(weight):
        shaped = weight.reshape(own, ring, per_ring, groups, size)
        return shaped.transpose(3, 1, 0, 2, 4).reshape(nb, own, span)

    def from_owner(slots):
        shaped = slots.reshape(groups, ring, own, per_ring, size)
        return shaped.transpose(2, 1, 3, 0, 4).reshape(own, width)

    g_media, g_lat, g_ffn = (g.astype(F32)[:, None] for g in (media_gain, latent_gain, ffn_gain))
    q_scaled = (query_weight * g_lat).astype(BF)
    in_scaled = (in_weight * g_ffn).astype(BF)
    extra = (-(3 * span + 2)) % 128 + 2
    gain_columns = jnp.concatenate(
        [media_gain[:, None], latent_gain[:, None], jnp.zeros((own, extra - 2), BF)], 1
    )
    attn_parts = jnp.concatenate(
        [
            by_owner(kv_weight[:, :width]),
            by_owner(kv_weight[:, width:]),
            by_owner(q_scaled),
            jnp.broadcast_to(gain_columns, (nb, own, extra)),
        ],
        2,
    )
    ffn_parts = jnp.concatenate(
        [
            in_scaled.reshape(own, nb, part_hidden).transpose(1, 0, 2),
            down_weight.reshape(own, nb, part_hidden).transpose(1, 0, 2),
        ],
        2,
    )

    def columns(parts):
        mine = lax.all_to_all(parts, "blk", 0, 0, tiled=True)
        return lax.all_gather(mine.reshape(nb * own, -1), "dp", axis=0, tiled=True)

    attn_w = columns(attn_parts)
    ffn_w = columns(ffn_parts)
    all_out = lax.all_gather(out_weight, "dp", axis=0, tiled=False)
    ring_groups = [[g * ring + i for i in range(ring)] for g in range(groups)]
    out_w = lax.all_to_all(
        all_out.reshape(ring, per_ring, own, width), "blk", 0, 0, axis_index_groups=ring_groups
    )
    out_w = out_w.transpose(1, 0, 2, 3).reshape(span, width)
    out_w = jnp.pad(out_w, ((0, pad - span), (0, 0)))

    lat_float = latents.astype(F32).reshape(images * lat_rows, width)
    media_float = media.astype(F32).reshape(images * media_rows, width)
    media_norm, media_inverse = normalize(media_float)
    lat_norm, lat_inverse = normalize(lat_float)
    media_slots = gather_slots(media_norm.astype(BF))
    lat_slots = gather_slots(lat_norm.astype(BF))
    cot_flat = cotangent.reshape(images * lat_rows, width)
    cot_slots = gather_slots(cot_flat)

    def padded(block):
        return jnp.pad(block, ((0, 0), (0, pad - span)))

    w_k, w_v = attn_w[:, :span].astype(F32), attn_w[:, span : 2 * span].astype(F32)
    w_q = attn_w[:, 2 * span : 3 * span]
    row_media = attn_w[:, 3 * span : 3 * span + 1].astype(F32)
    row_lat = attn_w[:, 3 * span + 1 : 3 * span + 2].astype(F32)
    w_media = jnp.concatenate(
        [padded((w_k * row_media).astype(BF)), padded((w_v * row_media).astype(BF))], 1
    )
    w_lat = jnp.concatenate(
        [padded((w_k * row_lat).astype(BF)), padded((w_v * row_lat).astype(BF)), padded(w_q)], 1
    )
    all_media, all_lat = nb * images * media_rows, nb * images * lat_rows
    kv, lat_proj = call(
        partial(project_kernel, nb),
        [((all_media, 2 * pad), BF), ((all_lat, 3 * pad), F32)],
    )(*media_slots, *lat_slots, w_media, w_lat)
    kv4 = kv.reshape(nb, images, media_rows, 2 * pad)
    lat4 = lat_proj.reshape(nb, images, lat_rows, 3 * pad)
    half_shape = (nb // 2, images * lat_rows, width)
    attended, totals, even, odd = call(
        partial(attend_kernel, nb, heads, size),
        [
            ((nb, images, lat_rows, pad), F32),
            ((images, heads * nb * lat_rows, 128), F32),
            (half_shape, BF),
            (half_shape, BF),
        ],
        smem=2,
    )(me, media_lengths, kv4, lat4, out_w)
    mixed = lat_float + joined(scatter_sum(even, odd))
    ffn_norm, ffn_inverse = normalize(mixed)
    ffn_slots = gather_slots(ffn_norm.astype(BF))
    w_in, w_down = ffn_w[:, :part_hidden], ffn_w[:, part_hidden:]
    hidden, pre_grad, even, odd = call(
        partial(ffn_kernel, nb),
        [((all_lat, part_hidden), BF), ((all_lat, part_hidden), BF), (half_shape, BF), (half_shape, BF)],
    )(*ffn_slots, *cot_slots, w_in, w_down)
    ffn_back = joined(scatter_sum(even, odd))
    even, odd = call(partial(down_kernel, nb), [(half_shape, BF), (half_shape, BF)])(hidden, w_down)
    resampled = (mixed + joined(scatter_sum(even, odd))).astype(BF).reshape(latents.shape)
    mixed_grad = cot_flat.astype(F32) + norm_back(ffn_back, ffn_norm, ffn_inverse)
    branch_slots = gather_slots(mixed_grad.astype(BF))
    kv_grad, lat_grad = pl.pallas_call(
        partial(attend_back_kernel, nb, heads, size),
        out_shape=[
            jax.ShapeDtypeStruct(kv4.shape, BF),
            jax.ShapeDtypeStruct((all_lat, 3 * pad), BF),
        ],
        in_specs=[pl.BlockSpec(memory_space=pltpu.SMEM)] * 2
        + [pl.BlockSpec(memory_space=pltpu.VMEM)] * (5 + nb),
        out_specs=[pl.BlockSpec(memory_space=pltpu.VMEM)] * 2,
        scratch_shapes=[
            pltpu.VMEM((nb, images, lat_rows, 3 * pad), F32),
            pltpu.VMEM((nb, images, lat_rows, pad), F32),
        ],
        compiler_params=pltpu.CompilerParams(vmem_limit_bytes=48 * MIB),
    )(me, media_lengths, kv4, lat4, out_w, attended, totals, *branch_slots)
    kv_grad = kv_grad.reshape(all_media, 2 * pad)
    media_half = (nb // 2, images * media_rows, width)
    even, odd, even_lat, odd_lat = call(
        partial(input_grad_kernel, nb),
        [(media_half, BF), (media_half, BF), (half_shape, BF), (half_shape, BF)],
    )(kv_grad, lat_grad, w_media, w_lat)
    media_back = joined(scatter_sum(even, odd))
    lat_back = joined(scatter_sum(even_lat, odd_lat))
    media_grad = norm_back(media_back, media_norm, media_inverse).reshape(media.shape)
    latents_grad = (mixed_grad + norm_back(lat_back, lat_norm, lat_inverse)).reshape(latents.shape)

    grad_of = partial(weight_grad_kernel, nb)
    (g_in,) = call(grad_of, [((width, part_hidden), BF)])(*ffn_slots, pre_grad)
    (g_down,) = call(grad_of, [((width, part_hidden), BF)])(*cot_slots, hidden)
    att_flat = attended.reshape(all_lat, pad).astype(BF)
    branch_all = jnp.concatenate(branch_slots, 0)
    g_out = dot(att_flat, branch_all, TN)[:span].astype(BF)
    (g_media_kv,) = call(grad_of, [((width, 2 * pad), F32)])(*media_slots, kv_grad)
    (g_lat_qkv,) = call(grad_of, [((width, 3 * pad), F32)])(*lat_slots, lat_grad)
    gm_k, gm_v = g_media_kv[:, :span], g_media_kv[:, pad : pad + span]
    gl_k, gl_v = g_lat_qkv[:, :span], g_lat_qkv[:, pad : pad + span]
    gl_q = g_lat_qkv[:, 2 * pad : 2 * pad + span]
    gain_media = jnp.sum(gm_k * w_k + gm_v * w_v, 1, keepdims=True)
    gain_lat = jnp.sum(gl_k * w_k + gl_v * w_v, 1, keepdims=True)
    attn_grads = jnp.concatenate(
        [
            gm_k * row_media + gl_k * row_lat,
            gm_v * row_media + gl_v * row_lat,
            gl_q,
            gain_media,
            gain_lat,
            jnp.zeros((width, extra - 2), F32),
        ],
        1,
    ).astype(BF)

    def rows_of(grads):
        summed = lax.psum_scatter(grads, "dp", scatter_dimension=0, tiled=True)
        return lax.all_to_all(summed.reshape(nb, own, -1), "blk", 0, 0, tiled=True)

    in_slots = rows_of(g_in).astype(F32)
    down_slots = rows_of(g_down).astype(F32)
    attn_slots = rows_of(attn_grads).astype(F32)
    out_slots = lax.all_to_all(
        g_out.reshape(per_ring, ring, own, width).transpose(1, 0, 2, 3),
        "blk",
        0,
        0,
        axis_index_groups=ring_groups,
    )
    out_grad = lax.psum_scatter(
        out_slots.reshape(nd * own, width), "dp", scatter_dimension=0, tiled=True
    ).astype(F32)
    in_raw = in_slots.transpose(1, 0, 2).reshape(own, hidden_width)
    down_grad = down_slots.transpose(1, 0, 2).reshape(own, hidden_width)
    kv_out = jnp.concatenate(
        [from_owner(attn_slots[..., :span]), from_owner(attn_slots[..., span : 2 * span])], 1
    )
    q_raw = from_owner(attn_slots[..., 2 * span : 3 * span])
    gains = jnp.sum(attn_slots[..., 3 * span : 3 * span + 2], 0)
    media_gain_grad = gains[:, 0]
    latent_gain_grad = gains[:, 1] + jnp.sum(q_raw * query_weight.astype(F32), 1)
    ffn_gain_grad = jnp.sum(in_raw * in_weight.astype(F32), 1)
    return (
        resampled,
        latents_grad,
        media_grad,
        q_raw * g_lat,
        kv_out,
        out_grad,
        in_raw * g_ffn,
        down_grad,
        media_gain_grad,
        latent_gain_grad,
        ffn_gain_grad,
    )


def solution(mesh):
    rows = P("dp", "blk", None)
    weight = P(("dp", "blk"), None)
    gain = P(("dp", "blk"))
    return jax.shard_map(
        body,
        mesh=mesh,
        in_specs=(rows, rows, P("dp"), rows) + (weight,) * 5 + (gain,) * 3,
        out_specs=(rows,) * 3 + (weight,) * 5 + (gain,) * 3,
        check_vma=False,
    )
```

time: 1570 us -> 468 us (0.30)
  waiting for transfers between devices: 1120 us -> 145 us
  matrix products: 141 us -> 0.59 us
  local copies, waits for them, and re-layouts: 166 us -> 75.7 us
  Pallas kernels: 0 us -> 79.7 us
  starting transfers between devices: 2.05 us -> 77.9 us
  blocking collectives: 84.4 us -> 22.7 us
    all_gather x21 -> x2, waiting for transfers between devices: 836 us -> 11.8 us  [columns(): return lax.all_gather(mine.reshape(nb * own, -1), 'dp', axis=0, tiled=True)]
    unnamed x34 -> x6, waiting for transfers between devices: 199 us -> 0.76 us
    dot_general x27 -> x1, matrix products: 141 us -> 0.59 us  [dot(): lax.dot_general(left, right, (dims, ((), ())), preferred_element_type=F32)]
    ppermute x0 -> x65, waiting for transfers between devices: none -> 86.4 us  [swap(): lax.ppermute(array, axis, [(i, i ^ bit) for i in range(lax.axis_size(axis...]
    unnamed x2 -> x0, blocking collectives: 84.4 us -> none
    pallas_call x0 -> x10, Pallas kernels: none -> 79.7 us  [the longest x9 71.6 us: run(): pl.pallas_call(kernel, out_shape=outs, in_specs=specs, out_specs=[pl.Bloc...]
    all_gather x11 -> x0, local copies, waits for them, and re-layouts: 70.1 us -> none  [the longest x2 12.9 us: body(): lax.all_gather(keys[lower:upper], 'blk', axis=1, tiled=True)]
    ppermute x0 -> x65, starting transfers between devices: none -> 55.4 us  [swap(): lax.ppermute(array, axis, [(i, i ^ bit) for i in range(lax.axis_size(axis...]
  transfers between devices with their start and end apart: 30 -> 77, of which waited for: 24 -> 32; matrix products, arithmetic and copies ran while one was open for 21% -> 15% of each run, Pallas kernels for 0% -> 14%
where the time goes in v1:
time: 468 us; the launch traced here: 460 us
  waiting for transfers between devices  145 us (31%)
  Pallas kernels  79.7 us (17%)
  starting transfers between devices  77.9 us (17%)
  local copies, waits for them, and re-layouts  75.7 us (16%)
  other arithmetic  42.4 us (9%)
  blocking collectives  22.7 us (5%)
  between operations  16.1 us (3%)
    ppermute x65, waiting for transfers between devices, swap(): lax.ppermute(array, axis, [(i, i ^ bit) for i in range(lax.axis_size(axis...  86.4 us
    pallas_call x9, Pallas kernels, run(): pl.pallas_call(kernel, out_shape=outs, in_specs=specs, out_specs=[pl.Bloc...  71.6 us
    ppermute x65, starting transfers between devices, swap(): lax.ppermute(array, axis, [(i, i ^ bit) for i in range(lax.axis_size(axis...  55.4 us
    unnamed x227, local copies, waits for them, and re-layouts  40.6 us
    reduce_scatter x3, waiting for transfers between devices, rows_of(): summed = lax.psum_scatter(grads, 'dp', scatter_dimension=0, tiled=True)  40.6 us
    all_gather x1, blocking collectives, body(): all_out = lax.all_gather(out_weight, 'dp', axis=0, tiled=False)  17.6 us
    all_gather x2, waiting for transfers between devices, columns(): return lax.all_gather(mine.reshape(nb * own, -1), 'dp', axis=0, tiled=True)  11.8 us
    all_to_all x3, starting transfers between devices, rows_of(): return lax.all_to_all(summed.reshape(nb, own, -1), 'blk', 0, 0, tiled=True)  10.8 us
  transfers between devices with their start and end apart: 77, of which 32 were waited for; matrix products, arithmetic and copies ran while one was open for 15% of the time, Pallas kernels for 14%

profile of v1, /device:TPU:0, one launch (start us, length us, event | category | flops | bytes accessed | tf_op | source)
XLA Modules:
  0.0 460.4 jit_solution(4867273711630346499)
XLA Ops:
  10.6 3.0 collective-permute-start.3
  19.1 3.5 all-to-all-start
  23.0 17.6 %all-gather = bf16[192,1536]{1,0:T(8,128)(2,1)} all-gather(bf16[48,1536]{1,0:T(8,128)(2,1)S(1)} %copy-done.83), channel_id=2, replica_groups=mesh['dp'=4,'blk'=8] {'dp'}, dimensions={0}, use_global_device_ids=true | all-gather | bytes 737280 | tf_op jit(solution)/shard_map/all_gather | solution.py:355
  41.4 3.5 all-to-all-start.1
  48.3 4.3 all-to-all-start.2
  52.8 1.9 collective-permute-start.11
  56.2 16.4 %collective-permute-done.11.refs_12_.refs_4_ = bf16[64,1536]{1,0:T(8,128)(2,1)S(1)} collective-permute-done((bf16[64,1536]{1,0:T(8,128)(2,1)S(1)}, bf16[64,1536]{1,0:T(8,128)(2,1)S(1)}, u32[]{:S(2)}, u32[]{:S(2)}) %collective-permute-start.11) | collective-permute-done | bytes 196640 | tf_op jit(solution)/shard_map/ppermute | solution.py:21
  83.4 5.5 %collective-permute-done.5 = bf16[128,1536]{1,0:T(8,128)(2,1)} collective-permute-done((bf16[128,1536]{1,0:T(8,128)(2,1)}, bf16[128,1536]{1,0:T(8,128)(2,1)}, u32[]{:S(2)}, u32[]{:S(2)}) %collective-permute-start.5) | collective-permute-done | bytes 393248 | tf_op jit(solution)/shard_map/ppermute | solution.py:21
  90.6 3.5 collective-permute-done.6
  97.6 2.5 fusion.9
  106.1 11.3 %shard_map.203 = (bf16[2048,512]{1,0:T(8,128)(2,1)}, f32[512,768]{1,0:T(8,128)}) custom-call(bf16[256,1536]{1,0:T(8,128)(2,1)S(1)} %fusion.20.refs_0_, bf16[256,1536]{1,0:T(8,128)(2,1)} %collective-permute-done.refs_1_, bf16[256,1536]{1,0:T(8,128)(2,1)S(1)} %collective-permute-done.1.refs_2_, bf16[256,1536]{1,0:T(8,128)(2,1)S(1)} %collective-permute-done.2.refs_3_, ...), custom_call_target="tpu_custom_call" | custom-call | tf_op jit(solution)/shard_map/pallas_call | solution.py:98
  118.8 4.7 %shard_map.204 = (f32[8,8,8,256]{3,2,1,0:T(8,128)S(1)}, f32[8,128,128]{2,1,0:T(8,128)S(1)}, bf16[4,64,1536]{2,1,0:T(8,128)(2,1)S(1)}, bf16[4,64,1536]{2,1,0:T(8,128)(2,1)S(1)}) custom-call(s32[1]{0:T(128)} %bitcast.me_ref, s32[8]{0:T(128)S(1)} %copy-done.58, bf16[8,8,32,512]{3,2,1,0:T(8,128)(2,1)} %bitcast.266, f32[8,8,8,768]{3,2,1,0:T(8,128)S(1)} %bitcast.249, ...), custom_call_target="tpu_custom_call" | custom-call | tf_op jit(solution)/shard_map/pallas_call | solution.py:98
  129.1 3.2 collective-permute-done.32.refs_12_.refs_4_
  138.0 4.3 collective-permute-done.20
  144.0 2.9 collective-permute-done.18
  152.1 4.1 collective-permute-done.24.refs_4_
  159.7 4.1 collective-permute-done.22.refs_2_
  167.2 2.3 collective-permute-done.27
  171.1 11.8 %all-gather.6.cloned.1.call-done = bf16[1536,1536]{1,0:T(8,128)(2,1)} async-done(((bf16[384,1536]{1,0:T(8,128)(2,1)}), bf16[1536,1536]{1,0:T(8,128)(2,1)}) %all-gather.6.cloned.1.call-update) | async-done | bytes 4718608 | tf_op jit(solution)/shard_map/all_gather | solution.py:351
  182.9 4.9 %fusion.79 = (bf16[1536,768]{1,0:T(8,128)(2,1)}, bf16[1536,768]{1,0:T(8,128)(2,1)}) fusion(bf16[1536,1536]{1,0:T(8,128)(2,1)} %all-gather.6.cloned.1.call-done), kind=kLoop, calls=%fused_computation.218 | loop fusion | bytes 9437184 | tf_op jit(solution)/shard_map/slice | solution.py:406
  194.8 16.7 %shard_map.205 = (bf16[512,768]{1,0:T(8,128)(2,1)S(1)}, bf16[512,768]{1,0:T(8,128)(2,1)S(1)}, bf16[4,64,1536]{2,1,0:T(8,128)(2,1)S(1)}, bf16[4,64,1536]{2,1,0:T(8,128)(2,1)}) custom-call(bf16[64,1536]{1,0:T(8,128)(2,1)S(1)} %fusion.76.refs_0_, bf16[64,1536]{1,0:T(8,128)(2,1)} %collective-permute-done.21.refs_1_, bf16[64,1536]{1,0:T(8,128)(2,1)S(1)} %copy-done.28, ...), custom_call_target="tpu_custom_call" | custom-call | tf_op jit(solution)/shard_map/pallas_call | solution.py:98
  212.3 5.8 %shard_map.206 = (bf16[4,64,1536]{2,1,0:T(8,128)(2,1)S(1)}, bf16[4,64,1536]{2,1,0:T(8,128)(2,1)S(1)}) custom-call(bf16[512,768]{1,0:T(8,128)(2,1)S(1)} %get-tuple-element.33.hidden_ref.refs_8_, bf16[1536,768]{1,0:T(8,128)(2,1)S(1)} %copy-done), custom_call_target="tpu_custom_call" | custom-call | tf_op jit(solution)/shard_map/pallas_call | solution.py:98
  223.9 2.7 collective-permute-done.43
  235.0 2.2 collective-permute-done.41
  243.4 2.7 collective-permute-done.50.refs_4_
  256.3 5.1 %all_to_all.35 = bf16[2,2,48,1536]{3,2,1,0:T(8,128)(2,1)} all-to-all(bf16[2,2,48,1536]{3,2,1,0:T(8,128)(2,1)S(1)} %bitcast.283), channel_id=1, replica_groups={{0,1},{2,3},{4,5},{6,7},{8,9},{10,11},{12,13},{14,15},{16,17},{18,19},{..., dimensions={0} | all-to-all | bytes 1179648 | tf_op jit(solution)/shard_map/all_to_all | solution.py:474
  264.5 4.0 shard_map.211
  269.5 4.1 shard_map.212
  284.5 8.2 %shard_map.207 = (bf16[8,8,32,512]{3,2,1,0:T(8,128)(2,1)}, bf16[512,768]{1,0:T(8,128)(2,1)S(1)}) custom-call(s32[1]{0:T(128)} %bitcast.me_ref, s32[8]{0:T(128)S(1)} %copy-done.58, bf16[8,8,32,512]{3,2,1,0:T(8,128)(2,1)} %bitcast.267, f32[8,8,8,768]{3,2,1,0:T(8,128)S(1)} %bitcast.250, bf16[256,1536]{1,0:T(8,128)(2,1)S(1)} %pad.25.wo_ref, ...), custom_call_target="tpu_custom_call" | custom-call | tf_op jit(solution)/shard_map/pallas_call | solution.py:416
  292.7 1.9 copy-done.2
  294.5 11.9 %shard_map.208 = (bf16[4,256,1536]{2,1,0:T(8,128)(2,1)}, bf16[4,256,1536]{2,1,0:T(8,128)(2,1)}, bf16[4,64,1536]{2,1,0:T(8,128)(2,1)S(1)}, bf16[4,64,1536]{2,1,0:T(8,128)(2,1)S(1)}) custom-call(bf16[2048,512]{1,0:T(8,128)(2,1)S(1)} %bitcast.248, bf16[512,768]{1,0:T(8,128)(2,1)S(1)} %get-tuple-element.41.dlat_ref.refs_8_, bf16[1536,512]{1,0:T(8,128)(2,1)S(1)} %copy-done.1, ...), custom_call_target="tpu_custom_call" | custom-call | tf_op jit(solution)/shard_map/pallas_call | solution.py:98
  308.5 5.0 %shard_map.210 = f32[1536,768]{1,0:T(8,128)} custom-call(bf16[64,1536]{1,0:T(8,128)(2,1)S(1)} %fusion.37.refs_8_.refs_0_, bf16[64,1536]{1,0:T(8,128)(2,1)} %collective-permute-done.8.refs_9_.refs_1_, bf16[64,1536]{1,0:T(8,128)(2,1)} %collective-permute-done.9.refs_10_.refs_2_, bf16[64,1536]{1,0:T(8,128)(2,1)} %collective-permute-done.10.refs_11_.refs_3_, ...), custom_call_target="tpu_custom_call" | custom-call | tf_op jit(solution)/shard_map/pallas_call | solution.py:98
  315.4 8.2 %shard_map.209 = f32[1536,512]{1,0:T(8,128)} custom-call(bf16[256,1536]{1,0:T(8,128)(2,1)S(1)} %fusion.20.refs_0_, bf16[256,1536]{1,0:T(8,128)(2,1)} %collective-permute-done.refs_1_, bf16[256,1536]{1,0:T(8,128)(2,1)S(1)} %copy-done.8, bf16[256,1536]{1,0:T(8,128)(2,1)S(1)} %copy-done.10, bf16[256,1536]{1,0:T(8,128)(2,1)S(1)} %copy-done.6, ...), custom_call_target="tpu_custom_call" | custom-call | tf_op jit(solution)/shard_map/pallas_call | solution.py:98
  323.6 4.0 fusion.13
  330.8 5.2 %concatenate.86 = bf16[1536,640]{1,0:T(8,128)(2,1)} concatenate(bf16[1536,192]{1,0:T(8,128)(2,1)S(1)} %get-tuple-element.57, bf16[1536,192]{1,0:T(8,128)(2,1)} %get-tuple-element.58, bf16[1536,192]{1,0:T(8,128)(2,1)S(1)} %slice.528, bf16[1536,1]{1,0:T(8,128)(2,1)} %broadcast_in_dim.44, bf16[1536,1]{1,0:T(8,128)(2,1)} %broadcast_in_dim.45, bf16[1536,62]{1,0:T(8,128)(2,1)} %broadcast_in_dim.43), dimensions={1} | concatenate | bytes 3932160 | tf_op jit(solution)/shard_map/concatenate | solution.py:455
  339.6 4.8 %collective-permute-done.58 = bf16[2,32,1536]{2,1,0:T(8,128)(2,1)S(1)} collective-permute-done((bf16[2,32,1536]{2,1,0:T(8,128)(2,1)S(1)}, bf16[2,32,1536]{2,1,0:T(8,128)(2,1)S(1)}, u32[]{:S(2)}, u32[]{:S(2)}) %collective-permute-start.58) | collective-permute-done | bytes 196640 | tf_op jit(solution)/shard_map/ppermute | solution.py:21
  346.9 2.4 collective-permute-done.59
  354.2 3.5 all-to-all-start.5
  357.8 3.8 convert_add_fusion
  361.6 2.6 copy-done.65
  364.3 15.1 %reduce-scatter.11.cloned.1.call-done = bf16[384,768]{1,0:T(8,128)(2,1)} async-done(((bf16[1536,768]{1,0:T(8,128)(2,1)}), bf16[384,768]{1,0:T(8,128)(2,1)}) %reduce-scatter.11.cloned.1.call-update) | async-done | bytes 589840 | tf_op jit(solution)/shard_map/reduce_scatter | solution.py:468
  379.4 3.7 all-to-all-start.6
  384.6 2.1 collective-permute-start.63
  388.3 5.7 %all-to-all-done.6 = bf16[8,48,768]{2,1,0:T(8,128)(2,1)S(1)} async-done(((bf16[8,48,768]{2,1,0:T(8,128)(2,1)}), bf16[8,48,768]{2,1,0:T(8,128)(2,1)S(1)}, u32[]{:S(2)}, u32[]{:S(2)}) %all-to-all-start.6) | async-done | bytes 589856 | tf_op jit(solution)/shard_map/all_to_all | solution.py:469
  397.1 25.5 %reduce-scatter.5.cloned.1.call-done = bf16[384,640]{1,0:T(8,128)(2,1)} async-done(((bf16[1536,640]{1,0:T(8,128)(2,1)}), bf16[384,640]{1,0:T(8,128)(2,1)}) %reduce-scatter.5.cloned.1.call-update) | async-done | bytes 491536 | tf_op jit(solution)/shard_map/reduce_scatter | solution.py:468
  422.6 3.6 all-to-all-start.3
  428.1 2.1 collective-permute-start.64
  433.6 9.5 %collective-permute-done.64 = bf16[128,1536]{1,0:T(8,128)(2,1)S(1)} collective-permute-done((bf16[128,1536]{1,0:T(8,128)(2,1)S(1)}, bf16[128,1536]{1,0:T(8,128)(2,1)S(1)}, u32[]{:S(2)}, u32[]{:S(2)}) %collective-permute-start.64) | collective-permute-done | bytes 393248 | tf_op jit(solution)/shard_map/ppermute | solution.py:21
  (516 shorter events, 157.4 us)
Async XLA Ops:
  10.6 65.7 %collective-permute-start.3 = (bf16[256,1536]{1,0:T(8,128)(2,1)S(1)}, bf16[256,1536]{1,0:T(8,128)(2,1)S(1)}, u32[]{:S(2)}, u32[]{:S(2)}) collective-permute-start(bf16[256,1536]{1,0:T(8,128)(2,1)S(1)} %fusion.20.refs_0_), channel_id=1, source_target_pairs={{0,4},{1,5},{2,6},{3,7},{4,0},{5,1},{6,2},{7,3},{8,12},{9,13},{10,... | collective-permute-start | bytes 2359304 | tf_op jit(solution)/shard_map/ppermute | solution.py:21
  13.6 67.8 %collective-permute-start.1 = (bf16[256,1536]{1,0:T(8,128)(2,1)S(1)}, bf16[256,1536]{1,0:T(8,128)(2,1)S(1)}, u32[]{:S(2)}, u32[]{:S(2)}) collective-permute-start(bf16[256,1536]{1,0:T(8,128)(2,1)S(1)} %fusion.20.refs_0_), channel_id=1, source_target_pairs={{0,2},{1,3},{2,0},{3,1},{4,6},{5,7},{6,4},{7,5},{8,10},{9,11},{10,... | collective-permute-start | bytes 2359304 | tf_op jit(solution)/shard_map/ppermute | solution.py:21
  19.1 21.5 %all-to-all-start = ((bf16[8,48,640]{2,1,0:T(8,128)(2,1)}), bf16[8,48,640]{2,1,0:T(8,128)(2,1)S(1)}, u32[]{:S(2)}, u32[]{:S(2)}) async-start(bf16[8,48,640]{2,1,0:T(8,128)(2,1)} %pad_maximum_fusion.3), calls=%async_computation | async-start | bytes 983040 | tf_op jit(solution)/shard_map/all_to_all | solution.py:350
  44.9 51.0 %all-gather.4.cloned.1.call-start = ((), (), s32[]{:S(2)}) async-start(), calls=%async_computation.11 | async-start | bytes 2457600 | tf_op jit(solution)/shard_map/all_gather | solution.py:351
  48.3 34.9 %all-to-all-start.2 = ((bf16[8,48,1536]{2,1,0:T(8,128)(2,1)}), bf16[8,48,1536]{2,1,0:T(8,128)(2,1)}, u32[]{:S(2)}, u32[]{:S(2)}) async-start(bf16[8,48,1536]{2,1,0:T(8,128)(2,1)} %pad_maximum_fusion.1), calls=%async_computation.2 | async-start | bytes 2359296 | tf_op jit(solution)/shard_map/all_to_all | solution.py:350
  52.6 130.3 %all-gather.6.cloned.1.call-start = ((), (), s32[]{:S(2)}) async-start(), calls=%async_computation.12 | async-start | bytes 5898240 | tf_op jit(solution)/shard_map/all_gather | solution.py:351
  52.8 19.8 %collective-permute-start.11 = (bf16[64,1536]{1,0:T(8,128)(2,1)S(1)}, bf16[64,1536]{1,0:T(8,128)(2,1)S(1)}, u32[]{:S(2)}, u32[]{:S(2)}) collective-permute-start(bf16[64,1536]{1,0:T(8,128)(2,1)S(1)} %fusion.37.refs_8_.refs_0_), channel_id=1, source_target_pairs={{0,4},{1,5},{2,6},{3,7},{4,0},{5,1},{6,2},{7,3},{8,12},{9,13},{10,... | collective-permute-start | bytes 589832 | tf_op jit(solution)/shard_map/ppermute | solution.py:21
  54.7 20.1 %collective-permute-start.9 = (bf16[64,1536]{1,0:T(8,128)(2,1)S(1)}, bf16[64,1536]{1,0:T(8,128)(2,1)}, u32[]{:S(2)}, u32[]{:S(2)}) collective-permute-start(bf16[64,1536]{1,0:T(8,128)(2,1)S(1)} %fusion.37.refs_8_.refs_0_), channel_id=1, source_target_pairs={{0,2},{1,3},{2,0},{3,1},{4,6},{5,7},{6,4},{7,5},{8,10},{9,11},{10,... | collective-permute-start | bytes 589832 | tf_op jit(solution)/shard_map/ppermute | solution.py:21
  74.7 25.4 %collective-permute-start.8 = (bf16[64,1536]{1,0:T(8,128)(2,1)S(1)}, bf16[64,1536]{1,0:T(8,128)(2,1)}, u32[]{:S(2)}, u32[]{:S(2)}) collective-permute-start(bf16[64,1536]{1,0:T(8,128)(2,1)S(1)} %fusion.37.refs_8_.refs_0_), channel_id=1, source_target_pairs={{0,1},{1,0},{2,3},{3,2},{4,5},{5,4},{6,7},{7,6},{8,9},{9,8},{10,11... | collective-permute-start | bytes 589832 | tf_op jit(solution)/shard_map/ppermute | solution.py:21
  74.8 30.2 %collective-permute-start = (bf16[256,1536]{1,0:T(8,128)(2,1)S(1)}, bf16[256,1536]{1,0:T(8,128)(2,1)}, u32[]{:S(2)}, u32[]{:S(2)}) collective-permute-start(bf16[256,1536]{1,0:T(8,128)(2,1)S(1)} %fusion.20.refs_0_), channel_id=1, source_target_pairs={{0,1},{1,0},{2,3},{3,2},{4,5},{5,4},{6,7},{7,6},{8,9},{9,8},{10,11... | collective-permute-start | bytes 2359304 | tf_op jit(solution)/shard_map/ppermute | solution.py:21
  78.2 10.7 %collective-permute-start.5 = (bf16[128,1536]{1,0:T(8,128)(2,1)}, bf16[128,1536]{1,0:T(8,128)(2,1)}, u32[]{:S(2)}, u32[]{:S(2)}) collective-permute-start(bf16[128,1536]{1,0:T(8,128)(2,1)} %slice.336), channel_id=1, source_target_pairs={{0,2},{1,3},{2,0},{3,1},{4,6},{5,7},{6,4},{7,5},{8,10},{9,11},{10,... | collective-permute-start | bytes 1179656 | tf_op jit(solution)/shard_map/ppermute | solution.py:21
  81.4 19.3 %collective-permute-start.12 = (bf16[64,1536]{1,0:T(8,128)(2,1)S(1)}, bf16[64,1536]{1,0:T(8,128)(2,1)}, u32[]{:S(2)}, u32[]{:S(2)}) collective-permute-start(bf16[64,1536]{1,0:T(8,128)(2,1)S(1)} %collective-permute-done.11.refs_12_.refs_4_), channel_id=1, source_target_pairs={{0,1},{1,0},{2,3},{3,2},{4,5},{5,4},{6,7},{7,6},{8,9},{9,8},{10,11... | collective-permute-start | bytes 589832 | tf_op jit(solution)/shard_map/ppermute | solution.py:21
  82.3 11.8 %collective-permute-start.6 = (bf16[128,1536]{1,0:T(8,128)(2,1)}, bf16[128,1536]{1,0:T(8,128)(2,1)}, u32[]{:S(2)}, u32[]{:S(2)}) collective-permute-start(bf16[128,1536]{1,0:T(8,128)(2,1)} %slice.337), channel_id=1, source_target_pairs={{0,4},{1,5},{2,6},{3,7},{4,0},{5,1},{6,2},{7,3},{8,12},{9,13},{10,... | collective-permute-start | bytes 1179656 | tf_op jit(solution)/shard_map/ppermute | solution.py:21
  83.3 269.3 %reduce-scatter.7.cloned.1.call-start = ((), (), s32[]{:S(2)}) async-start(), calls=%async_computation.14 | async-start | bytes 737280 | tf_op jit(solution)/shard_map/reduce_scatter | solution.py:481
  88.8 14.2 %collective-permute-start.10 = (bf16[64,1536]{1,0:T(8,128)(2,1)}, bf16[64,1536]{1,0:T(8,128)(2,1)}, u32[]{:S(2)}, u32[]{:S(2)}) collective-permute-start(bf16[64,1536]{1,0:T(8,128)(2,1)} %collective-permute-done.9.refs_10_.refs_2_), channel_id=1, source_target_pairs={{0,1},{1,0},{2,3},{3,2},{4,5},{5,4},{6,7},{7,6},{8,9},{9,8},{10,11... | collective-permute-start | bytes 589832 | tf_op jit(solution)/shard_map/ppermute | solution.py:21
  94.1 11.0 %collective-permute-start.4 = (bf16[256,1536]{1,0:T(8,128)(2,1)S(1)}, bf16[256,1536]{1,0:T(8,128)(2,1)}, u32[]{:S(2)}, u32[]{:S(2)}) collective-permute-start(bf16[256,1536]{1,0:T(8,128)(2,1)S(1)} %collective-permute-done.3.refs_4_), channel_id=1, source_target_pairs={{0,1},{1,0},{2,3},{3,2},{4,5},{5,4},{6,7},{7,6},{8,9},{9,8},{10,11... | collective-permute-start | bytes 2359304 | tf_op jit(solution)/shard_map/ppermute | solution.py:21
  124.6 7.7 %collective-permute-start.32 = (bf16[64,1536]{1,0:T(8,128)(2,1)S(1)}, bf16[64,1536]{1,0:T(8,128)(2,1)S(1)}, u32[]{:S(2)}, u32[]{:S(2)}) collective-permute-start(bf16[64,1536]{1,0:T(8,128)(2,1)S(1)} %bitcast.251), channel_id=1, source_target_pairs={{0,4},{1,5},{2,6},{3,7},{4,0},{5,1},{6,2},{7,3},{8,12},{9,13},{10,... | collective-permute-start | bytes 589832 | tf_op jit(solution)/shard_map/ppermute | solution.py:21
  124.9 8.1 %collective-permute-start.30 = (bf16[64,1536]{1,0:T(8,128)(2,1)S(1)}, bf16[64,1536]{1,0:T(8,128)(2,1)S(1)}, u32[]{:S(2)}, u32[]{:S(2)}) collective-permute-start(bf16[64,1536]{1,0:T(8,128)(2,1)S(1)} %bitcast.252), channel_id=1, source_target_pairs={{0,2},{1,3},{2,0},{3,1},{4,6},{5,7},{6,4},{7,5},{8,10},{9,11},{10,... | collective-permute-start | bytes 589832 | tf_op jit(solution)/shard_map/ppermute | solution.py:21
  126.9 9.9 %collective-permute-start.17 = (bf16[2,32,1536]{2,1,0:T(8,128)(2,1)S(1)}, bf16[2,32,1536]{2,1,0:T(8,128)(2,1)S(1)}, u32[]{:S(2)}, u32[]{:S(2)}) collective-permute-start(bf16[2,32,1536]{2,1,0:T(8,128)(2,1)S(1)} %slice_bitcast_fusion.29), channel_id=1, source_target_pairs={{0,2},{1,3},{2,0},{3,1},{4,6},{5,7},{6,4},{7,5},{8,10},{9,11},{10,... | collective-permute-start | bytes 589832 | tf_op jit(solution)/shard_map/ppermute | solution.py:21
  127.3 9.5 %collective-permute-start.19 = (bf16[2,32,1536]{2,1,0:T(8,128)(2,1)S(1)}, bf16[2,32,1536]{2,1,0:T(8,128)(2,1)S(1)}, u32[]{:S(2)}, u32[]{:S(2)}) collective-permute-start(bf16[2,32,1536]{2,1,0:T(8,128)(2,1)S(1)} %slice_bitcast_fusion.27), channel_id=1, source_target_pairs={{0,4},{1,5},{2,6},{3,7},{4,0},{5,1},{6,2},{7,3},{8,12},{9,13},{10,... | collective-permute-start | bytes 589832 | tf_op jit(solution)/shard_map/ppermute | solution.py:21
  129.1 41.0 %collective-permute-start.29 = (bf16[64,1536]{1,0:T(8,128)(2,1)S(1)}, bf16[64,1536]{1,0:T(8,128)(2,1)}, u32[]{:S(2)}, u32[]{:S(2)}) collective-permute-start(bf16[64,1536]{1,0:T(8,128)(2,1)S(1)} %bitcast.253), channel_id=1, source_target_pairs={{0,1},{1,0},{2,3},{3,2},{4,5},{5,4},{6,7},{7,6},{8,9},{9,8},{10,11... | collective-permute-start | bytes 589832 | tf_op jit(solution)/shard_map/ppermute | solution.py:21
  133.0 15.7 %collective-permute-start.34 = (bf16[32,1536]{1,0:T(8,128)(2,1)}, bf16[32,1536]{1,0:T(8,128)(2,1)}, u32[]{:S(2)}, u32[]{:S(2)}) collective-permute-start(bf16[32,1536]{1,0:T(8,128)(2,1)} %slice.355), channel_id=1, source_target_pairs={{0,2},{1,3},{2,0},{3,1},{4,6},{5,7},{6,4},{7,5},{8,10},{9,11},{10,... | collective-permute-start | bytes 294920 | tf_op jit(solution)/shard_map/ppermute | solution.py:21
  133.7 23.3 %collective-permute-start.35 = (bf16[32,1536]{1,0:T(8,128)(2,1)}, bf16[32,1536]{1,0:T(8,128)(2,1)}, u32[]{:S(2)}, u32[]{:S(2)}) collective-permute-start(bf16[32,1536]{1,0:T(8,128)(2,1)} %slice.356), channel_id=1, source_target_pairs={{0,4},{1,5},{2,6},{3,7},{4,0},{5,1},{6,2},{7,3},{8,12},{9,13},{10,... | collective-permute-start | bytes 294920 | tf_op jit(solution)/shard_map/ppermute | solution.py:21
  136.9 33.8 %collective-permute-start.33 = (bf16[64,1536]{1,0:T(8,128)(2,1)S(1)}, bf16[64,1536]{1,0:T(8,128)(2,1)}, u32[]{:S(2)}, u32[]{:S(2)}) collective-permute-start(bf16[64,1536]{1,0:T(8,128)(2,1)S(1)} %collective-permute-done.32.refs_12_.refs_4_), channel_id=1, source_target_pairs={{0,1},{1,0},{2,3},{3,2},{4,5},{5,4},{6,7},{7,6},{8,9},{9,8},{10,11... | collective-permute-start | bytes 589832 | tf_op jit(solution)/shard_map/ppermute | solution.py:21
  146.9 23.8 %collective-permute-start.31 = (bf16[64,1536]{1,0:T(8,128)(2,1)S(1)}, bf16[64,1536]{1,0:T(8,128)(2,1)}, u32[]{:S(2)}, u32[]{:S(2)}) collective-permute-start(bf16[64,1536]{1,0:T(8,128)(2,1)S(1)} %collective-permute-done.30.refs_10_.refs_2_), channel_id=1, source_target_pairs={{0,1},{1,0},{2,3},{3,2},{4,5},{5,4},{6,7},{7,6},{8,9},{9,8},{10,11... | collective-permute-start | bytes 589832 | tf_op jit(solution)/shard_map/ppermute | solution.py:21
  156.1 7.7 %collective-permute-start.22 = (bf16[64,1536]{1,0:T(8,128)(2,1)S(1)}, bf16[64,1536]{1,0:T(8,128)(2,1)S(1)}, u32[]{:S(2)}, u32[]{:S(2)}) collective-permute-start(bf16[64,1536]{1,0:T(8,128)(2,1)S(1)} %fusion.76.refs_0_), channel_id=1, source_target_pairs={{0,2},{1,3},{2,0},{3,1},{4,6},{5,7},{6,4},{7,5},{8,10},{9,11},{10,... | collective-permute-start | bytes 589832 | tf_op jit(solution)/shard_map/ppermute | solution.py:21
  157.0 7.8 %collective-permute-start.26 = (bf16[32,1536]{1,0:T(8,128)(2,1)S(1)}, bf16[32,1536]{1,0:T(8,128)(2,1)S(1)}, u32[]{:S(2)}, u32[]{:S(2)}) collective-permute-start(bf16[32,1536]{1,0:T(8,128)(2,1)S(1)} %slice.353), channel_id=1, source_target_pairs={{0,2},{1,3},{2,0},{3,1},{4,6},{5,7},{6,4},{7,5},{8,10},{9,11},{10,... | collective-permute-start | bytes 294920 | tf_op jit(solution)/shard_map/ppermute | solution.py:21
  163.8 24.0 %collective-permute-start.36 = (bf16[64,1536]{1,0:T(8,128)(2,1)}, bf16[64,1536]{1,0:T(8,128)(2,1)}, u32[]{:S(2)}, u32[]{:S(2)}) collective-permute-start(bf16[64,1536]{1,0:T(8,128)(2,1)} %constant_dynamic-update-slice_fusion.6.refs_14_.refs_6_), channel_id=1, source_target_pairs={{0,1},{1,0},{2,3},{3,2},{4,5},{5,4},{6,7},{7,6},{8,9},{9,8},{10,11... | collective-permute-start | bytes 589832 | tf_op jit(solution)/shard_map/ppermute | solution.py:21
  169.5 18.3 %collective-permute-start.21 = (bf16[64,1536]{1,0:T(8,128)(2,1)S(1)}, bf16[64,1536]{1,0:T(8,128)(2,1)}, u32[]{:S(2)}, u32[]{:S(2)}) collective-permute-start(bf16[64,1536]{1,0:T(8,128)(2,1)S(1)} %fusion.76.refs_0_), channel_id=1, source_target_pairs={{0,1},{1,0},{2,3},{3,2},{4,5},{5,4},{6,7},{7,6},{8,9},{9,8},{10,11... | collective-permute-start | bytes 589832 | tf_op jit(solution)/shard_map/ppermute | solution.py:21
  170.1 17.7 %collective-permute-start.25 = (bf16[64,1536]{1,0:T(8,128)(2,1)S(1)}, bf16[64,1536]{1,0:T(8,128)(2,1)}, u32[]{:S(2)}, u32[]{:S(2)}) collective-permute-start(bf16[64,1536]{1,0:T(8,128)(2,1)S(1)} %collective-permute-done.24.refs_4_), channel_id=1, source_target_pairs={{0,1},{1,0},{2,3},{3,2},{4,5},{5,4},{6,7},{7,6},{8,9},{9,8},{10,11... | collective-permute-start | bytes 589832 | tf_op jit(solution)/shard_map/ppermute | solution.py:21
  170.6 17.2 %collective-permute-start.23 = (bf16[64,1536]{1,0:T(8,128)(2,1)S(1)}, bf16[64,1536]{1,0:T(8,128)(2,1)S(1)}, u32[]{:S(2)}, u32[]{:S(2)}) collective-permute-start(bf16[64,1536]{1,0:T(8,128)(2,1)S(1)} %collective-permute-done.22.refs_2_), channel_id=1, source_target_pairs={{0,1},{1,0},{2,3},{3,2},{4,5},{5,4},{6,7},{7,6},{8,9},{9,8},{10,11... | collective-permute-start | bytes 589832 | tf_op jit(solution)/shard_map/ppermute | solution.py:21
  170.7 17.8 %collective-permute-start.28 = (bf16[64,1536]{1,0:T(8,128)(2,1)}, bf16[64,1536]{1,0:T(8,128)(2,1)S(1)}, u32[]{:S(2)}, u32[]{:S(2)}) collective-permute-start(bf16[64,1536]{1,0:T(8,128)(2,1)} %constant_dynamic-update-slice_fusion.4.refs_6_), channel_id=1, source_target_pairs={{0,1},{1,0},{2,3},{3,2},{4,5},{5,4},{6,7},{7,6},{8,9},{9,8},{10,11... | collective-permute-start | bytes 589832 | tf_op jit(solution)/shard_map/ppermute | solution.py:21
  220.6 7.9 %collective-permute-start.45 = (bf16[2,32,1536]{2,1,0:T(8,128)(2,1)S(1)}, bf16[2,32,1536]{2,1,0:T(8,128)(2,1)S(1)}, u32[]{:S(2)}, u32[]{:S(2)}) collective-permute-start(bf16[2,32,1536]{2,1,0:T(8,128)(2,1)S(1)} %slice_bitcast_fusion.19), channel_id=1, source_target_pairs={{0,4},{1,5},{2,6},{3,7},{4,0},{5,1},{6,2},{7,3},{8,12},{9,13},{10,... | collective-permute-start | bytes 589832 | tf_op jit(solution)/shard_map/ppermute | solution.py:21
  222.4 10.0 %collective-permute-start.40 = (bf16[2,32,1536]{2,1,0:T(8,128)(2,1)S(1)}, bf16[2,32,1536]{2,1,0:T(8,128)(2,1)S(1)}, u32[]{:S(2)}, u32[]{:S(2)}) collective-permute-start(bf16[2,32,1536]{2,1,0:T(8,128)(2,1)S(1)} %slice_bitcast_fusion.23), channel_id=1, source_target_pairs={{0,4},{1,5},{2,6},{3,7},{4,0},{5,1},{6,2},{7,3},{8,12},{9,13},{10,... | collective-permute-start | bytes 589832 | tf_op jit(solution)/shard_map/ppermute | solution.py:21
  223.1 10.1 %collective-permute-start.38 = (bf16[2,32,1536]{2,1,0:T(8,128)(2,1)S(1)}, bf16[2,32,1536]{2,1,0:T(8,128)(2,1)S(1)}, u32[]{:S(2)}, u32[]{:S(2)}) collective-permute-start(bf16[2,32,1536]{2,1,0:T(8,128)(2,1)S(1)} %slice_bitcast_fusion.25), channel_id=1, source_target_pairs={{0,2},{1,3},{2,0},{3,1},{4,6},{5,7},{6,4},{7,5},{8,10},{9,11},{10,... | collective-permute-start | bytes 589832 | tf_op jit(solution)/shard_map/ppermute | solution.py:21
  261.4 92.8 %reduce-scatter.9.cloned.1.call-start = ((), (), s32[]{:S(2)}) async-start(), calls=%async_computation.15 | async-start | bytes 2949120 | tf_op jit(solution)/shard_map/reduce_scatter | solution.py:468
  268.5 111.0 %reduce-scatter.11.cloned.1.call-start = ((), (), s32[]{:S(2)}) async-start(), calls=%async_computation.16 | async-start | bytes 2949120 | tf_op jit(solution)/shard_map/reduce_scatter | solution.py:468
  273.6 149.0 %reduce-scatter.5.cloned.1.call-start = ((), (), s32[]{:S(2)}) async-start(), calls=%async_computation.13 | async-start | bytes 2457600 | tf_op jit(solution)/shard_map/reduce_scatter | solution.py:468
  306.5 29.5 %collective-permute-start.55 = (bf16[4,64,1536]{2,1,0:T(8,128)(2,1)S(1)}, bf16[4,64,1536]{2,1,0:T(8,128)(2,1)}, u32[]{:S(2)}, u32[]{:S(2)}) collective-permute-start(bf16[4,64,1536]{2,1,0:T(8,128)(2,1)S(1)} %get-tuple-element.43), channel_id=1, source_target_pairs={{0,1},{1,0},{2,3},{3,2},{4,5},{5,4},{6,7},{7,6},{8,9},{9,8},{10,11... | collective-permute-start | bytes 2359304 | tf_op jit(solution)/shard_map/ppermute | solution.py:21
  329.7 28.1 %collective-permute-start.60 = (bf16[4,256,1536]{2,1,0:T(8,128)(2,1)}, bf16[4,256,1536]{2,1,0:T(8,128)(2,1)}, u32[]{:S(2)}, u32[]{:S(2)}) collective-permute-start(bf16[4,256,1536]{2,1,0:T(8,128)(2,1)} %get-tuple-element.45), channel_id=1, source_target_pairs={{0,1},{1,0},{2,3},{3,2},{4,5},{5,4},{6,7},{7,6},{8,9},{9,8},{10,11... | collective-permute-start | bytes 9437192 | tf_op jit(solution)/shard_map/ppermute | solution.py:21
  338.1 8.1 %collective-permute-start.56 = (bf16[2,32,1536]{2,1,0:T(8,128)(2,1)S(1)}, bf16[2,32,1536]{2,1,0:T(8,128)(2,1)S(1)}, u32[]{:S(2)}, u32[]{:S(2)}) collective-permute-start(bf16[2,32,1536]{2,1,0:T(8,128)(2,1)S(1)} %slice_bitcast_fusion.17), channel_id=1, source_target_pairs={{0,2},{1,3},{2,0},{3,1},{4,6},{5,7},{6,4},{7,5},{8,10},{9,11},{10,... | collective-permute-start | bytes 589832 | tf_op jit(solution)/shard_map/ppermute | solution.py:21
  354.2 25.2 %all-to-all-start.5 = ((bf16[8,48,768]{2,1,0:T(8,128)(2,1)}), bf16[8,48,768]{2,1,0:T(8,128)(2,1)S(1)}, u32[]{:S(2)}, u32[]{:S(2)}) async-start(bf16[8,48,768]{2,1,0:T(8,128)(2,1)} %bitcast.295), calls=%async_computation.8 | async-start | bytes 1179648 | tf_op jit(solution)/shard_map/all_to_all | solution.py:469
  379.4 14.6 %all-to-all-start.6 = ((bf16[8,48,768]{2,1,0:T(8,128)(2,1)}), bf16[8,48,768]{2,1,0:T(8,128)(2,1)S(1)}, u32[]{:S(2)}, u32[]{:S(2)}) async-start(bf16[8,48,768]{2,1,0:T(8,128)(2,1)} %bitcast.294), calls=%async_computation.10 | async-start | bytes 1179648 | tf_op jit(solution)/shard_map/all_to_all | solution.py:469
  384.6 41.6 %collective-permute-start.63 = (bf16[2,128,1536]{2,1,0:T(8,128)(2,1)S(1)}, bf16[2,128,1536]{2,1,0:T(8,128)(2,1)}, u32[]{:S(2)}, u32[]{:S(2)}) collective-permute-start(bf16[2,128,1536]{2,1,0:T(8,128)(2,1)S(1)} %slice_bitcast_fusion.3), channel_id=1, source_target_pairs={{0,4},{1,5},{2,6},{3,7},{4,0},{5,1},{6,2},{7,3},{8,12},{9,13},{10,... | collective-permute-start | bytes 2359304 | tf_op jit(solution)/shard_map/ppermute | solution.py:21
  386.7 43.5 %collective-permute-start.61 = (bf16[2,128,1536]{2,1,0:T(8,128)(2,1)S(1)}, bf16[2,128,1536]{2,1,0:T(8,128)(2,1)}, u32[]{:S(2)}, u32[]{:S(2)}) collective-permute-start(bf16[2,128,1536]{2,1,0:T(8,128)(2,1)S(1)} %slice_bitcast_fusion.5), channel_id=1, source_target_pairs={{0,2},{1,3},{2,0},{3,1},{4,6},{5,7},{6,4},{7,5},{8,10},{9,11},{10,... | collective-permute-start | bytes 2359304 | tf_op jit(solution)/shard_map/ppermute | solution.py:21
  422.6 24.7 %all-to-all-start.3 = ((bf16[8,48,640]{2,1,0:T(8,128)(2,1)}), bf16[8,48,640]{2,1,0:T(8,128)(2,1)S(1)}, u32[]{:S(2)}, u32[]{:S(2)}) async-start(bf16[8,48,640]{2,1,0:T(8,128)(2,1)} %bitcast.297), calls=%async_computation.4 | async-start | bytes 983040 | tf_op jit(solution)/shard_map/all_to_all | solution.py:469
  428.1 15.1 %collective-permute-start.64 = (bf16[128,1536]{1,0:T(8,128)(2,1)S(1)}, bf16[128,1536]{1,0:T(8,128)(2,1)S(1)}, u32[]{:S(2)}, u32[]{:S(2)}) collective-permute-start(bf16[128,1536]{1,0:T(8,128)(2,1)S(1)} %fusion.41), channel_id=1, source_target_pairs={{0,2},{1,3},{2,0},{3,1},{4,6},{5,7},{6,4},{7,5},{8,10},{9,11},{10,... | collective-permute-start | bytes 1179656 | tf_op jit(solution)/shard_map/ppermute | solution.py:21
  432.1 11.9 %collective-permute-start.62 = (bf16[128,1536]{1,0:T(8,128)(2,1)S(1)}, bf16[128,1536]{1,0:T(8,128)(2,1)S(1)}, u32[]{:S(2)}, u32[]{:S(2)}) collective-permute-start(bf16[128,1536]{1,0:T(8,128)(2,1)S(1)} %fusion.40), channel_id=1, source_target_pairs={{0,4},{1,5},{2,6},{3,7},{4,0},{5,1},{6,2},{7,3},{8,12},{9,13},{10,... | collective-permute-start | bytes 1179656 | tf_op jit(solution)/shard_map/ppermute | solution.py:21
  (138 other events, 1009.1 us)
Sparse Core Ops, SparseCore 0:
  47.9 45.1 all-gather.3
  94.6 88.2 all-gather.5
  261.5 19.5 reduce-scatter.6
  283.3 46.4 reduce-scatter.8
  331.9 47.5 reduce-scatter.10
  381.6 40.9 reduce-scatter.4

commit v2 on v1

v2 whole, which is shorter than its diff:
```python
from functools import partial
import math

import jax
import jax.numpy as jnp
from jax import lax
from jax.experimental import pallas as pl
from jax.experimental.pallas import tpu as pltpu
from jax.sharding import PartitionSpec as P

HEADS = 16
NORM_EPS = 1e-05
MASKED = -1e30
GAUSS_DENSITY = 0.3989422804014327
BF = jnp.bfloat16
F32 = jnp.float32
MIB = 1 << 20
NT = ((1,), (1,))
TN = ((0,), (0,))


def swap(array, bit, axis="blk"):
    return lax.ppermute(array, axis, [(i, i ^ bit) for i in range(lax.axis_size(axis))])


def gather_first(block):
    slots = {0: block}
    for offset in range(2, lax.axis_size("blk"), 2):
        if offset & (offset - 1) == 0:
            slots[offset] = swap(block, offset)
    return slots


def gather_rest(slots, *before):
    count = lax.axis_size("blk")
    half = slots[0].shape[0] // 2
    slots = dict(slots)
    if before:
        slots[2] = after(slots[2], *before)
    for offset in range(2, count, 2):
        low = offset & -offset
        high = 1 << (offset.bit_length() - 1)
        if low != high:
            slots[offset] = jnp.concatenate(
                [swap(slots[offset ^ low][:half], low), swap(slots[offset ^ high][half:], high)], 0
            )
    for offset in range(0, count, 2):
        slots[offset + 1] = swap(slots[offset], 1)
    return [slots[k] for k in range(count)]


def gather_slots(block):
    return gather_rest(gather_first(block))


def fold_kernel(terms, lowest, *refs):
    ins, outs = refs[: 2 * terms], refs[2 * terms : 2 * terms + 4]
    held, made, sems, out_sems = (
        refs[2 * terms + 4 : 4 * terms + 4],
        refs[4 * terms + 4 : 4 * terms + 8],
        refs[-2],
        refs[-1],
    )
    slots = ins[0].shape[0]
    pairs = [(ins[t].at[m], held[t].at[m]) for m in range(slots) for t in range(2 * terms)]
    copies = begin(pairs, sems)
    rows = outs[0].shape[1]
    written = []
    for m in range(slots):
        for t in range(2 * terms):
            copies[2 * terms * m + t].wait()
        for i in range(2):
            if terms == 1:
                left, right, here = held[0], held[1], slice(i * rows, (i + 1) * rows)
            else:
                left, right, here = held[2 * i], held[2 * i + 1], slice(0, rows)
            total = left[m, here, :].astype(F32) + right[m, here, :].astype(F32)
            half = slots // 2
            side, place = (m % 2, m // 2) if lowest[i] else (m // half, m % half)
            made[2 * i + side][place] = total.astype(outs[2 * i + side].dtype)
            copy = pltpu.make_async_copy(
                made[2 * i + side].at[place], outs[2 * i + side].at[place], out_sems.at[len(written)]
            )
            copy.start()
            written.append(copy)
    for copy in written:
        copy.wait()


def fold(*terms):
    flat = [t for pair in terms for t in pair]
    slots, rows, width = flat[0].shape
    if len(terms) == 1:
        rows //= 2
    half = (slots // 2, rows, width)
    scratch = [pltpu.VMEM(t.shape, t.dtype) for t in flat]
    scratch += [pltpu.VMEM(half, kind) for kind in (F32, BF, F32, BF)]
    scratch += [
        pltpu.SemaphoreType.DMA((slots * len(flat),)),
        pltpu.SemaphoreType.DMA((2 * slots,)),
    ]
    return call(
        partial(fold_kernel, len(terms), (True, False)),
        [(half, kind, "h") for kind in (F32, BF, F32, BF)],
        "h" * len(flat),
        scratch,
    )(*flat)


def scatter_sum(even, odd, hooks=()):
    hooks = list(hooks)
    got = swap(odd, 1)
    if hooks:
        got = after(got, *hooks.pop(0)(odd))
    keep_a, send_a, keep_b, send_b = fold((even, got))
    low, high = 2, lax.axis_size("blk") // 2
    while True:
        got_a, got_b = swap(send_a, low), swap(send_b, high)
        if hooks:
            got_a = after(got_a, *hooks.pop(0)(send_a))
        if low * 2 >= lax.axis_size("blk"):
            return keep_a[0], got_a[0], keep_b[0], got_b[0]
        keep_a, send_a, keep_b, send_b = fold((keep_a, got_a), (keep_b, got_b))
        low, high = low * 2, high // 2


def after(array, *others):
    return lax.optimization_barrier((array, *others))[0]


def dot(left, right, dims=((1,), (0,))):
    return lax.dot_general(left, right, (dims, ((), ())), preferred_element_type=F32)


def call(kernel, outs, spaces, scratch=(), vmem=56, cost=2):
    kinds = {"s": pltpu.SMEM, "v": pltpu.VMEM, "h": pl.ANY, "d": pl.ANY}
    fetched = [i for i, letter in enumerate(spaces) if letter == "d"]
    count = len(spaces) + len(outs) + len(scratch)

    def fetching(*refs):
        refs, held = list(refs[:count]), refs[count:]
        copies = begin([(refs[i], held[j]) for j, i in enumerate(fetched)], held[-1])
        for j, i in enumerate(fetched):
            copies[j].wait()
            refs[i] = held[j]
        kernel(*refs)

    def run(*operands):
        held = [pltpu.VMEM(operands[i].shape, operands[i].dtype) for i in fetched]
        if fetched:
            held.append(pltpu.SemaphoreType.DMA((len(fetched),)))
        return pl.pallas_call(
            fetching if fetched else kernel,
            out_shape=[jax.ShapeDtypeStruct(shape, kind) for shape, kind, _ in outs],
            in_specs=[pl.BlockSpec(memory_space=kinds[s]) for s in spaces],
            out_specs=[pl.BlockSpec(memory_space=kinds[s]) for _, _, s in outs],
            scratch_shapes=[*scratch, *held],
            compiler_params=pltpu.CompilerParams(vmem_limit_bytes=vmem * MIB),
            cost_estimate=pl.CostEstimate(
                flops=int(cost * 1.15e9), bytes_accessed=int(cost * 3.6e6), transcendentals=0
            ),
        )(*operands)

    return run


def begin(pairs, sems):
    copies = [pltpu.make_async_copy(s, d, sems.at[i]) for i, (s, d) in enumerate(pairs)]
    for copy in copies:
        copy.start()
    return copies


def normalize(values):
    center = values - jnp.mean(values, -1, keepdims=True)
    inverse = lax.rsqrt(jnp.mean(center * center, -1, keepdims=True) + NORM_EPS)
    return (center * inverse, inverse)


def norm_back(grad_norm, normed, inverse):
    return inverse * (
        grad_norm
        - jnp.mean(grad_norm, -1, keepdims=True)
        - normed * jnp.mean(grad_norm * normed, -1, keepdims=True)
    )


def owned_heads(count, ring, per_ring, b):
    groups = count // ring
    return [((b % ring) * per_ring + j) * groups + b // ring for j in range(per_ring)]


def split_attn_kernel(lay, ring, per_ring, kv, query, gains, out):
    count, own, _ = out.shape
    width = query.shape[1]
    size = lay.size
    scaled = (query[...].astype(F32) * gains[:, 1:2]).astype(BF)
    both = kv[...]
    lane = lax.broadcasted_iota(jnp.int32, (own, lay.width - lay.gain_at), 1)
    tail = jnp.where(lane == 0, gains[:, 0:1], jnp.where(lane == 1, gains[:, 1:2], 0.0))
    tail = tail.astype(BF)
    for b in range(count):
        heads = owned_heads(count, ring, per_ring, b)
        pieces = []
        for source, base in ((both, 0), (both, width), (scaled, 0)):
            pieces += [source[:, base + h * size : base + (h + 1) * size] for h in heads]
            if lay.step > lay.span:
                pieces.append(jnp.zeros((own, lay.step - lay.span), BF))
        out[b] = jnp.concatenate(pieces + [tail], 1)


def split_ffn_kernel(count, w_in, w_down, gains, out):
    part = out.shape[2] // 2
    planes = out.shape[0] // count
    for b in range(count):
        for p in range(2):
            cols = slice((2 * b + p) * part, (2 * b + p + 1) * part)
            scaled = (w_in[:, cols].astype(F32) * gains[:, 2:3]).astype(BF)
            down = w_down[:, cols]
            for d in range(p, planes, 2):
                out[d * count + b, :, :part] = scaled
                out[d * count + b, :, part:] = down


def finish_ffn_kernel(count, of_in, of_down, w_in, gains, in_grad, down_grad, gain_grad):
    planes = of_in.shape[0] // count
    part = of_in.shape[2]
    gain = gains[:, 2:3]
    total = jnp.zeros((w_in.shape[0], 1), F32)
    for b in range(count):
        for p in range(2):
            cols = slice((2 * b + p) * part, (2 * b + p + 1) * part)
            raw = of_in[p * count + b].astype(F32)
            down = of_down[p * count + b].astype(F32)
            for d in range(p + 2, planes, 2):
                raw = raw + of_in[d * count + b].astype(F32)
                down = down + of_down[d * count + b].astype(F32)
            total = total + jnp.sum(raw * w_in[:, cols].astype(F32), 1, keepdims=True)
            in_grad[:, cols] = raw * gain
            down_grad[:, cols] = down
    gain_grad[...] = jnp.broadcast_to(total, gain_grad.shape)


def finish_attn_kernel(lay, ring, per_ring, slots, query, gains, q_grad, kv_grad, gain_grad):
    count, own, _ = slots.shape
    width = query.shape[1]
    size = lay.size
    place = {}
    tail = jnp.zeros((own, lay.width - lay.gain_at), F32)
    for b in range(count):
        block = slots[b].astype(F32)
        for j, h in enumerate(owned_heads(count, ring, per_ring, b)):
            for i, at in enumerate((0, lay.step, lay.q_at)):
                place[i, h] = block[:, at + j * size : at + (j + 1) * size]
        tail = tail + block[:, lay.gain_at :]
    heads = width // size
    kv_grad[:, :width] = jnp.concatenate([place[0, h] for h in range(heads)], 1)
    kv_grad[:, width:] = jnp.concatenate([place[1, h] for h in range(heads)], 1)
    raw = jnp.concatenate([place[2, h] for h in range(heads)], 1)
    q_grad[...] = raw * gains[:, 1:2]
    of_query = jnp.sum(raw * query[...].astype(F32), 1, keepdims=True)
    lane = lax.broadcasted_iota(jnp.int32, gain_grad.shape, 1)
    gain_grad[...] = jnp.where(lane == 0, tail[:, 0:1], tail[:, 1:2] + of_query)


def prepare_kernel(media, lats, out):
    rows = media.shape[0]
    out[:rows, :] = normalize(media[...].astype(F32))[0].astype(BF)
    out[rows:, :] = normalize(lats[...].astype(F32))[0].astype(BF)


class Layout:
    def __init__(self, span, size):
        self.span, self.size = span, size
        pad = -(-span // 128) * 128
        if (2 * span) % 128 == 0:
            self.step, self.v_at = span, span // 128 * 128
        else:
            self.step, self.v_at = pad, pad
        self.block = pad
        self.v_off = self.step - self.v_at
        self.q_at = 2 * self.step
        self.gain_at = self.q_at + span if self.step == span else 3 * pad
        self.width = -(-(self.gain_at + 2) // 128) * 128
        self.heads = span // size

    def keys(self, values):
        return values[..., : self.block]

    def values(self, values):
        return values[..., self.v_at : self.v_at + self.block]

    def queries(self, values):
        return values[..., self.q_at : self.q_at + self.block]

    def pack(self, keys, values):
        shared = self.block - self.v_at
        if not shared:
            return jnp.concatenate([keys, values], 1)
        return jnp.concatenate(
            [keys[:, : self.v_at], keys[:, self.v_at :] + values[:, :shared], values[:, shared:]], 1
        )

    def masks(self, rows, offset):
        lane = lax.broadcasted_iota(jnp.int32, (rows, self.block), 1) - offset
        return [
            (lane >= h * self.size) & (lane < (h + 1) * self.size) for h in range(self.heads)
        ]


def stacked(values, masks):
    return jnp.concatenate([jnp.where(m, values, jnp.zeros_like(values)) for m in masks], 0)


def unstacked(values, masks):
    rows = values.shape[0] // len(masks)
    total = jnp.zeros((rows, values.shape[1]), F32)
    for h, m in enumerate(masks):
        total = jnp.where(m, values[h * rows : (h + 1) * rows], total)
    return total


def media_allowed(me, length, count, media_rows, rows):
    column = lax.broadcasted_iota(jnp.int32, (rows, count * media_rows), 1)
    index = ((column // media_rows) ^ me) * media_rows + column % media_rows
    return index < length


def scale_weights(lay, w, wm, wl):
    row_media = w[:, lay.gain_at : lay.gain_at + 1].astype(F32)
    row_lat = w[:, lay.gain_at + 1 : lay.gain_at + 2].astype(F32)
    base = w[:, : lay.q_at].astype(F32)
    wm[...] = (base * row_media).astype(BF)
    wl[:, : lay.q_at] = (base * row_lat).astype(BF)
    wl[:, lay.q_at :] = w[:, lay.q_at :]


def put_slots(part, count, even, odd):
    rows = part.shape[0] // count
    for k in range(count):
        (odd if k % 2 else even)[k // 2] = part[k * rows : (k + 1) * rows]


def own_rows(lay, ring, me, wo_all, wo):
    at = pl.multiple_of((me % ring) * lay.span, lay.span)
    wo[...] = jnp.zeros(wo.shape, wo.dtype)
    wo[lay.v_off : lay.v_off + lay.span, :] = wo_all[pl.ds(at, lay.span), :]


def forward_kernel(count, lay, ring, me_ref, len_ref, *refs):
    slots = refs[:count]
    w_hbm, wo_hbm, kv_ref, lat_ref, att_ref, lse_ref = refs[count : count + 6]
    even, odd = refs[count + 6 : count + 8]
    xm, xl, w, wm, wl, wo_all, wo, sems = refs[count + 8 :]
    images, media_rows = kv_ref.shape[1:3]
    lat_rows = lat_ref.shape[2]
    rows = count * lat_rows
    block_m, block_l = images * media_rows, images * lat_rows
    pairs = [(w_hbm, w), (wo_hbm, wo_all)]
    for k in range(count):
        pairs.append((slots[k].at[pl.ds(0, block_m)], xm.at[pl.ds(k * block_m, block_m)]))
        pairs.append((slots[k].at[pl.ds(block_m, block_l)], xl.at[pl.ds(k * block_l, block_l)]))
    copies = begin(pairs, sems)
    copies[0].wait()
    scale_weights(lay, w, wm, wl)
    for k in range(count):
        copies[2 + 2 * k].wait()
        proj = dot(xm[k * block_m : (k + 1) * block_m, :], wm[...]).astype(BF)
        kv_ref[k] = proj.reshape(images, media_rows, lay.q_at)
    for k in range(count):
        copies[3 + 2 * k].wait()
    lat_ref[...] = dot(xl[...], wl[...]).reshape(lat_ref.shape)

    scale = 1.0 / math.sqrt(lay.size)
    q_masks, v_masks = lay.masks(rows, 0), lay.masks(rows, lay.v_off)
    me = me_ref[0]
    for i in range(images):
        kv = kv_ref[:, i].reshape(count * media_rows, lay.q_at)
        lat = lat_ref[:, i].reshape(rows, lay.width).astype(BF)
        queries = stacked(lay.queries(lat), q_masks)
        allowed = media_allowed(me, len_ref[i], count, media_rows, lay.heads * rows)
        scores = jnp.where(allowed, dot(queries, lay.keys(kv), NT) * scale, MASKED)
        lat_scores = dot(queries, lay.keys(lat), NT) * scale
        top = jnp.maximum(
            jnp.max(scores, -1, keepdims=True), jnp.max(lat_scores, -1, keepdims=True)
        )
        probs = jnp.where(allowed, jnp.exp(scores - top), 0.0)
        lat_probs = jnp.exp(lat_scores - top)
        denominator = jnp.sum(probs, -1, keepdims=True) + jnp.sum(lat_probs, -1, keepdims=True)
        weighted = dot(probs.astype(BF), lay.values(kv)) + dot(
            lat_probs.astype(BF), lay.values(lat)
        )
        attended = unstacked(weighted / denominator, v_masks)
        att_ref[:, i] = attended.reshape(count, lat_rows, lay.block)
        lse_ref[i] = jnp.broadcast_to(top + jnp.log(denominator), (lay.heads * rows, 128))
    copies[1].wait()
    own_rows(lay, ring, me, wo_all, wo)
    flat = att_ref[...].reshape(count * block_l, lay.block).astype(BF)
    put_slots(dot(flat, wo[...]).astype(BF), count, even, odd)


def backward_kernel(count, lay, ring, me_ref, len_ref, *refs):
    branch = refs[:count]
    kv_hbm, lat_hbm, wo_hbm, att_hbm, lse_hbm, dkv_ref, dlat_ref = refs[count : count + 7]
    br, kv_ref, lat_ref, wo_all, wo, att_ref, lse_ref, dwide, datt, sems = refs[count + 7 :]
    images, media_rows = kv_ref.shape[1:3]
    lat_rows = lat_ref.shape[2]
    rows = count * lat_rows
    block_m, block_l = images * media_rows, images * lat_rows
    pairs = [(branch[k], br.at[pl.ds(k * block_l, block_l)]) for k in range(count)]
    pairs += [
        (wo_hbm, wo_all),
        (lat_hbm, lat_ref),
        (att_hbm, att_ref),
        (lse_hbm, lse_ref),
        (kv_hbm, kv_ref),
    ]
    copies = begin(pairs, sems)
    for k in range(count + 1):
        copies[k].wait()
    own_rows(lay, ring, me_ref[0], wo_all, wo)
    datt[...] = dot(br[...], wo[...], NT).reshape(datt.shape)
    for copy in copies[count + 1 :]:
        copy.wait()

    scale = 1.0 / math.sqrt(lay.size)
    q_masks, v_masks = lay.masks(rows, 0), lay.masks(rows, lay.v_off)
    me = me_ref[0]
    for i in range(images):
        kv = kv_ref[:, i].reshape(count * media_rows, lay.q_at)
        lat = lat_ref[:, i].reshape(rows, lay.width).astype(BF)
        queries = stacked(lay.queries(lat), q_masks)
        grads = datt[:, i].reshape(rows, lay.block).astype(BF)
        attended = att_ref[:, i].reshape(rows, lay.block)
        grad_heads = stacked(grads, v_masks)
        delta = jnp.sum(stacked(grads.astype(F32) * attended, v_masks), -1, keepdims=True)
        total = lse_ref[i][:, :1]
        allowed = media_allowed(me, len_ref[i], count, media_rows, lay.heads * rows)
        scores = jnp.where(allowed, dot(queries, lay.keys(kv), NT) * scale, MASKED)
        lat_scores = dot(queries, lay.keys(lat), NT) * scale
        probs = jnp.where(allowed, jnp.exp(scores - total), 0.0)
        lat_probs = jnp.exp(lat_scores - total)
        score_grad = (probs * (dot(grad_heads, lay.values(kv), NT) - delta)).astype(BF)
        lat_score_grad = (lat_probs * (dot(grad_heads, lay.values(lat), NT) - delta)).astype(BF)
        query_grad = scale * unstacked(
            dot(score_grad, lay.keys(kv)) + dot(lat_score_grad, lay.keys(lat)), q_masks
        )
        dkv_ref[:, i] = (
            lay.pack(scale * dot(score_grad, queries, TN), dot(probs.astype(BF), grad_heads, TN))
            .astype(BF)
            .reshape(count, media_rows, lay.q_at)
        )
        dlat = jnp.concatenate(
            [
                lay.pack(
                    scale * dot(lat_score_grad, queries, TN),
                    dot(lat_probs.astype(BF), grad_heads, TN),
                ),
                query_grad,
            ],
            1,
        )
        dwide[:, i] = jnp.pad(dlat, ((0, 0), (0, lay.width - dlat.shape[1]))).reshape(
            count, lat_rows, lay.width
        )
    dlat_ref[...] = dwide[...].reshape(count * block_l, lay.width).astype(BF)


def input_grad_kernel(count, lay, dkv_ref, dlat_ref, w, even, odd, wm, wl):
    block_l = dlat_ref.shape[0] // count
    block_m = even.shape[1] - block_l
    scale_weights(lay, w, wm, wl)
    lat_back = dot(dlat_ref[...], wl[...], NT).astype(BF)
    for k in range(count):
        out = odd if k % 2 else even
        back = dot(dkv_ref[k].reshape(block_m, lay.q_at), wm[...], NT).astype(BF)
        out[k // 2, :block_m] = back
        out[k // 2, block_m:] = lat_back[k * block_l : (k + 1) * block_l]


def attn_weight_grad_kernel(count, lay, ring, me_ref, *refs):
    slots, branch = refs[:count], refs[count : 2 * count]
    dkv, dlat, w, att, grads, out_keep, out_send, xm, xl, br, out_all, sems = refs[2 * count :]
    images, media_rows = dkv.shape[1:3]
    block_m, block_l = images * media_rows, dlat.shape[0] // count
    pairs = []
    for k in range(count):
        pairs.append((slots[k].at[pl.ds(0, block_m)], xm.at[pl.ds(k * block_m, block_m)]))
        pairs.append((slots[k].at[pl.ds(block_m, block_l)], xl.at[pl.ds(k * block_l, block_l)]))
        pairs.append((branch[k], br.at[pl.ds(k * block_l, block_l)]))
    copies = begin(pairs, sems)
    for copy in copies:
        copy.wait()
    flat = att[...].reshape(count * block_l, lay.block).astype(BF)
    total = dot(flat, br[...], TN)[lay.v_off : lay.v_off + lay.span]
    per_ring, own = out_keep.shape[0], out_keep.shape[1]
    for q in range(per_ring * ring):
        out_all[q] = total[q * own : (q + 1) * own].astype(BF)
    me = me_ref[0]
    for j in range(per_ring):
        for r in range(ring):
            piece = out_all[j * ring + ((me % ring) ^ r)]
            if r:
                out_send[r - 1, j] = piece
            else:
                out_keep[j] = piece
    right = dkv[...].reshape(count * block_m, lay.q_at)
    width = xm.shape[1]
    step = 256 if width % 256 == 0 else 128
    for at in range(0, width, step):
        g_media = dot(xm[:, at : at + step], right, TN)
        g_lat = dot(xl[:, at : at + step], dlat[...], TN)
        block = w[at : at + step, :].astype(F32)
        base = block[:, : lay.q_at]
        row_media = block[:, lay.gain_at : lay.gain_at + 1]
        row_lat = block[:, lay.gain_at + 1 : lay.gain_at + 2]
        gain_media = jnp.sum(g_media * base, 1, keepdims=True)
        gain_lat = jnp.sum(g_lat[:, : lay.q_at] * base, 1, keepdims=True)
        rest = g_lat[:, lay.q_at :]
        lane = lax.broadcasted_iota(jnp.int32, rest.shape, 1) + lay.q_at
        rest = jnp.where(lane == lay.gain_at, gain_media, rest)
        rest = jnp.where(lane == lay.gain_at + 1, gain_lat, rest)
        grads[at : at + step, : lay.q_at] = (
            g_media * row_media + g_lat[:, : lay.q_at] * row_lat
        ).astype(BF)
        grads[at : at + step, lay.q_at :] = rest.astype(BF)


def mixed_kernel(keep_a, got_a, keep_b, got_b, lats, mixed, normed):
    half = keep_a.shape[0]
    for at, keep, got in ((0, keep_a, got_a), (half, keep_b, got_b)):
        value = keep[...] + got[...].astype(F32) + lats[at : at + half, :].astype(F32)
        mixed[at : at + half, :] = value
        normed[at : at + half, :] = normalize(value)[0].astype(BF)


def erf_parts(values):
    cdf = 0.5 * (1.0 + lax.erf(values * 0.7071067811865476))
    return cdf, cdf + values * jnp.exp(-0.5 * values * values) * GAUSS_DENSITY


def ffn_kernel(count, *refs):
    rows_in, cots = refs[:count], refs[count : 2 * count]
    w_hbm, hidden, pre_grad, even, odd, x, c, w, sems = refs[2 * count :]
    rows = rows_in[0].shape[0]
    part = w.shape[1] // 2
    pairs = [(w_hbm, w)]
    pairs += [(rows_in[k], x.at[pl.ds(k * rows, rows)]) for k in range(count)]
    pairs += [(cots[k], c.at[pl.ds(k * rows, rows)]) for k in range(count)]
    copies = begin(pairs, sems)
    copies[0].wait()
    step = 2
    for k in range(0, count, step):
        here = slice(k * rows, (k + step) * rows)
        for copy in copies[1 + k : 1 + k + step]:
            copy.wait()
        pre = dot(x[here, :], w[:, :part])
        cdf, slope = erf_parts(pre)
        hidden[here, :] = (pre * cdf).astype(BF)
        for copy in copies[1 + count + k : 1 + count + k + step]:
            copy.wait()
        grad = (dot(c[here, :], w[:, part:]) * slope).astype(BF)
        pre_grad[here, :] = grad
        back = dot(grad, w[:, :part], NT).astype(BF)
        even[k // 2] = back[:rows]
        odd[k // 2] = back[rows:]


def down_kernel(count, hidden, w, even, odd):
    part = hidden.shape[1]
    put_slots(dot(hidden[...], w[:, part:], NT).astype(BF), count, even, odd)


def ffn_weight_grad_kernel(count, *refs):
    rows_in, right = refs[:count], refs[count]
    total, x, sems = refs[count + 1 :]
    rows = rows_in[0].shape[0]
    copies = begin([(r, x.at[pl.ds(k * rows, rows)]) for k, r in enumerate(rows_in)], sems)
    for copy in copies:
        copy.wait()
    width = x.shape[1]
    step = 256 if width % 256 == 0 else 128
    for at in range(0, width, step):
        total[at : at + step, :] = dot(x[:, at : at + step], right[...], TN).astype(BF)


def add_kernel(left, right, out):
    out[...] = (left[...].astype(F32) + right[...].astype(F32)).astype(out.dtype)


def resampled_kernel(keep, got, far, mixed, out):
    total = mixed[...] + keep[...] + got[...].astype(F32) + far[...].astype(F32)
    out[...] = total.astype(out.dtype)


def ffn_back_kernel(keep, got, far, mixed, cot, mixed_grad, branch):
    normed, inverse = normalize(mixed[...])
    back = keep[...] + got[...].astype(F32) + far[...].astype(F32)
    grad = cot[...].astype(F32) + norm_back(back, normed, inverse)
    mixed_grad[...] = grad
    branch[...] = grad.astype(BF)


def final_kernel(keep_a, got_a, keep_b, got_b, media, lats, mixed_grad, media_grad, lat_grad):
    half, rows = keep_a.shape[0], media.shape[0]
    first = keep_a[...] + got_a[...].astype(F32)
    normed, inverse = normalize(media[:half, :].astype(F32))
    media_grad[:half, :] = norm_back(first, normed, inverse)
    second = keep_b[...] + got_b[...].astype(F32)
    normed, inverse = normalize(media[half:, :].astype(F32))
    media_grad[half:, :] = norm_back(second[: rows - half], normed, inverse)
    normed, inverse = normalize(lats[...].astype(F32))
    lat_grad[...] = mixed_grad[...] + norm_back(second[rows - half :], normed, inverse)


def body(
    latents,
    media,
    media_lengths,
    cotangent,
    query_weight,
    kv_weight,
    out_weight,
    in_weight,
    down_weight,
    media_gain,
    latent_gain,
    ffn_gain,
):
    images, lat_rows, width = latents.shape
    media_rows = media.shape[1]
    nb, nd = lax.axis_size("blk"), lax.axis_size("dp")
    size = width // HEADS
    heads = HEADS // nb
    own = query_weight.shape[0]
    plane = nb * own
    span = heads * size
    lay = Layout(span, size)
    hidden_width = in_weight.shape[1]
    part = hidden_width // nb // 2
    me = lax.axis_index("blk").astype(jnp.int32).reshape(1)
    dz = lax.axis_index("dp").astype(jnp.int32).reshape(1)
    ring = size // own
    per_ring = nd // ring
    groups = nb // ring
    block_m, block_l = images * media_rows, images * lat_rows
    block = block_m + block_l
    all_m, all_l = nb * block_m, nb * block_l

    sems = pltpu.SemaphoreType.DMA

    gains = jnp.stack([media_gain, latent_gain, ffn_gain], 1).astype(F32)
    (attn_parts,) = call(
        partial(split_attn_kernel, lay, ring, per_ring), [((nb, own, lay.width), BF, "v")], "vvv"
    )(kv_weight, query_weight, gains)
    quick = ring == 2 and own % 16 == 0
    if quick:
        out_near = [out_weight] + [swap(out_weight, k, "dp") for k in range(1, nd)]
    else:
        ring_groups = [[g * ring + i for i in range(ring)] for g in range(groups)]
        out_w = lax.all_gather(out_weight, "dp", axis=0, tiled=False)
        out_w = lax.all_gather(out_w, "blk", axis=0, tiled=False, axis_index_groups=ring_groups)
        out_w = out_w.transpose(1, 0, 2, 3).reshape(nd * ring * own, width)
        out_near = [out_w]

    cot_flat = cotangent.reshape(block_l, width)
    cot_far = swap(cot_flat, 1, "dp")
    mine = lax.all_to_all(attn_parts, "blk", 0, 0, tiled=True).reshape(plane, -1)
    attn_w = lax.all_gather(after(mine, cot_far, *out_near), "dp", axis=0, tiled=True)

    media_flat = media.reshape(block_m, width)
    lat_flat = latents.reshape(block_l, width)
    (normed,) = call(prepare_kernel, [((block, width), BF, "v")], "dd", cost=3)(
        after(media_flat, attn_parts), lat_flat
    )
    slots_first = gather_first(normed)
    (ffn_parts,) = call(
        partial(split_ffn_kernel, nb), [((nd * nb, own, 2 * part), BF, "v")], "ddv", cost=5
    )(after(in_weight, *slots_first.values()), down_weight, gains)
    slots = gather_rest(slots_first, ffn_parts, *out_near)
    ffn_w = lax.all_to_all(after(ffn_parts, attn_w), ("dp", "blk"), 0, 0, tiled=True)
    ffn_w = ffn_w.reshape(width, 2 * part)

    if quick:
        near = jnp.stack(out_near)
        far = swap(near, 1)
        core = lax.axis_index("blk") % 2
        both = jnp.where(core == 0, jnp.stack([near, far], 1), jnp.stack([far, near], 1))
        out_w = [lax.dynamic_index_in_dim(both, dz[0] ^ k, 0, False) for k in range(nd)]
        out_w = jnp.concatenate(out_w, 0).reshape(nd * ring * own, width)

    def pair(block):
        return jnp.concatenate([block, swap(block, 1, "dp")], 0)

    cot_first = gather_first(after(jnp.concatenate([cot_flat, cot_far], 0), *slots))

    half_l = (nb // 2, block_l, width)
    half_pair = (nb // 2, 2 * block_l, width)
    half_all = (nb // 2, block, width)
    kv, lat_proj, attended, totals, even, odd = call(
        partial(forward_kernel, nb, lay, ring),
        [
            ((nb, images, media_rows, lay.q_at), BF, "v"),
            ((nb, images, lat_rows, lay.width), F32, "v"),
            ((nb, images, lat_rows, lay.block), F32, "v"),
            ((images, heads * nb * lat_rows, 128), F32, "v"),
            (half_l, BF, "v"),
            (half_l, BF, "v"),
        ],
        "ss" + "h" * (nb + 2),
        [
            pltpu.VMEM((all_m, width), BF),
            pltpu.VMEM((all_l, width), BF),
            pltpu.VMEM((width, lay.width), BF),
            pltpu.VMEM((width, lay.q_at), BF),
            pltpu.VMEM((width, lay.width), BF),
            pltpu.VMEM((ring * span, width), BF),
            pltpu.VMEM((lay.block, width), BF),
            sems((2 + 2 * nb,)),
        ],
        cost=14,
    )(me, media_lengths, *slots, attn_w, out_w)
    mixed, ffn_in = call(
        mixed_kernel, [((block_l, width), F32, "v"), ((block_l, width), BF, "v")], "ddddd"
    )(*scatter_sum(even, after(odd, *cot_first.values())), lat_flat)
    cot_slots = gather_rest(cot_first)
    in_slots = gather_slots(pair(ffn_in))
    hidden, pre_grad, even, odd = call(
        partial(ffn_kernel, nb),
        [((2 * all_l, part), BF, "v")] * 2 + [(half_pair, BF, "v")] * 2,
        "h" * (2 * nb + 1),
        [
            pltpu.VMEM((2 * all_l, width), BF),
            pltpu.VMEM((2 * all_l, width), BF),
            pltpu.VMEM((width, 2 * part), BF),
            sems((2 * nb + 1,)),
        ],
        cost=11,
    )(*in_slots, *cot_slots, ffn_w)

    def both_planes(terms):
        keep, got, keep_far, got_far = terms
        (sent,) = call(add_kernel, [(keep_far.shape, BF, "v")], "dd")(keep_far, got_far)
        return keep, got, sent, swap(sent, 1, "dp")

    def ffn_weight_grad(rows, right):
        return call(
            partial(ffn_weight_grad_kernel, nb),
            [((width, part), BF, "v")],
            "h" * nb + "d",
            [pltpu.VMEM((2 * all_l, width), BF), sems((nb,))],
            cost=6,
        )(*rows, right)

    def to_rows(grads):
        return lax.all_to_all(
            grads.reshape(nd * nb, own, part), ("dp", "blk"), 0, 0, tiled=True
        )

    made = {}

    def beside_scatter(sent):
        made["down"] = ffn_weight_grad(cot_slots, after(hidden, sent))
        return made["down"]

    keep, got, sent, far = both_planes(scatter_sum(even, odd, [lambda sent: (), beside_scatter]))
    made["in"] = ffn_weight_grad(in_slots, after(pre_grad, sent))
    even_d, odd_d = call(partial(down_kernel, nb), [(half_pair, BF, "v")] * 2, "dd", cost=5)(
        after(hidden, *made["in"]), ffn_w
    )
    mixed_grad, branch = call(
        ffn_back_kernel, [((block_l, width), F32, "v"), ((block_l, width), BF, "v")], "d" * 5
    )(keep, got, after(far, even_d), mixed, cot_flat)
    down_terms = scatter_sum(even_d, odd_d)
    branch_slots = gather_slots(branch)
    ffn_sums = to_rows(made["in"][0]), to_rows(made["down"][0])

    dkv, dlat = call(
        partial(backward_kernel, nb, lay, ring),
        [(kv.shape, BF, "v"), ((all_l, lay.width), BF, "v")],
        "ss" + "h" * (nb + 5),
        [
            pltpu.VMEM((all_l, width), BF),
            pltpu.VMEM(kv.shape, BF),
            pltpu.VMEM(lat_proj.shape, F32),
            pltpu.VMEM((ring * span, width), BF),
            pltpu.VMEM((lay.block, width), BF),
            pltpu.VMEM(attended.shape, F32),
            pltpu.VMEM(totals.shape, F32),
            pltpu.VMEM(lat_proj.shape, F32),
            pltpu.VMEM(attended.shape, F32),
            sems((nb + 5,)),
        ],
        cost=9,
    )(me, media_lengths, *branch_slots, kv, lat_proj, out_w, attended, totals)

    attn_grads, out_keep, out_send = call(
        partial(attn_weight_grad_kernel, nb, lay, ring),
        [
            ((width, lay.width), BF, "v"),
            ((per_ring, own, width), BF, "v"),
            ((ring - 1, per_ring, own, width), BF, "v"),
        ],
        "s" + "h" * (2 * nb) + "dddd",
        [
            pltpu.VMEM((all_m, width), BF),
            pltpu.VMEM((all_l, width), BF),
            pltpu.VMEM((all_l, width), BF),
            pltpu.VMEM((per_ring * ring, own, width), BF),
            sems((3 * nb,)),
        ],
        cost=13,
    )(me, *slots, *branch_slots, dkv, dlat, attn_w, attended)

    keep, got, _, far = both_planes(down_terms)
    (resampled,) = call(resampled_kernel, [((block_l, width), BF, "v")], "dddd")(
        keep, got, far, mixed
    )
    attn_sum = lax.psum_scatter(attn_grads, "dp", scatter_dimension=0, tiled=True)

    even, odd = call(
        partial(input_grad_kernel, nb, lay),
        [(half_all, BF, "v"), (half_all, BF, "v")],
        "ddd",
        [pltpu.VMEM((width, lay.q_at), BF), pltpu.VMEM((width, lay.width), BF)],
        cost=10,
    )(after(dkv, attn_grads), dlat, attn_w)

    media_grad, latents_grad = call(
        final_kernel, [((block_m, width), F32, "v"), ((block_l, width), F32, "v")], "d" * 7, cost=5
    )(
        *scatter_sum(even, odd, [lambda sent: (), lambda sent: (attn_sum,)]),
        media_flat,
        lat_flat,
        mixed_grad,
    )

    in_grad, down_grad, ffn_gain_grad = call(
        partial(finish_ffn_kernel, nb),
        [((own, hidden_width), F32, "v")] * 2 + [((own, 128), F32, "v")],
        "dddv",
        cost=4,
    )(*ffn_sums, in_weight, gains)

    attn_slots = lax.all_to_all(attn_sum.reshape(nb, own, -1), "blk", 0, 0, tiled=True)
    query_grad, kv_grad, gain_grads = call(
        partial(finish_attn_kernel, lay, ring, per_ring),
        [((own, width), F32, "v"), ((own, 2 * width), F32, "v"), ((own, 128), F32, "v")],
        "ddv",
    )(attn_slots, query_weight, gains)

    out_send = after(out_send, attn_sum)
    pieces = [out_keep] + [swap(out_send[r - 1], r) for r in range(1, ring)]
    pieces = jnp.stack(pieces)
    rank = lax.axis_index("blk") % ring
    pieces = [lax.dynamic_index_in_dim(pieces, rank ^ r, 0, False) for r in range(ring)]
    out_rows = jnp.concatenate(pieces, 0).reshape(nd * own, width)
    out_grad = lax.psum_scatter(out_rows, "dp", scatter_dimension=0, tiled=True).astype(F32)
    return (
        resampled.reshape(latents.shape),
        latents_grad.reshape(latents.shape),
        media_grad.reshape(media.shape),
        query_grad,
        kv_grad,
        out_grad,
        in_grad,
        down_grad,
        gain_grads[:, 0],
        gain_grads[:, 1],
        ffn_gain_grad[:, 0],
    )


def solution(mesh):
    rows = P("dp", "blk", None)
    weight = P(("dp", "blk"), None)
    gain = P(("dp", "blk"))
    return jax.shard_map(
        body,
        mesh=mesh,
        in_specs=(rows, rows, P("dp"), rows) + (weight,) * 5 + (gain,) * 3,
        out_specs=(rows,) * 3 + (weight,) * 5 + (gain,) * 3,
        check_vma=False,
    )
```

time: 468 us -> 397 us (0.85)
  local copies, waits for them, and re-layouts: 75.7 us -> 24.1 us
  Pallas kernels: 79.7 us -> 130 us
  other arithmetic: 42.4 us -> 5.55 us
  blocking collectives: 22.7 us -> 0 us
  starting transfers between devices: 77.9 us -> 72.5 us
    pallas_call x10 -> x27, Pallas kernels: 79.7 us -> 130 us  [run(): pl.pallas_call(fetching if fetched else kernel, out_shape=[jax.ShapeDtype...]
    ppermute x65 -> x61, waiting for transfers between devices: 86.4 us -> 120 us  [swap(): lax.ppermute(array, axis, [(i, i ^ bit) for i in range(lax.axis_size(axis...]
    reduce_scatter x4 -> x2, waiting for transfers between devices: 40.6 us -> 13.7 us  [the longest x1 13.7 us: body(): lax.psum_scatter(attn_grads, 'dp', scatter_dimension=0, tiled=True)]
    unnamed x227 -> x111, local copies, waits for them, and re-layouts: 40.6 us -> 18.7 us
    all_gather x1 -> x0, blocking collectives: 17.6 us -> none  [body(): all_out = lax.all_gather(out_weight, 'dp', axis=0, tiled=False)]
    reduce_sum x16 -> x0, other arithmetic: 12.2 us -> none  [the longest x1 4.01 us: body(): gain_lat = jnp.sum(gl_k * w_k + gl_v * w_v, 1, keepdims=True)]
    add x25 -> x0, other arithmetic: 11.7 us -> none  [the longest x5 5.83 us: scatter_sum(): total = even.astype(F32) + swap(odd, 1).astype(F32)]
    concatenate x7 -> x5, local copies, waits for them, and re-layouts: 9.83 us -> 0.08 us  [the longest x4 0.07 us: gather_rest(): jnp.concatenate([swap(slots[offset ^ low][:half], low), swap(slots[offset...]
  transfers between devices with their start and end apart: 77 -> 69, of which waited for: 32 -> 34; matrix products, arithmetic and copies ran while one was open for 15% -> 2% of each run, Pallas kernels for 14% -> 28%
where the time goes in v2:
time: 397 us; the launch traced here: 392 us
  waiting for transfers between devices  145 us (37%)
  Pallas kernels  130 us (33%)
  starting transfers between devices  72.5 us (18%)
  local copies, waits for them, and re-layouts  24.1 us (6%)
  between operations  14.8 us (4%)
  other arithmetic  5.55 us (1%)
    pallas_call x27, Pallas kernels, run(): pl.pallas_call(fetching if fetched else kernel, out_shape=[jax.ShapeDtype...  130 us
    ppermute x61, waiting for transfers between devices, swap(): lax.ppermute(array, axis, [(i, i ^ bit) for i in range(lax.axis_size(axis...  120 us
    ppermute x61, starting transfers between devices, swap(): lax.ppermute(array, axis, [(i, i ^ bit) for i in range(lax.axis_size(axis...  49.7 us
    unnamed x111, local copies, waits for them, and re-layouts  18.7 us
    reduce_scatter x1, waiting for transfers between devices, body(): lax.psum_scatter(attn_grads, 'dp', scatter_dimension=0, tiled=True)  13.7 us
    all_gather x1, waiting for transfers between devices, body(): lax.all_gather(after(mine, cot_far, *out_near), 'dp', axis=0, tiled=True)  11.8 us
    all_to_all x2, starting transfers between devices, to_rows(): lax.all_to_all(grads.reshape(nd * nb, own, part), ('dp', 'blk'), 0, 0, ti...  9.68 us
  transfers between devices with their start and end apart: 69, of which 34 were waited for; matrix products, arithmetic and copies ran while one was open for 2% of the time, Pallas kernels for 28%

profile of v2, /device:TPU:0, one launch (start us, length us, event | category | flops | bytes accessed | tf_op | source)
XLA Modules:
  0.0 392.0 jit_solution(13748562893769535127)
XLA Ops:
  10.7 5.2 %all-to-all-start = ((bf16[8,48,640]{2,1,0:T(8,128)(2,1)}), bf16[8,48,640]{2,1,0:T(8,128)(2,1)S(1)}, u32[]{:S(2)}, u32[]{:S(2)}) async-start(bf16[8,48,640]{2,1,0:T(8,128)(2,1)} %shard_map.203), calls=%async_computation | async-start | bytes 983040 | tf_op jit(solution)/shard_map/all_to_all | solution.py:668
  15.9 2.7 shard_map.204.refs_0_.refs_1_
  24.2 2.6 collective-permute-start.4
  26.8 5.3 %collective-permute-done.3 = bf16[48,1536]{1,0:T(8,128)(2,1)S(1)} collective-permute-done((bf16[48,1536]{1,0:T(8,128)(2,1)S(1)}, bf16[48,1536]{1,0:T(8,128)(2,1)S(1)}, u32[]{:S(2)}, u32[]{:S(2)}) %collective-permute-start.3) | collective-permute-done | bytes 147488 | tf_op jit(solution)/shard_map/ppermute | solution.py:23
  32.1 3.2 collective-permute-start.5
  35.4 4.7 %collective-permute-done.5 = bf16[48,1536]{1,0:T(8,128)(2,1)S(1)} collective-permute-done((bf16[48,1536]{1,0:T(8,128)(2,1)S(1)}, bf16[48,1536]{1,0:T(8,128)(2,1)S(1)}, u32[]{:S(2)}, u32[]{:S(2)}) %collective-permute-start.5) | collective-permute-done | bytes 147488 | tf_op jit(solution)/shard_map/ppermute | solution.py:23
  41.0 4.6 %collective-permute-done.1.refs_2_.refs_3_ = bf16[320,1536]{1,0:T(8,128)(2,1)} collective-permute-done((bf16[320,1536]{1,0:T(8,128)(2,1)}, bf16[320,1536]{1,0:T(8,128)(2,1)}, u32[]{:S(2)}, u32[]{:S(2)}) %collective-permute-start.1) | collective-permute-done | bytes 983072 | tf_op jit(solution)/shard_map/ppermute | solution.py:23
  48.1 3.7 shard_map.205
  54.3 5.3 %collective-permute-done.8 = bf16[160,1536]{1,0:T(8,128)(2,1)S(1)} collective-permute-done((bf16[160,1536]{1,0:T(8,128)(2,1)S(1)}, bf16[160,1536]{1,0:T(8,128)(2,1)S(1)}, u32[]{:S(2)}, u32[]{:S(2)}) %collective-permute-start.8) | collective-permute-done | bytes 491552 | tf_op jit(solution)/shard_map/ppermute | solution.py:23
  59.7 6.2 %collective-permute-done.9 = bf16[160,1536]{1,0:T(8,128)(2,1)S(1)} collective-permute-done((bf16[160,1536]{1,0:T(8,128)(2,1)S(1)}, bf16[160,1536]{1,0:T(8,128)(2,1)S(1)}, u32[]{:S(2)}, u32[]{:S(2)}) %collective-permute-start.9) | collective-permute-done | bytes 491552 | tf_op jit(solution)/shard_map/ppermute | solution.py:23
  70.9 11.8 %all-gather.2.cloned.1.call-done.refs_8_.refs_19_.refs_2_ = bf16[1536,640]{1,0:T(8,128)(2,1)} async-done(((bf16[384,640]{1,0:T(8,128)(2,1)}), bf16[1536,640]{1,0:T(8,128)(2,1)}) %all-gather.2.cloned.1.call-update) | async-done | bytes 1966096 | tf_op jit(solution)/shard_map/all_gather | solution.py:669
  82.7 3.6 all-to-all-start.1
  86.3 14.4 %shard_map.206 = (bf16[8,8,32,384]{3,2,1,0:T(8,128)(2,1)}, f32[8,8,8,640]{3,2,1,0:T(8,128)}, f32[8,8,8,256]{3,2,1,0:T(8,128)}, f32[8,128,128]{2,1,0:T(8,128)}, b...) custom-call(s32[1]{0:T(128)} %bitcast.me_ref.refs_0_, s32[8]{0:T(128)} %len_ref.3, ...), custom_call_target="tpu_custom_call" | custom-call | flops 16099999744 | bytes 50400000 | tf_op jit(solution)/shard_map/pallas_call | solution.py:152
  109.8 11.1 %collective-permute-done.16.refs_1_ = bf16[2,32,1536]{2,1,0:T(8,128)(2,1)S(1)} collective-permute-done((bf16[2,32,1536]{2,1,0:T(8,128)(2,1)}, bf16[2,32,1536]{2,1,0:T(8,128)(2,1)S(1)}, u32[]{:S(2)}, u32[]{:S(2)}) %collective-permute-start.16) | collective-permute-done | bytes 196640 | tf_op jit(solution)/shard_map/ppermute | solution.py:23
  126.1 3.9 collective-permute-done.18
  136.0 6.6 %collective-permute-done.20 = bf16[64,1536]{1,0:T(8,128)(2,1)S(1)} collective-permute-done((bf16[64,1536]{1,0:T(8,128)(2,1)}, bf16[64,1536]{1,0:T(8,128)(2,1)S(1)}, u32[]{:S(2)}, u32[]{:S(2)}) %collective-permute-start.20) | collective-permute-done | bytes 196640 | tf_op jit(solution)/shard_map/ppermute | solution.py:23
  145.8 8.5 %collective-permute-done.24.refs_4_ = bf16[128,1536]{1,0:T(8,128)(2,1)S(1)} collective-permute-done((bf16[128,1536]{1,0:T(8,128)(2,1)S(1)}, bf16[128,1536]{1,0:T(8,128)(2,1)S(1)}, u32[]{:S(2)}, u32[]{:S(2)}) %collective-permute-start.24) | collective-permute-done | bytes 393248 | tf_op jit(solution)/shard_map/ppermute | solution.py:23
  156.6 5.5 %collective-permute-done.26 = bf16[64,1536]{1,0:T(8,128)(2,1)S(1)} collective-permute-done((bf16[64,1536]{1,0:T(8,128)(2,1)S(1)}, bf16[64,1536]{1,0:T(8,128)(2,1)S(1)}, u32[]{:S(2)}, u32[]{:S(2)}) %collective-permute-start.26) | collective-permute-done | bytes 196640 | tf_op jit(solution)/shard_map/ppermute | solution.py:23
  162.4 5.4 %collective-permute-done.27 = bf16[64,1536]{1,0:T(8,128)(2,1)S(1)} collective-permute-done((bf16[64,1536]{1,0:T(8,128)(2,1)S(1)}, bf16[64,1536]{1,0:T(8,128)(2,1)S(1)}, u32[]{:S(2)}, u32[]{:S(2)}) %collective-permute-start.27) | collective-permute-done | bytes 196640 | tf_op jit(solution)/shard_map/ppermute | solution.py:23
  172.8 11.1 %shard_map.210 = (bf16[1024,384]{1,0:T(8,128)(2,1)}, bf16[1024,384]{1,0:T(8,128)(2,1)}, bf16[4,128,1536]{2,1,0:T(8,128)(2,1)}, bf16[4,128,1536]{2,1,0:T(8,128)(2,1)}) custom-call(bf16[128,1536]{1,0:T(8,128)(2,1)} %copy-done.16, bf16[128,1536]{1,0:T(8,128)(2,1)} %copy-done.31, bf16[128,1536]{1,0:T(8,128)(2,1)} %copy-done.13, bf16[128,1536]{1,0:T(8,128)(2,1)} %copy-done.33, ...), custom_call_target="tpu_custom_call" | custom-call | flops 12650000384 | bytes 39600000 | tf_op jit(solution)/shard_map/pallas_call | solution.py:152
  184.1 3.5 collective-permute-done.35.refs_1_
  188.8 2.7 shard_map.211
  192.0 5.9 %shard_map.212 = bf16[1536,384]{1,0:T(8,128)(2,1)} custom-call(bf16[128,1536]{1,0:T(8,128)(2,1)} %copy-done.5, bf16[128,1536]{1,0:T(8,128)(2,1)} %copy-done.29, bf16[128,1536]{1,0:T(8,128)(2,1)} %copy-done.10, bf16[128,1536]{1,0:T(8,128)(2,1)} %copy-done.30, bf16[128,1536]{1,0:T(8,128)(2,1)} %copy-done.11, bf16[128,1536]{1,0:T(8,128)(2,1)} %copy-done.32, ...), custom_call_target="tpu_custom_call" | custom-call | flops 6899999744 | bytes 21600000 | tf_op jit(solution)/shard_map/pallas_call | solution.py:152
  197.9 5.1 %collective-permute-done.36.refs_1_ = bf16[2,64,1536]{2,1,0:T(8,128)(2,1)S(1)} collective-permute-done((bf16[2,64,1536]{2,1,0:T(8,128)(2,1)}, bf16[2,64,1536]{2,1,0:T(8,128)(2,1)S(1)}, u32[]{:S(2)}, u32[]{:S(2)}) %collective-permute-start.36) | collective-permute-done | bytes 393248 | tf_op jit(solution)/shard_map/ppermute | solution.py:23
  203.8 2.5 shard_map.213
  208.3 4.4 %collective-permute-done.38 = bf16[1,64,1536]{2,1,0:T(8,128)(2,1)S(1)} collective-permute-done((bf16[1,64,1536]{2,1,0:T(8,128)(2,1)}, bf16[1,64,1536]{2,1,0:T(8,128)(2,1)S(1)}, u32[]{:S(2)}, u32[]{:S(2)}) %collective-permute-start.38) | collective-permute-done | bytes 196640 | tf_op jit(solution)/shard_map/ppermute | solution.py:23
  215.3 5.9 %shard_map.215 = bf16[1536,384]{1,0:T(8,128)(2,1)} custom-call(bf16[128,1536]{1,0:T(8,128)(2,1)} %copy-done.16, bf16[128,1536]{1,0:T(8,128)(2,1)} %copy-done.31, bf16[128,1536]{1,0:T(8,128)(2,1)} %copy-done.13, bf16[128,1536]{1,0:T(8,128)(2,1)} %copy-done.33, bf16[128,1536]{1,0:T(8,128)(2,1)} %copy-done.12, bf16[128,1536]{1,0:T(8,128)(2,1)} %copy-done.34, ...), custom_call_target="tpu_custom_call" | custom-call | flops 6899999744 | bytes 21600000 | tf_op jit(solution)/shard_map/pallas_call | solution.py:152
  221.2 5.4 %shard_map.216 = (bf16[4,128,1536]{2,1,0:T(8,128)(2,1)}, bf16[4,128,1536]{2,1,0:T(8,128)(2,1)}) custom-call(bf16[1024,384]{1,0:T(8,128)(2,1)} %get-tuple-element.120.refs_8_.refs_0_, bf16[1536,768]{1,0:T(8,128)(2,1)} %bitcast.56), custom_call_target="tpu_custom_call" | custom-call | flops 5750000128 | bytes 18000000 | tf_op jit(solution)/shard_map/pallas_call | solution.py:152
  227.3 2.5 shard_map.221
  231.5 4.3 %collective-permute-done.50.refs_4_.refs_13_ = bf16[64,1536]{1,0:T(8,128)(2,1)S(1)} collective-permute-done((bf16[64,1536]{1,0:T(8,128)(2,1)}, bf16[64,1536]{1,0:T(8,128)(2,1)S(1)}, u32[]{:S(2)}, u32[]{:S(2)}) %collective-permute-start.50) | collective-permute-done | bytes 196640 | tf_op jit(solution)/shard_map/ppermute | solution.py:23
  243.2 3.9 all-to-all-start.4
  248.4 8.7 %shard_map.222 = (bf16[8,8,32,384]{3,2,1,0:T(8,128)(2,1)}, bf16[512,640]{1,0:T(8,128)(2,1)}) custom-call(s32[1]{0:T(128)} %bitcast.me_ref.refs_0_, s32[8]{0:T(128)} %len_ref.3, bf16[64,1536]{1,0:T(8,128)(2,1)} %get-tuple-element.135.refs_0_.refs_9_, bf16[64,1536]{1,0:T(8,128)(2,1)} %copy-done.41, bf16[64,1536]{1,0:T(8,128)(2,1)} %copy-done.18, ...), custom_call_target="tpu_custom_call" | custom-call | flops 10350000128 | bytes 32400000 | tf_op jit(solution)/shard_map/pallas_call | solution.py:152
  257.1 12.8 %shard_map.223 = (bf16[1536,640]{1,0:T(8,128)(2,1)}, bf16[2,48,1536]{2,1,0:T(8,128)(2,1)}, bf16[1,2,48,1536]{3,2,1,0:T(8,128)(2,1)}) custom-call(s32[1]{0:T(128)} %bitcast.me_ref.refs_0_, bf16[320,1536]{1,0:T(8,128)(2,1)} %shard_map.204.refs_0_.refs_1_, bf16[320,1536]{1,0:T(8,128)(2,1)} %collective-permute-done.refs_1_.refs_2_, ...), custom_call_target="tpu_custom_call" | custom-call | flops 14949999616 | bytes 46800000 | tf_op jit(solution)/shard_map/pallas_call | solution.py:152
  269.9 10.0 %shard_map.224 = (bf16[4,320,1536]{2,1,0:T(8,128)(2,1)}, bf16[4,320,1536]{2,1,0:T(8,128)(2,1)}) custom-call(bf16[8,8,32,384]{3,2,1,0:T(8,128)(2,1)} %get-tuple-element.143.refs_17_.refs_0_, bf16[512,640]{1,0:T(8,128)(2,1)} %get-tuple-element.141.refs_18_.refs_1_, bf16[1536,640]{1,0:T(8,128)(2,1)} %all-gather.2.cloned.1.call-done.refs_8_.refs_19_.refs_2_), custom_call_target="tpu_custom_call" | custom-call | flops 11500000256 | bytes 36000000 | tf_op jit(solution)/shard_map/pallas_call | solution.py:152
  281.6 5.8 %all-to-all-start.3 = ((bf16[32,48,384]{2,1,0:T(8,128)(2,1)}), bf16[32,48,384]{2,1,0:T(8,128)(2,1)S(1)}, u32[]{:S(2)}, u32[]{:S(2)}) async-start(bf16[32,48,384]{2,1,0:T(8,128)(2,1)} %bitcast.46), calls=%async_computation.5 | async-start | bytes 2359296 | tf_op jit(solution)/shard_map/all_to_all | solution.py:756
  289.4 2.7 shard_map.217
  295.4 12.5 %collective-permute-done.40.refs_1_ = bf16[2,64,1536]{2,1,0:T(8,128)(2,1)S(1)} collective-permute-done((bf16[2,64,1536]{2,1,0:T(8,128)(2,1)}, bf16[2,64,1536]{2,1,0:T(8,128)(2,1)S(1)}, u32[]{:S(2)}, u32[]{:S(2)}) %collective-permute-start.40) | collective-permute-done | bytes 393248 | tf_op jit(solution)/shard_map/ppermute | solution.py:23
  308.8 2.5 shard_map.218
  313.7 5.8 %collective-permute-done.43 = bf16[1,64,1536]{2,1,0:T(8,128)(2,1)S(1)} collective-permute-done((bf16[1,64,1536]{2,1,0:T(8,128)(2,1)}, bf16[1,64,1536]{2,1,0:T(8,128)(2,1)S(1)}, u32[]{:S(2)}, u32[]{:S(2)}) %collective-permute-start.43) | collective-permute-done | bytes 196640 | tf_op jit(solution)/shard_map/ppermute | solution.py:23
  323.7 6.3 %shard_map.225 = (f32[2,160,1536]{2,1,0:T(8,128)}, bf16[2,160,1536]{2,1,0:T(8,128)(2,1)}, f32[2,160,1536]{2,1,0:T(8,128)}, bf16[2,160,1536]{2,1,0:T(8,128)(2,1)}) custom-call(bf16[4,320,1536]{2,1,0:T(8,128)(2,1)} %get-tuple-element.144.refs_0_, bf16[4,320,1536]{2,1,0:T(8,128)(2,1)} %collective-permute-done.55.refs_1_), custom_call_target="tpu_custom_call" | custom-call | flops 2300000000 | bytes 7200000 | tf_op jit(solution)/shard_map/pallas_call | solution.py:152
  330.0 2.5 collective-permute-start.56
  332.4 13.7 %reduce-scatter.3.cloned.1.call-done = bf16[384,640]{1,0:T(8,128)(2,1)} async-done(((bf16[1536,640]{1,0:T(8,128)(2,1)}), bf16[384,640]{1,0:T(8,128)(2,1)}) %reduce-scatter.3.cloned.1.call-update) | async-done | bytes 491536 | tf_op jit(solution)/shard_map/reduce_scatter | solution.py:819
  347.2 4.2 %shard_map.229 = (f32[48,6144]{1,0:T(8,128)}, f32[48,6144]{1,0:T(8,128)}, f32[48,128]{1,0:T(8,128)}) custom-call(bf16[32,48,384]{2,1,0:T(8,128)(2,1)} %copy-done.3, bf16[32,48,384]{2,1,0:T(8,128)(2,1)} %copy-done.2, bf16[48,6144]{1,0:T(8,128)(2,1)} %refs_2_.1, f32[48,3]{1,0:T(8,128)} %convert_element_type.6.gains.refs_2_.refs_3_), custom_call_target="tpu_custom_call" | custom-call | flops 4600000000 | bytes 14400000 | tf_op jit(solution)/shard_map/pallas_call | solution.py:152
  352.8 3.8 all-to-all-start.2
  359.1 3.8 shard_map.226
  369.3 2.9 shard_map.228
  373.7 3.1 collective-permute-done.58
  379.0 4.6 %shard_map.227 = (f32[256,1536]{1,0:T(8,128)}, f32[64,1536]{1,0:T(8,128)}) custom-call(f32[160,1536]{1,0:T(8,128)} %bitcast.88, bf16[160,1536]{1,0:T(8,128)(2,1)} %bitcast.76, f32[160,1536]{1,0:T(8,128)} %bitcast.89, bf16[160,1536]{1,0:T(8,128)(2,1)} %bitcast.77, bf16[256,1536]{1,0:T(8,128)(2,1)} %bitcast.75, bf16[64,1536]{1,0:T(8,128)(2,1)} %bitcast.81, ...), custom_call_target="tpu_custom_call" | custom-call | flops 5750000128 | bytes 18000000 | tf_op jit(solution)/shard_map/pallas_call | solution.py:152
  (257 shorter events, 99.7 us)
Async XLA Ops:
  10.7 29.5 %all-to-all-start = ((bf16[8,48,640]{2,1,0:T(8,128)(2,1)}), bf16[8,48,640]{2,1,0:T(8,128)(2,1)S(1)}, u32[]{:S(2)}, u32[]{:S(2)}) async-start(bf16[8,48,640]{2,1,0:T(8,128)(2,1)} %shard_map.203), calls=%async_computation | async-start | bytes 983040 | tf_op jit(solution)/shard_map/all_to_all | solution.py:668
  15.9 66.8 %all-gather.2.cloned.1.call-start = ((), (), s32[]{:S(2)}) async-start(), calls=%async_computation.7 | async-start | bytes 2457600 | tf_op jit(solution)/shard_map/all_gather | solution.py:669
  18.6 26.9 %collective-permute-start.1 = (bf16[320,1536]{1,0:T(8,128)(2,1)}, bf16[320,1536]{1,0:T(8,128)(2,1)}, u32[]{:S(2)}, u32[]{:S(2)}) collective-permute-start(bf16[320,1536]{1,0:T(8,128)(2,1)} %shard_map.204.refs_0_.refs_1_), channel_id=1, source_target_pairs={{0,2},{1,3},{2,0},{3,1},{4,6},{5,7},{6,4},{7,5},{8,10},{9,11},{10,... | collective-permute-start | bytes 2949128 | tf_op jit(solution)/shard_map/ppermute | solution.py:23
  20.7 25.2 %collective-permute-start.2 = (bf16[320,1536]{1,0:T(8,128)(2,1)}, bf16[320,1536]{1,0:T(8,128)(2,1)}, u32[]{:S(2)}, u32[]{:S(2)}) collective-permute-start(bf16[320,1536]{1,0:T(8,128)(2,1)} %shard_map.204.refs_0_.refs_1_), channel_id=1, source_target_pairs={{0,4},{1,5},{2,6},{3,7},{4,0},{5,1},{6,2},{7,3},{8,12},{9,13},{10,... | collective-permute-start | bytes 2949128 | tf_op jit(solution)/shard_map/ppermute | solution.py:23
  22.1 9.9 %collective-permute-start.3 = (bf16[48,1536]{1,0:T(8,128)(2,1)S(1)}, bf16[48,1536]{1,0:T(8,128)(2,1)S(1)}, u32[]{:S(2)}, u32[]{:S(2)}) collective-permute-start(bf16[48,1536]{1,0:T(8,128)(2,1)S(1)} %copy-done.9), channel_id=1, source_target_pairs={{0,8},{8,0},{16,24},{24,16},{1,9},{9,1},{17,25},{25,17},{2,10},{10... | collective-permute-start | bytes 442376 | tf_op jit(solution)/shard_map/ppermute | solution.py:23
  23.7 16.4 %collective-permute-start.11 = (bf16[64,1536]{1,0:T(8,128)(2,1)S(1)}, bf16[64,1536]{1,0:T(8,128)(2,1)S(1)}, u32[]{:S(2)}, u32[]{:S(2)}) collective-permute-start(bf16[64,1536]{1,0:T(8,128)(2,1)S(1)} %bitcast.65), channel_id=1, source_target_pairs={{0,8},{8,0},{16,24},{24,16},{1,9},{9,1},{17,25},{25,17},{2,10},{10... | collective-permute-start | bytes 589832 | tf_op jit(solution)/shard_map/ppermute | solution.py:23
  24.2 11.3 %collective-permute-start.4 = (bf16[48,1536]{1,0:T(8,128)(2,1)S(1)}, bf16[48,1536]{1,0:T(8,128)(2,1)S(1)}, u32[]{:S(2)}, u32[]{:S(2)}) collective-permute-start(bf16[48,1536]{1,0:T(8,128)(2,1)S(1)} %copy-done.9), channel_id=1, source_target_pairs={{0,16},{8,24},{16,0},{24,8},{1,17},{9,25},{17,1},{25,9},{2,18},{10... | collective-permute-start | bytes 442376 | tf_op jit(solution)/shard_map/ppermute | solution.py:23
  46.9 12.7 %collective-permute-start.8 = (bf16[160,1536]{1,0:T(8,128)(2,1)S(1)}, bf16[160,1536]{1,0:T(8,128)(2,1)S(1)}, u32[]{:S(2)}, u32[]{:S(2)}) collective-permute-start(bf16[160,1536]{1,0:T(8,128)(2,1)S(1)} %slice.44), channel_id=1, source_target_pairs={{0,2},{1,3},{2,0},{3,1},{4,6},{5,7},{6,4},{7,5},{8,10},{9,11},{10,... | collective-permute-start | bytes 1474568 | tf_op jit(solution)/shard_map/ppermute | solution.py:23
  52.9 13.0 %collective-permute-start.9 = (bf16[160,1536]{1,0:T(8,128)(2,1)S(1)}, bf16[160,1536]{1,0:T(8,128)(2,1)S(1)}, u32[]{:S(2)}, u32[]{:S(2)}) collective-permute-start(bf16[160,1536]{1,0:T(8,128)(2,1)S(1)} %slice.34), channel_id=1, source_target_pairs={{0,4},{1,5},{2,6},{3,7},{4,0},{5,1},{6,2},{7,3},{8,12},{9,13},{10,... | collective-permute-start | bytes 1474568 | tf_op jit(solution)/shard_map/ppermute | solution.py:23
  53.5 14.7 %collective-permute-start = (bf16[320,1536]{1,0:T(8,128)(2,1)}, bf16[320,1536]{1,0:T(8,128)(2,1)}, u32[]{:S(2)}, u32[]{:S(2)}) collective-permute-start(bf16[320,1536]{1,0:T(8,128)(2,1)} %shard_map.204.refs_0_.refs_1_), channel_id=1, source_target_pairs={{0,1},{1,0},{2,3},{3,2},{4,5},{5,4},{6,7},{7,6},{8,9},{9,8},{10,11... | collective-permute-start | bytes 2949128 | tf_op jit(solution)/shard_map/ppermute | solution.py:23
  53.6 12.4 %collective-permute-start.12 = (bf16[4,48,1536]{2,1,0:T(8,128)(2,1)S(1)}, bf16[4,48,1536]{2,1,0:T(8,128)(2,1)S(1)}, u32[]{:S(2)}, u32[]{:S(2)}) collective-permute-start(bf16[4,48,1536]{2,1,0:T(8,128)(2,1)S(1)} %get-tuple-element.176), channel_id=1, source_target_pairs={{0,1},{1,0},{2,3},{3,2},{4,5},{5,4},{6,7},{7,6},{8,9},{9,8},{10,11... | collective-permute-start | bytes 1769480 | tf_op jit(solution)/shard_map/ppermute | solution.py:23
  54.2 14.0 %collective-permute-start.6 = (bf16[320,1536]{1,0:T(8,128)(2,1)}, bf16[320,1536]{1,0:T(8,128)(2,1)S(1)}, u32[]{:S(2)}, u32[]{:S(2)}) collective-permute-start(bf16[320,1536]{1,0:T(8,128)(2,1)} %collective-permute-done.1.refs_2_.refs_3_), channel_id=1, source_target_pairs={{0,1},{1,0},{2,3},{3,2},{4,5},{5,4},{6,7},{7,6},{8,9},{9,8},{10,11... | collective-permute-start | bytes 2949128 | tf_op jit(solution)/shard_map/ppermute | solution.py:23
  59.6 8.6 %collective-permute-start.7 = (bf16[320,1536]{1,0:T(8,128)(2,1)}, bf16[320,1536]{1,0:T(8,128)(2,1)S(1)}, u32[]{:S(2)}, u32[]{:S(2)}) collective-permute-start(bf16[320,1536]{1,0:T(8,128)(2,1)} %collective-permute-done.2.refs_4_.refs_5_), channel_id=1, source_target_pairs={{0,1},{1,0},{2,3},{3,2},{4,5},{5,4},{6,7},{7,6},{8,9},{9,8},{10,11... | collective-permute-start | bytes 2949128 | tf_op jit(solution)/shard_map/ppermute | solution.py:23
  69.2 31.6 %collective-permute-start.13 = (bf16[128,1536]{1,0:T(8,128)(2,1)S(1)}, bf16[128,1536]{1,0:T(8,128)(2,1)S(1)}, u32[]{:S(2)}, u32[]{:S(2)}) collective-permute-start(bf16[128,1536]{1,0:T(8,128)(2,1)S(1)} %pad_maximum_fusion.3.refs_8_.refs_0_), channel_id=1, source_target_pairs={{0,2},{1,3},{2,0},{3,1},{4,6},{5,7},{6,4},{7,5},{8,10},{9,11},{10,... | collective-permute-start | bytes 1179656 | tf_op jit(solution)/shard_map/ppermute | solution.py:23
  70.1 30.7 %collective-permute-start.14 = (bf16[128,1536]{1,0:T(8,128)(2,1)S(1)}, bf16[128,1536]{1,0:T(8,128)(2,1)S(1)}, u32[]{:S(2)}, u32[]{:S(2)}) collective-permute-start(bf16[128,1536]{1,0:T(8,128)(2,1)S(1)} %pad_maximum_fusion.3.refs_8_.refs_0_), channel_id=1, source_target_pairs={{0,4},{1,5},{2,6},{3,7},{4,0},{5,1},{6,2},{7,3},{8,12},{9,13},{10,... | collective-permute-start | bytes 1179656 | tf_op jit(solution)/shard_map/ppermute | solution.py:23
  82.7 88.5 %all-to-all-start.1 = ((bf16[32,48,768]{2,1,0:T(8,128)(2,1)}), bf16[32,48,768]{2,1,0:T(8,128)(2,1)S(1)}, u32[]{:S(2)}, u32[]{:S(2)}) async-start(bf16[32,48,768]{2,1,0:T(8,128)(2,1)} %shard_map.205), calls=%async_computation.1 | async-start | bytes 4718592 | tf_op jit(solution)/shard_map/all_to_all | solution.py:681
  106.5 14.4 %collective-permute-start.16 = (bf16[2,32,1536]{2,1,0:T(8,128)(2,1)}, bf16[2,32,1536]{2,1,0:T(8,128)(2,1)S(1)}, u32[]{:S(2)}, u32[]{:S(2)}) collective-permute-start(bf16[2,32,1536]{2,1,0:T(8,128)(2,1)} %get-tuple-element.98), channel_id=1, source_target_pairs={{0,2},{1,3},{2,0},{3,1},{4,6},{5,7},{6,4},{7,5},{8,10},{9,11},{10,... | collective-permute-start | bytes 589832 | tf_op jit(solution)/shard_map/ppermute | solution.py:23
  108.4 12.6 %collective-permute-start.17 = (bf16[2,32,1536]{2,1,0:T(8,128)(2,1)}, bf16[2,32,1536]{2,1,0:T(8,128)(2,1)S(1)}, u32[]{:S(2)}, u32[]{:S(2)}) collective-permute-start(bf16[2,32,1536]{2,1,0:T(8,128)(2,1)} %get-tuple-element.100), channel_id=1, source_target_pairs={{0,4},{1,5},{2,6},{3,7},{4,0},{5,1},{6,2},{7,3},{8,12},{9,13},{10,... | collective-permute-start | bytes 589832 | tf_op jit(solution)/shard_map/ppermute | solution.py:23
  124.4 20.7 %collective-permute-start.32 = (bf16[64,1536]{1,0:T(8,128)(2,1)S(1)}, bf16[64,1536]{1,0:T(8,128)(2,1)S(1)}, u32[]{:S(2)}, u32[]{:S(2)}) collective-permute-start(bf16[64,1536]{1,0:T(8,128)(2,1)S(1)} %slice.47), channel_id=1, source_target_pairs={{0,2},{1,3},{2,0},{3,1},{4,6},{5,7},{6,4},{7,5},{8,10},{9,11},{10,... | collective-permute-start | bytes 589832 | tf_op jit(solution)/shard_map/ppermute | solution.py:23
  132.8 9.8 %collective-permute-start.20 = (bf16[64,1536]{1,0:T(8,128)(2,1)}, bf16[64,1536]{1,0:T(8,128)(2,1)S(1)}, u32[]{:S(2)}, u32[]{:S(2)}) collective-permute-start(bf16[64,1536]{1,0:T(8,128)(2,1)} %get-tuple-element.105), channel_id=1, source_target_pairs={{0,8},{8,0},{16,24},{24,16},{1,9},{9,1},{17,25},{25,17},{2,10},{10... | collective-permute-start | bytes 589832 | tf_op jit(solution)/shard_map/ppermute | solution.py:23
  142.6 11.7 %collective-permute-start.24 = (bf16[128,1536]{1,0:T(8,128)(2,1)S(1)}, bf16[128,1536]{1,0:T(8,128)(2,1)S(1)}, u32[]{:S(2)}, u32[]{:S(2)}) collective-permute-start(bf16[128,1536]{1,0:T(8,128)(2,1)S(1)} %constant_dynamic-update-slice_fusion.2.refs_0_), channel_id=1, source_target_pairs={{0,4},{1,5},{2,6},{3,7},{4,0},{5,1},{6,2},{7,3},{8,12},{9,13},{10,... | collective-permute-start | bytes 1179656 | tf_op jit(solution)/shard_map/ppermute | solution.py:23
  143.1 24.7 %collective-permute-start.29 = (bf16[128,1536]{1,0:T(8,128)(2,1)S(1)}, bf16[128,1536]{1,0:T(8,128)(2,1)S(1)}, u32[]{:S(2)}, u32[]{:S(2)}) collective-permute-start(bf16[128,1536]{1,0:T(8,128)(2,1)S(1)} %pad_maximum_fusion.3.refs_8_.refs_0_), channel_id=1, source_target_pairs={{0,1},{1,0},{2,3},{3,2},{4,5},{5,4},{6,7},{7,6},{8,9},{9,8},{10,11... | collective-permute-start | bytes 1179656 | tf_op jit(solution)/shard_map/ppermute | solution.py:23
  143.1 13.3 %collective-permute-start.33 = (bf16[64,1536]{1,0:T(8,128)(2,1)S(1)}, bf16[64,1536]{1,0:T(8,128)(2,1)S(1)}, u32[]{:S(2)}, u32[]{:S(2)}) collective-permute-start(bf16[64,1536]{1,0:T(8,128)(2,1)S(1)} %slice.48), channel_id=1, source_target_pairs={{0,4},{1,5},{2,6},{3,7},{4,0},{5,1},{6,2},{7,3},{8,12},{9,13},{10,... | collective-permute-start | bytes 589832 | tf_op jit(solution)/shard_map/ppermute | solution.py:23
  144.8 23.6 %collective-permute-start.30 = (bf16[128,1536]{1,0:T(8,128)(2,1)S(1)}, bf16[128,1536]{1,0:T(8,128)(2,1)S(1)}, u32[]{:S(2)}, u32[]{:S(2)}) collective-permute-start(bf16[128,1536]{1,0:T(8,128)(2,1)S(1)} %collective-permute-done.13.refs_10_.refs_2_), channel_id=1, source_target_pairs={{0,1},{1,0},{2,3},{3,2},{4,5},{5,4},{6,7},{7,6},{8,9},{9,8},{10,11... | collective-permute-start | bytes 1179656 | tf_op jit(solution)/shard_map/ppermute | solution.py:23
  145.0 11.4 %collective-permute-start.22 = (bf16[128,1536]{1,0:T(8,128)(2,1)S(1)}, bf16[128,1536]{1,0:T(8,128)(2,1)S(1)}, u32[]{:S(2)}, u32[]{:S(2)}) collective-permute-start(bf16[128,1536]{1,0:T(8,128)(2,1)S(1)} %constant_dynamic-update-slice_fusion.2.refs_0_), channel_id=1, source_target_pairs={{0,2},{1,3},{2,0},{3,1},{4,6},{5,7},{6,4},{7,5},{8,10},{9,11},{10,... | collective-permute-start | bytes 1179656 | tf_op jit(solution)/shard_map/ppermute | solution.py:23
  154.3 14.2 %collective-permute-start.31 = (bf16[128,1536]{1,0:T(8,128)(2,1)S(1)}, bf16[128,1536]{1,0:T(8,128)(2,1)S(1)}, u32[]{:S(2)}, u32[]{:S(2)}) collective-permute-start(bf16[128,1536]{1,0:T(8,128)(2,1)S(1)} %collective-permute-done.14.refs_12_.refs_4_), channel_id=1, source_target_pairs={{0,1},{1,0},{2,3},{3,2},{4,5},{5,4},{6,7},{7,6},{8,9},{9,8},{10,11... | collective-permute-start | bytes 1179656 | tf_op jit(solution)/shard_map/ppermute | solution.py:23
  156.5 12.4 %collective-permute-start.34 = (bf16[128,1536]{1,0:T(8,128)(2,1)S(1)}, bf16[128,1536]{1,0:T(8,128)(2,1)S(1)}, u32[]{:S(2)}, u32[]{:S(2)}) collective-permute-start(bf16[128,1536]{1,0:T(8,128)(2,1)S(1)} %constant_dynamic-update-slice_fusion.6.refs_14_.refs_6_), channel_id=1, source_target_pairs={{0,1},{1,0},{2,3},{3,2},{4,5},{5,4},{6,7},{7,6},{8,9},{9,8},{10,11... | collective-permute-start | bytes 1179656 | tf_op jit(solution)/shard_map/ppermute | solution.py:23
  191.5 11.4 %collective-permute-start.36 = (bf16[2,64,1536]{2,1,0:T(8,128)(2,1)}, bf16[2,64,1536]{2,1,0:T(8,128)(2,1)S(1)}, u32[]{:S(2)}, u32[]{:S(2)}) collective-permute-start(bf16[2,64,1536]{2,1,0:T(8,128)(2,1)} %get-tuple-element.112), channel_id=1, source_target_pairs={{0,2},{1,3},{2,0},{3,1},{4,6},{5,7},{6,4},{7,5},{8,10},{9,11},{10,... | collective-permute-start | bytes 1179656 | tf_op jit(solution)/shard_map/ppermute | solution.py:23
  191.6 11.4 %collective-permute-start.37 = (bf16[2,64,1536]{2,1,0:T(8,128)(2,1)}, bf16[2,64,1536]{2,1,0:T(8,128)(2,1)S(1)}, u32[]{:S(2)}, u32[]{:S(2)}) collective-permute-start(bf16[2,64,1536]{2,1,0:T(8,128)(2,1)} %get-tuple-element.116), channel_id=1, source_target_pairs={{0,4},{1,5},{2,6},{3,7},{4,0},{5,1},{6,2},{7,3},{8,12},{9,13},{10,... | collective-permute-start | bytes 1179656 | tf_op jit(solution)/shard_map/ppermute | solution.py:23
  208.0 18.6 %collective-permute-start.45 = (bf16[1,64,1536]{2,1,0:T(8,128)(2,1)}, bf16[1,64,1536]{2,1,0:T(8,128)(2,1)S(1)}, u32[]{:S(2)}, u32[]{:S(2)}) collective-permute-start(bf16[1,64,1536]{2,1,0:T(8,128)(2,1)} %get-tuple-element.133), channel_id=1, source_target_pairs={{0,4},{1,5},{2,6},{3,7},{4,0},{5,1},{6,2},{7,3},{8,12},{9,13},{10,... | collective-permute-start | bytes 589832 | tf_op jit(solution)/shard_map/ppermute | solution.py:23
  215.2 11.4 %collective-permute-start.46 = (bf16[64,1536]{1,0:T(8,128)(2,1)}, bf16[64,1536]{1,0:T(8,128)(2,1)S(1)}, u32[]{:S(2)}, u32[]{:S(2)}) collective-permute-start(bf16[64,1536]{1,0:T(8,128)(2,1)} %shard_map.214), channel_id=1, source_target_pairs={{0,8},{8,0},{16,24},{24,16},{1,9},{9,1},{17,25},{25,17},{2,10},{10... | collective-permute-start | bytes 589832 | tf_op jit(solution)/shard_map/ppermute | solution.py:23
  237.2 10.3 %collective-permute-start.47 = (bf16[64,1536]{1,0:T(8,128)(2,1)}, bf16[64,1536]{1,0:T(8,128)(2,1)S(1)}, u32[]{:S(2)}, u32[]{:S(2)}) collective-permute-start(bf16[64,1536]{1,0:T(8,128)(2,1)} %get-tuple-element.135.refs_0_.refs_9_), channel_id=1, source_target_pairs={{0,1},{1,0},{2,3},{3,2},{4,5},{5,4},{6,7},{7,6},{8,9},{9,8},{10,11... | collective-permute-start | bytes 589832 | tf_op jit(solution)/shard_map/ppermute | solution.py:23
  243.2 37.4 %all-to-all-start.4 = ((bf16[32,48,384]{2,1,0:T(8,128)(2,1)}), bf16[32,48,384]{2,1,0:T(8,128)(2,1)S(1)}, u32[]{:S(2)}, u32[]{:S(2)}) async-start(bf16[32,48,384]{2,1,0:T(8,128)(2,1)} %bitcast.47), calls=%async_computation.6 | async-start | bytes 2359296 | tf_op jit(solution)/shard_map/all_to_all | solution.py:756
  247.0 99.1 %reduce-scatter.3.cloned.1.call-start = ((), (), s32[]{:S(2)}) async-start(), calls=%async_computation.8 | async-start | bytes 2457600 | tf_op jit(solution)/shard_map/reduce_scatter | solution.py:819
  279.9 43.8 %collective-permute-start.55 = (bf16[4,320,1536]{2,1,0:T(8,128)(2,1)}, bf16[4,320,1536]{2,1,0:T(8,128)(2,1)}, u32[]{:S(2)}, u32[]{:S(2)}) collective-permute-start(bf16[4,320,1536]{2,1,0:T(8,128)(2,1)} %get-tuple-element.145), channel_id=1, source_target_pairs={{0,1},{1,0},{2,3},{3,2},{4,5},{5,4},{6,7},{7,6},{8,9},{9,8},{10,11... | collective-permute-start | bytes 11796488 | tf_op jit(solution)/shard_map/ppermute | solution.py:23
  280.3 9.1 %collective-permute-start.39 = (bf16[4,128,1536]{2,1,0:T(8,128)(2,1)}, bf16[4,128,1536]{2,1,0:T(8,128)(2,1)}, u32[]{:S(2)}, u32[]{:S(2)}) collective-permute-start(bf16[4,128,1536]{2,1,0:T(8,128)(2,1)} %get-tuple-element.122), channel_id=1, source_target_pairs={{0,1},{1,0},{2,3},{3,2},{4,5},{5,4},{6,7},{7,6},{8,9},{9,8},{10,11... | collective-permute-start | bytes 4718600 | tf_op jit(solution)/shard_map/ppermute | solution.py:23
  281.6 64.6 %all-to-all-start.3 = ((bf16[32,48,384]{2,1,0:T(8,128)(2,1)}), bf16[32,48,384]{2,1,0:T(8,128)(2,1)S(1)}, u32[]{:S(2)}, u32[]{:S(2)}) async-start(bf16[32,48,384]{2,1,0:T(8,128)(2,1)} %bitcast.46), calls=%async_computation.5 | async-start | bytes 2359296 | tf_op jit(solution)/shard_map/all_to_all | solution.py:756
  292.1 15.8 %collective-permute-start.40 = (bf16[2,64,1536]{2,1,0:T(8,128)(2,1)}, bf16[2,64,1536]{2,1,0:T(8,128)(2,1)S(1)}, u32[]{:S(2)}, u32[]{:S(2)}) collective-permute-start(bf16[2,64,1536]{2,1,0:T(8,128)(2,1)} %get-tuple-element.124), channel_id=1, source_target_pairs={{0,2},{1,3},{2,0},{3,1},{4,6},{5,7},{6,4},{7,5},{8,10},{9,11},{10,... | collective-permute-start | bytes 1179656 | tf_op jit(solution)/shard_map/ppermute | solution.py:23
  293.9 14.0 %collective-permute-start.41 = (bf16[2,64,1536]{2,1,0:T(8,128)(2,1)}, bf16[2,64,1536]{2,1,0:T(8,128)(2,1)S(1)}, u32[]{:S(2)}, u32[]{:S(2)}) collective-permute-start(bf16[2,64,1536]{2,1,0:T(8,128)(2,1)} %get-tuple-element.126), channel_id=1, source_target_pairs={{0,4},{1,5},{2,6},{3,7},{4,0},{5,1},{6,2},{7,3},{8,12},{9,13},{10,... | collective-permute-start | bytes 1179656 | tf_op jit(solution)/shard_map/ppermute | solution.py:23
  312.8 53.6 %collective-permute-start.42 = (bf16[1,64,1536]{2,1,0:T(8,128)(2,1)}, bf16[1,64,1536]{2,1,0:T(8,128)(2,1)}, u32[]{:S(2)}, u32[]{:S(2)}) collective-permute-start(bf16[1,64,1536]{2,1,0:T(8,128)(2,1)} %get-tuple-element.128), channel_id=1, source_target_pairs={{0,4},{1,5},{2,6},{3,7},{4,0},{5,1},{6,2},{7,3},{8,12},{9,13},{10,... | collective-permute-start | bytes 589832 | tf_op jit(solution)/shard_map/ppermute | solution.py:23
  322.0 44.5 %collective-permute-start.44 = (bf16[64,1536]{1,0:T(8,128)(2,1)}, bf16[64,1536]{1,0:T(8,128)(2,1)}, u32[]{:S(2)}, u32[]{:S(2)}) collective-permute-start(bf16[64,1536]{1,0:T(8,128)(2,1)} %shard_map.219), channel_id=1, source_target_pairs={{0,8},{8,0},{16,24},{24,16},{1,9},{9,1},{17,25},{25,17},{2,10},{10... | collective-permute-start | bytes 589832 | tf_op jit(solution)/shard_map/ppermute | solution.py:23
  330.0 27.9 %collective-permute-start.56 = (bf16[2,160,1536]{2,1,0:T(8,128)(2,1)}, bf16[2,160,1536]{2,1,0:T(8,128)(2,1)S(1)}, u32[]{:S(2)}, u32[]{:S(2)}) collective-permute-start(bf16[2,160,1536]{2,1,0:T(8,128)(2,1)} %get-tuple-element.147), channel_id=1, source_target_pairs={{0,2},{1,3},{2,0},{3,1},{4,6},{5,7},{6,4},{7,5},{8,10},{9,11},{10,... | collective-permute-start | bytes 2949128 | tf_op jit(solution)/shard_map/ppermute | solution.py:23
  332.4 25.4 %collective-permute-start.57 = (bf16[2,160,1536]{2,1,0:T(8,128)(2,1)}, bf16[2,160,1536]{2,1,0:T(8,128)(2,1)S(1)}, u32[]{:S(2)}, u32[]{:S(2)}) collective-permute-start(bf16[2,160,1536]{2,1,0:T(8,128)(2,1)} %get-tuple-element.150), channel_id=1, source_target_pairs={{0,4},{1,5},{2,6},{3,7},{4,0},{5,1},{6,2},{7,3},{8,12},{9,13},{10,... | collective-permute-start | bytes 2949128 | tf_op jit(solution)/shard_map/ppermute | solution.py:23
  346.1 10.5 %collective-permute-start.60 = (bf16[2,48,1536]{2,1,0:T(8,128)(2,1)}, bf16[2,48,1536]{2,1,0:T(8,128)(2,1)S(1)}, u32[]{:S(2)}, u32[]{:S(2)}) collective-permute-start(bf16[2,48,1536]{2,1,0:T(8,128)(2,1)} %bitcast.78), channel_id=1, source_target_pairs={{0,1},{1,0},{2,3},{3,2},{4,5},{5,4},{6,7},{7,6},{8,9},{9,8},{10,11... | collective-permute-start | bytes 884744 | tf_op jit(solution)/shard_map/ppermute | solution.py:23
  352.8 15.7 %all-to-all-start.2 = ((bf16[8,48,640]{2,1,0:T(8,128)(2,1)}), bf16[8,48,640]{2,1,0:T(8,128)(2,1)S(1)}, u32[]{:S(2)}, u32[]{:S(2)}) async-start(bf16[8,48,640]{2,1,0:T(8,128)(2,1)} %bitcast.39), calls=%async_computation.3 | async-start | bytes 983040 | tf_op jit(solution)/shard_map/all_to_all | solution.py:845
  356.6 27.0 %reduce-scatter.5.cloned.1.call-start = ((), (), s32[]{:S(2)}) async-start(), calls=%async_computation.9 | async-start | bytes 737280 | tf_op jit(solution)/shard_map/reduce_scatter | solution.py:858
  362.9 13.9 %collective-permute-start.58 = (bf16[1,160,1536]{2,1,0:T(8,128)(2,1)}, bf16[1,160,1536]{2,1,0:T(8,128)(2,1)S(1)}, u32[]{:S(2)}, u32[]{:S(2)}) collective-permute-start(bf16[1,160,1536]{2,1,0:T(8,128)(2,1)} %get-tuple-element.152), channel_id=1, source_target_pairs={{0,4},{1,5},{2,6},{3,7},{4,0},{5,1},{6,2},{7,3},{8,12},{9,13},{10,... | collective-permute-start | bytes 1474568 | tf_op jit(solution)/shard_map/ppermute | solution.py:23
  365.0 13.2 %collective-permute-start.59 = (bf16[1,160,1536]{2,1,0:T(8,128)(2,1)}, bf16[1,160,1536]{2,1,0:T(8,128)(2,1)S(1)}, u32[]{:S(2)}, u32[]{:S(2)}) collective-permute-start(bf16[1,160,1536]{2,1,0:T(8,128)(2,1)} %get-tuple-element.154), channel_id=1, source_target_pairs={{0,2},{1,3},{2,0},{3,1},{4,6},{5,7},{6,4},{7,5},{8,10},{9,11},{10,... | collective-permute-start | bytes 1474568 | tf_op jit(solution)/shard_map/ppermute | solution.py:23
  (74 other events, 428.6 us)
Sparse Core Ops, SparseCore 0:
  41.1 41.5 all-gather.1
  280.4 65.7 reduce-scatter.2
  359.7 22.9 reduce-scatter.4
